TPU v7x, 32 devices: a whole 2x2x4 slice. The times are simulated.
32 devices in a mesh: groups: 2 (over y), pair: 4 (over z), aux: 4 (over x, core).
Axes of the slice: x: 2, y: 2, z: 4, core: 2. Of those that a mesh axis runs over, the one named last changes fastest.
Arguments:
- panels: bfloat16 [128, 48, 768], P(('groups', 'pair')), parts along dimension 0, may hold values from -4 to 4
- amplitudes: bfloat16 [128, 2304], P(('groups', 'pair')), parts along dimension 0, may hold values from -4 to 4
- fitted_ints: bfloat16 [128, 2, 512, 768], P(('groups', 'pair'), None, 'aux'), parts along dimension 0, may hold values from -4 to 4
- pno_energy: float32 [128, 48], P(('groups', 'pair')), parts along dimension 0, may hold values from 0.3 to 3
- fock_occ: float32 [128, 64], P('groups'), parts along dimension 0, may hold values from -2.3 to 2.3, as said below
- pno_count: int32 [128], P(('groups', 'pair')), parts along dimension 0, may hold values from 12 to 48, as said below
- pair_pos: int32 [128], P('groups'), parts along dimension 0, may hold values from 0 to 63, as said below
- coupling: int32 [128, 28, 2], P('groups'), parts along dimension 0, may hold values from 0 to 63, as said below
- coupling_lmo: int32 [128, 28], P('groups'), parts along dimension 0, may hold values from 0 to 63
- pair_lmo: int32 [128, 2], P('groups'), parts along dimension 0, may hold values from 0 to 63
Outputs:
- residual: float32 [128, 2304], P(('groups', 'pair', 'aux')), parts along dimension 0
There are 2 independent parts, one for each index of `groups`. A program takes and returns all parts, laid end to end along the dimension named above; each array names one. Nothing has to cross between parts.
Inputs may be any that keep to these rules, and one draw needn't show every extreme that they name: `pair_pos`: a permutation: every position once. `coupling`: for the 4 consecutive positions of one device in the output, the 224 pairs they name lie at most 56 on one pair index, and exactly 56 on some pair index. `pno_count`: some pair uses all 48. `fock_occ`: symmetric.
All inputs are finite; a program needn't handle non-finite values.
Results may differ from a plain program's by a relative error of at most 0.0037.
Values may be sent and summed in bfloat16 or wider, within the bound.
No kernel may reach another device: no remote copies, remote signals or barrier semaphores. Data moves between devices by JAX's collectives and lax.ppermute only.
A program may use at most 128 MiB of HBM per device.

v0:
```python
import jax
import jax.numpy as jnp
from jax import lax
from jax.sharding import PartitionSpec as P


def route_block(
    block_index,
    pair_pos,
    coupling,
    coupling_lmo,
    pair_lmo,
    fock_occ,
    per_aux,
    per_dev,
    pair_devices,
):
    highest = lax.Precision.HIGHEST
    row_first = block_index * per_aux
    labels = lax.dynamic_slice_in_dim(coupling, row_first, per_aux, 0).reshape(-1)
    target = jnp.take(pair_pos, labels, axis=0)
    owner_dev = target // per_dev
    local_pair = target % per_dev
    device_range = jnp.arange(pair_devices, dtype=jnp.int32)
    owner_hot = (owner_dev[:, None] == device_range[None, :]).astype(jnp.int32)
    running = jnp.cumsum(owner_hot, axis=0) - 1
    slot_index = jnp.sum(running * owner_hot, axis=1)
    lmo_rows = lax.dynamic_slice_in_dim(pair_lmo, row_first, per_aux, 0)
    k_rows = lax.dynamic_slice_in_dim(coupling_lmo, row_first, per_aux, 0)
    lmo_range = jnp.arange(fock_occ.shape[0], dtype=jnp.int32)
    hot_k = (k_rows[:, :, None] == lmo_range[None, None, :]).astype(jnp.float32)
    hot_i = (lmo_rows[:, 0:1] == lmo_range[None, :]).astype(jnp.float32)
    hot_j = (lmo_rows[:, 1:2] == lmo_range[None, :]).astype(jnp.float32)
    fock_k = jnp.einsum("qcl,lm->qcm", hot_k, fock_occ, precision=highest)
    weight_left = jnp.sum(fock_k * hot_j[:, None, :], axis=2)
    fock_i = jnp.dot(hot_i, fock_occ, precision=highest)
    weight_right = jnp.sum(fock_i[:, None, :] * hot_k, axis=2)
    weight = jnp.stack([weight_left, weight_right], axis=2).reshape(-1)
    return (owner_dev, local_pair, slot_index, weight)


def slot_tables(routes, pair_index, capacity):
    owner_dev, local_pair, slot_index, weight = routes
    is_mine = owner_dev == pair_index
    slot_range = jnp.arange(capacity, dtype=jnp.int32)
    slot_hot = (is_mine[:, :, None] & (slot_index[:, :, None] == slot_range[None, None, :])).astype(
        jnp.int32
    )
    pair_of_slot = jnp.sum(slot_hot * local_pair[:, :, None], axis=1)
    filled = jnp.sum(slot_hot, axis=1)
    return (slot_hot, pair_of_slot, filled)


def sandwich(
    left_panels, right_panels, right_amps, pattern_intersection, pattern_half, pattern_coupled
):
    intersection = jnp.einsum(
        pattern_intersection, left_panels, right_panels, preferred_element_type=jnp.float32
    ).astype(jnp.bfloat16)
    half_product = jnp.einsum(
        pattern_half, intersection, right_amps, preferred_element_type=jnp.float32
    ).astype(jnp.bfloat16)
    return jnp.einsum(
        pattern_coupled, half_product, intersection, preferred_element_type=jnp.float32
    )


def on_device(
    panels,
    amplitudes,
    fitted_ints,
    pno_energy,
    fock_occ,
    pno_count,
    pair_pos,
    coupling,
    coupling_lmo,
    pair_lmo,
):
    highest = lax.Precision.HIGHEST
    per_dev, pno_width, pao_width = panels.shape
    pair_devices = lax.axis_size("pair")
    aux_devices = lax.axis_size("aux")
    per_aux = per_dev // aux_devices
    ncpl_two = 2 * coupling.shape[1]
    requests = per_aux * ncpl_two
    capacity = -(-requests // pair_devices)
    pair_index = lax.axis_index("pair")
    aux_index = lax.axis_index("aux")
    live_rows = lax.broadcasted_iota(jnp.int32, (per_dev, pno_width), 1) < pno_count[:, None]
    masked_panels = jnp.where(live_rows[:, :, None], panels, jnp.zeros_like(panels))
    live_block = (live_rows[:, :, None] & live_rows[:, None, :]).reshape(
        per_dev, pno_width * pno_width
    )
    masked_amps = jnp.where(live_block, amplitudes, jnp.zeros_like(amplitudes))
    fitted = jnp.einsum(
        "phqw,paw->phqa", fitted_ints, masked_panels, preferred_element_type=jnp.float32
    ).astype(jnp.bfloat16)
    product = jnp.einsum(
        "pqa,pqb->pab", fitted[:, 0], fitted[:, 1], preferred_element_type=jnp.float32
    )
    exchange_k = lax.psum_scatter(
        product.reshape(per_aux * lax.axis_size("aux"), pno_width * pno_width),
        "aux",
        scatter_dimension=0,
        tiled=True,
    )
    own_first = aux_index * per_aux
    own_panels = lax.dynamic_slice_in_dim(masked_panels, own_first, per_aux, 0)

    def route_of(block_index):
        return route_block(
            block_index,
            pair_pos,
            coupling,
            coupling_lmo,
            pair_lmo,
            fock_occ,
            per_aux,
            per_dev,
            pair_devices,
        )

    requester_blocks = jnp.arange(pair_devices, dtype=jnp.int32) * aux_devices + aux_index
    all_routes = jax.vmap(route_of)(requester_blocks)
    slot_hot, pair_of_slot, filled = slot_tables(all_routes, pair_index, capacity)
    send_panels = jnp.take(masked_panels, pair_of_slot, axis=0)
    send_panels = jnp.where(filled[:, :, None, None] > 0, send_panels, jnp.zeros_like(send_panels))
    send_amps = jnp.take(masked_amps, pair_of_slot, axis=0)
    send_amps = jnp.where(filled[:, :, None] > 0, send_amps, jnp.zeros_like(send_amps))
    recv_panels, recv_amps = (
        lax.all_to_all(send_panels, "pair", split_axis=0, concat_axis=0, tiled=True),
        lax.all_to_all(send_amps, "pair", split_axis=0, concat_axis=0, tiled=True),
    )
    owner_dev, local_pair, slot_index, weight = route_of(pair_index * aux_devices + aux_index)
    flat_slot = owner_dev * capacity + slot_index
    far_panels = jnp.take(
        recv_panels.reshape(pair_devices * capacity, pno_width, pao_width), flat_slot, axis=0
    )
    far_panels = far_panels.reshape(per_aux, ncpl_two, pno_width, pao_width)
    far_amps = jnp.take(
        recv_amps.reshape(pair_devices * capacity, pno_width * pno_width), flat_slot, axis=0
    )
    far_amps = far_amps.reshape(per_aux, ncpl_two, pno_width, pno_width)
    coupled = sandwich(
        own_panels, far_panels, far_amps, "qaw,qrbw->qrab", "qrab,qrbc->qrac", "qrac,qrdc->qrad"
    )
    coupling_sum = jnp.einsum(
        "qr,qrab->qab", weight.reshape(per_aux, ncpl_two), coupled, precision=highest
    )
    coupling_sum = coupling_sum.reshape(per_aux, pno_width * pno_width)
    own_amps = lax.dynamic_slice_in_dim(masked_amps, own_first, per_aux, 0)
    own_energy = lax.dynamic_slice_in_dim(pno_energy, own_first, per_aux, 0)
    own_live = lax.dynamic_slice_in_dim(live_block, own_first, per_aux, 0)
    own_lmo = lax.dynamic_slice_in_dim(pair_lmo, pair_index * per_dev + own_first, per_aux, 0)
    lmo_range = jnp.arange(fock_occ.shape[0], dtype=jnp.int32)
    occ_diag = jnp.diagonal(fock_occ)
    lmo_hot = (own_lmo[:, :, None] == lmo_range[None, None, :]).astype(jnp.float32)
    occ_pair = jnp.sum(lmo_hot * occ_diag[None, None, :], axis=(1, 2))
    energy_gap = own_energy[:, :, None] + own_energy[:, None, :] - occ_pair[:, None, None]
    diag_term = energy_gap.reshape(per_aux, pno_width * pno_width) * own_amps.astype(jnp.float32)
    total = exchange_k + diag_term - coupling_sum
    return jnp.where(own_live, total, jnp.zeros_like(total))


def solution(mesh):
    placed = (
        P(("groups", "pair"), None, None),
        P(("groups", "pair"), None),
        P(("groups", "pair"), None, "aux", None),
        P(("groups", "pair"), None),
        P("groups", None),
        P(("groups", "pair")),
        P("groups"),
        P("groups", None, None),
        P("groups", None),
        P("groups", None),
    )
    return jax.shard_map(
        on_device,
        mesh=mesh,
        in_specs=placed,
        out_specs=P(("groups", "pair", "aux"), None),
        check_vma=False,
    )
```

profile of v0, /device:TPU:0, one launch (start us, length us, event | category | flops | bytes accessed | tf_op | source)
XLA Modules:
  0.0 466.1 jit_solution(12011150484307671180)
XLA Ops:
  6.5 0.9 constant_dynamic-slice_fusion
  8.0 0.9 copy.134
  8.9 0.6 gather_fusion.2
  9.9 5.5 %gather_fusion.3 = s32[896]{0:T(1024)S(1)} fusion(s32[64]{0:T(128)S(1)} %copy-done.2, s32[1024]{0:T(1024)S(1)} %pad_clamp_fusion.2), kind=kCustom, calls=%fused_computation.3 | custom fusion | bytes 10752 | tf_op jit(solution)/shard_map/vmap(jit(_take))/gather | solution.py:21
  15.6 1.9 gather_fusion.1
  17.7 1.2 reduce-window.14
  19.4 4.8 %reduce-window.16 = s32[4,4,2,128]{3,2,1,0:T(2,128)S(1)} reduce-window(s32[4,4,2,128]{3,2,1,0:T(2,128)S(1)} %reshape.420, s32[]{:T(128)} %constant.147.clone.1), window={size=1x1x1x128 pad=0_0x0_0x0_0x127_0}, to_apply=%region_7.8 | reduce-window | flops 520192 | bytes 32772 | tf_op jit(solution)/shard_map/reduce-window.2
  25.7 1.3 gather_fusion.6
  27.0 0.5 compare_and_fusion
  27.6 1.2 select_select_fusion.1
  28.8 6.3 %all-to-all-start.1 = ((bf16[4,56,2304]{2,1,0:T(8,128)(2,1)}), bf16[4,56,2304]{2,1,0:T(8,128)(2,1)S(1)}, u32[]{:S(2)}, u32[]{:S(2)}) async-start(bf16[4,56,2304]{2,1,0:T(8,128)(2,1)} %select_select_fusion.1), calls=%async_computation.1 | async-start | bytes 2064384 | tf_op jit(solution)/shard_map/all_to_all | solution.py:133
  35.3 9.9 %gather_fusion.4 = bf16[224,48,768]{2,1,0:T(8,128)(2,1)} fusion(bf16[16,48,768]{2,1,0:T(8,128)(2,1)S(1)} %broadcast_select_fusion.1, s32[1024]{0:T(1024)S(1)} %pad_clamp_fusion.1), kind=kCustom, calls=%fused_computation.4 | custom fusion | bytes 33031040 | tf_op jit(solution)/shard_map/jit(_take)/gather | solution.py:127
  45.2 14.5 %select_select_fusion = bf16[4,56,48,768]{3,2,1,0:T(8,128)(2,1)} fusion(bf16[4,56,48,768]{3,2,1,0:T(8,128)(2,1)} %bitcast.72, pred[4,56]{1,0:T(4,128)(4,1)S(1)} %copy-done.10, pred[4,56]{1,0:T(4,128)(4,1)S(1)} %copy-done.8), kind=kLoop, calls=%fused_computation.10 | loop fusion | flops 16515072 | bytes 33030592 | tf_op jit(solution)/shard_map/jit(_where)/select_n | solution.py:128
  59.6 0.9 all-to-all-done.1
  60.5 7.0 %all-to-all-start = ((bf16[4,56,48,768]{3,2,1,0:T(8,128)(2,1)}), bf16[4,56,48,768]{3,2,1,0:T(8,128)(2,1)}, u32[]{:S(2)}, u32[]{:S(2)}) async-start(bf16[4,56,48,768]{3,2,1,0:T(8,128)(2,1)} %select_select_fusion), calls=%async_computation | async-start | bytes 33030144 | tf_op jit(solution)/shard_map/all_to_all | solution.py:132
  67.5 4.7 %fusion.16 = bf16[16,2,128,48]{2,3,1,0:T(8,128)(2,1)S(1)} fusion(bf16[16,2,128,768]{3,2,1,0:T(8,128)(2,1)} %param.12, bf16[16,48,768]{2,1,0:T(8,128)(2,1)S(1)} %broadcast_select_fusion.1), kind=kOutput, calls=%fused_computation.20 | convolution fusion | flops 302186496 | bytes 7864320 | tf_op jit(solution)/shard_map/phqw,paw->phqa/dot_general | solution.py:96
  72.5 0.8 reshape.406
  74.5 0.7 copy.153
  75.2 0.8 gather_fusion
  76.0 0.7 constant_dynamic-slice_fusion.4
  76.8 0.7 add.240
  77.5 0.6 dynamic-slice
  78.9 1.3 gather_fusion.7
  80.2 0.8 copy.143
  81.0 2.6 gather.50
  83.6 4.2 broadcast_select_fusion
  87.8 6.0 %copy.145 = bf16[4,56,48,48]{3,2,1,0:T(8,128)(2,1)} copy(bf16[4,56,48,48]{1,0,3,2:T(4,128)(2,1)} %broadcast_select_fusion) | data formatting | bytes 2064384 | tf_op jit(solution)/shard_map/jit(_take)/select_n | solution.py:141
  93.8 330.4 %all-to-all-done = bf16[4,56,48,768]{3,2,1,0:T(8,128)(2,1)} async-done(((bf16[4,56,48,768]{3,2,1,0:T(8,128)(2,1)}), bf16[4,56,48,768]{3,2,1,0:T(8,128)(2,1)}, u32[]{:S(2)}, u32[]{:S(2)}) %all-to-all-start) | async-done | bytes 16515104 | tf_op jit(solution)/shard_map/all_to_all | solution.py:132
  424.2 15.6 %gather_fusion.5 = bf16[224,48,768]{2,1,0:T(8,128)(2,1)} fusion(bf16[224,48,768]{2,1,0:T(8,128)(2,1)} %bitcast.23, s32[1024]{0:T(1024)S(1)} %pad_clamp_fusion), kind=kCustom, calls=%fused_computation.5 | custom fusion | bytes 33031040 | tf_op jit(solution)/shard_map/jit(_take)/gather | solution.py:137
  439.7 11.8 %fusion = bf16[4,56,48,48]{3,2,1,0:T(8,128)(2,1)} fusion(bf16[4,56,48,768]{3,2,1,0:T(8,128)(2,1)} %bitcast.73, pred[4,56]{1,0:T(4,128)(4,1)S(1)} %copy-done.12, bf16[16,48,768]{2,1,0:T(8,128)(2,1)S(1)} %broadcast_select_fusion.1, s32[]{:T(128)S(6)} %select_n.233), kind=kOutput, calls=%fused_computation.8 | convolution fusion | flops 800980992 | bytes 17842692 | tf_op jit(solution)/shard_map/qaw,qrbw->qrab/dot_general | solution.py:57
  451.5 6.0 %multiply_reduce_fusion = f32[4,48,48]{2,1,0:T(8,128)S(1)} fusion(f32[4,56]{1,0:T(4,128)S(1)} %copy-done.13, bf16[4,56,48,48]{3,2,1,0:T(8,128)(2,1)} %fusion, bf16[4,56,48,48]{3,2,1,0:T(8,128)(2,1)} %copy.145), kind=kOutput, calls=%fused_computation.13 | convolution fusion | flops 100629504 | bytes 2102144 | tf_op jit(solution)/shard_map/qrac,qrdc->qrad/dot_general | solution.py:63
  457.6 1.6 fusion.24
  (103 shorter events, 5.3 us)
Async XLA Ops:
  6.5 67.1 %copy-start = (f32[64,64]{1,0:T(8,128)S(1)}, f32[64,64]{1,0:T(8,128)}, u32[]{:S(2)}) copy-start(f32[64,64]{1,0:T(8,128)} %param.14) | copy-start | bytes 49156
  6.5 3.3 copy-start.2
  9.8 15.4 %copy-start.14 = (s32[16]{0:T(128)S(1)}, s32[16]{0:T(128)}, u32[]{:S(2)}) copy-start(s32[16]{0:T(128)} %param.15) | copy-start | bytes 196
  9.8 15.8 %copy-start.5 = (bf16[16,2304]{1,0:T(8,128)(2,1)S(1)}, bf16[16,2304]{1,0:T(8,128)(2,1)}, u32[]{:S(2)}) copy-start(bf16[16,2304]{1,0:T(8,128)(2,1)} %param.11) | copy-start | bytes 221188
  25.3 2.3 copy-start.7
  27.0 8.1 %copy-start.3 = (bf16[16,48,768]{2,1,0:T(8,128)(2,1)S(1)}, bf16[16,48,768]{2,1,0:T(8,128)(2,1)}, u32[]{:S(2)}) copy-start(bf16[16,48,768]{2,1,0:T(8,128)(2,1)} %param.10) | copy-start | bytes 3538948
  27.6 1.2 copy-start.9
  28.8 31.7 %all-to-all-start.1 = ((bf16[4,56,2304]{2,1,0:T(8,128)(2,1)}), bf16[4,56,2304]{2,1,0:T(8,128)(2,1)S(1)}, u32[]{:S(2)}, u32[]{:S(2)}) async-start(bf16[4,56,2304]{2,1,0:T(8,128)(2,1)} %select_select_fusion.1), calls=%async_computation.1 | async-start | bytes 2064384 | tf_op jit(solution)/shard_map/all_to_all | solution.py:133
  35.3 9.9 %copy-start.8 = (pred[4,56]{1,0:T(4,128)(4,1)S(1)}, pred[4,56]{1,0:T(4,128)(4,1)}, u32[]{:S(2)}) copy-start(pred[4,56]{1,0:T(4,128)(4,1)} %copy-done.7) | copy-start | bytes 676
  35.3 9.9 %copy-start.10 = (pred[4,56]{1,0:T(4,128)(4,1)S(1)}, pred[4,56]{1,0:T(4,128)(4,1)}, u32[]{:S(2)}) copy-start(pred[4,56]{1,0:T(4,128)(4,1)} %copy-done.9) | copy-start | bytes 676
  60.5 363.7 %all-to-all-start = ((bf16[4,56,48,768]{3,2,1,0:T(8,128)(2,1)}), bf16[4,56,48,768]{3,2,1,0:T(8,128)(2,1)}, u32[]{:S(2)}, u32[]{:S(2)}) async-start(bf16[4,56,48,768]{3,2,1,0:T(8,128)(2,1)} %select_select_fusion), calls=%async_computation | async-start | bytes 33030144 | tf_op jit(solution)/shard_map/all_to_all | solution.py:132
  67.4 5.9 %copy-start.6 = (s32[64,28]{0,1:T(8,128)S(1)}, s32[64,28]{0,1:T(8,128)}, u32[]{:S(2)}) copy-start(s32[64,28]{0,1:T(8,128)} %param.18) | copy-start | bytes 21508
  67.5 6.1 %copy-start.11 = (s32[64,2]{0,1:T(2,128)S(1)}, s32[64,2]{0,1:T(2,128)}, u32[]{:S(2)}) copy-start(s32[64,2]{0,1:T(2,128)} %param.19) | copy-start | bytes 1540
  67.5 10.1 %copy-start.15 = (u32[32]{0:T(128)S(1)}, u32[32]{0:T(128)}, u32[]{:S(2)}) copy-start(u32[32]{0:T(128)} %constant.208) | copy-start | bytes 388
  67.5 390.1 %all-reduce.6.cloned.1.call-start = ((), (), s32[]{:S(2)}) async-start(), calls=%async_computation.2 | async-start | bytes 294912
  80.2 3.4 copy-start.12
  439.7 11.8 %copy-start.13 = (f32[4,56]{1,0:T(4,128)S(1)}, f32[4,56]{1,0:T(4,128)}, u32[]{:S(2)}) copy-start(f32[4,56]{1,0:T(4,128)} %copy.153) | copy-start | bytes 2692
  439.7 19.5 %copy-start.1 = (f32[64,64]{1,0:T(8,128)S(1)}, f32[64,64]{1,0:T(8,128)}, u32[]{:S(2)}) copy-start(f32[64,64]{1,0:T(8,128)} %param.14) | copy-start | bytes 49156
  451.5 6.1 %copy-start.4 = (f32[4,2304]{1,0:T(4,128)S(1)}, f32[4,2304]{1,0:T(4,128)}, u32[]{:S(2)}) copy-start(f32[4,2304]{1,0:T(4,128)} %add.240) | copy-start | bytes 110596
Sparse Core Ops, SparseCore 0:
  73.5 32.1 all-reduce.5
where the time goes:
time: 467 us; the launch traced here: 466 us
  waiting for transfers between devices  331 us (71%)
  local copies, waits for them, and re-layouts  54.3 us (12%)
  other arithmetic  29.6 us (6%)
  matrix products  23.2 us (5%)
  between operations  14.4 us (3%)
  starting transfers between devices  13.3 us (3%)
    all_to_all x1, waiting for transfers between devices, on_device(): lax.all_to_all(send_panels, 'pair', split_axis=0, concat_axis=0, tiled=True)  330 us
    gather x1, local copies, waits for them, and re-layouts, on_device(): jnp.take(recv_panels.reshape(pair_devices * capacity, pno_width, pao_widt...  15.6 us
    select_n x1, other arithmetic, on_device(): jnp.where(filled[:, :, None, None] > 0, send_panels, jnp.zeros_like(send_...  14.5 us
    dot_general x1, matrix products, sandwich(): jnp.einsum(pattern_intersection, left_panels, right_panels, preferred_ele...  11.8 us
    gather x1, local copies, waits for them, and re-layouts, on_device(): send_panels = jnp.take(masked_panels, pair_of_slot, axis=0)  9.86 us
  transfers between devices with their start and end apart: 3, of which 2 were waited for; matrix products, arithmetic and copies ran while one was open for 18% of the time, Pallas kernels for 0%

commit v1 on v0

v1 whole, which is shorter than its diff:
```python
import functools

import jax
import jax.numpy as jnp
from jax import lax
from jax.experimental import pallas as pl
from jax.experimental.pallas import tpu as pltpu
from jax.sharding import PartitionSpec as P

BF16 = jnp.bfloat16
F32 = jnp.float32
I32 = jnp.int32
HIGHEST = lax.Precision.HIGHEST
VMEM_BYTES = 32 * 1024 * 1024


def dot_nn(a, b, precision=None):
    return lax.dot_general(
        a, b, (((1,), (0,)), ((), ())), precision=precision, preferred_element_type=F32
    )


def dot_nt(a, b, precision=None):
    return lax.dot_general(
        a, b, (((1,), (1,)), ((), ())), precision=precision, preferred_element_type=F32
    )


def iota(shape, dim):
    return lax.broadcasted_iota(I32, shape, dim)


def floor_div(values, by):
    return jnp.floor((values.astype(F32) + 0.5) * (1.0 / by)).astype(I32)


def whole(memory_space=pltpu.VMEM):
    return pl.BlockSpec(memory_space=memory_space)


def tail_rows(block, chunks):
    return -(-(block * chunks) // 16) * 16


def masked_rows(panel, count):
    live = iota(panel.shape, 0) < count
    return jnp.where(live, panel.astype(F32), 0.0).astype(BF16)


def pack_kernel(block, width, chunks, panels, amps, count, out, held, sem):
    first = lax.axis_index("aux") * block
    copy = pltpu.make_async_copy(panels.at[pl.ds(first, block)], held, sem)
    copy.start()
    pao = held.shape[2]
    pairs = amps.shape[0]
    tail = tail_rows(block, chunks)
    row = iota((tail, pairs), 0)
    source = iota((tail, pairs), 1)
    rows = jnp.zeros((tail, pao), F32)
    for chunk in range(chunks):
        inside = (row >= chunk * block) & (row < (chunk + 1) * block)
        hot = (inside & (source == first + row - chunk * block)).astype(F32).astype(BF16)
        rows += dot_nn(hot, amps[:, chunk * pao : (chunk + 1) * pao])
    out[block * width :, :] = rows.astype(BF16)
    copy.wait()
    for j in range(block):
        out[j * width : (j + 1) * width, :] = masked_rows(held[j], count[first + j])


def pack(panels, amps, count, block):
    pairs, width, pao = panels.shape
    chunks = width * width // pao
    rows = block * width + tail_rows(block, chunks)
    return pl.pallas_call(
        functools.partial(pack_kernel, block, width, chunks),
        out_shape=jax.ShapeDtypeStruct((rows, pao), BF16),
        in_specs=[whole(pl.ANY), whole(), whole(pltpu.SMEM)],
        out_specs=whole(),
        scratch_shapes=[pltpu.VMEM((block, width, pao), BF16), pltpu.SemaphoreType.DMA],
        compiler_params=pltpu.CompilerParams(vmem_limit_bytes=VMEM_BYTES),
        name="pack",
    )(panels, amps, count)


def exchange_kernel(group, width, fit, panels, count, out, masked):
    step = pl.program_id(0)
    functions = fit.shape[2]
    for g in range(group):
        panel = masked_rows(panels[g], count[step * group + g])
        masked[g * width : (g + 1) * width, :] = panel
        if functions % 128 == 0:
            both = dot_nt(panel, fit[g].reshape(2 * functions, fit.shape[3])).astype(BF16)
            left, right = both[:, :functions], both[:, functions:]
        else:
            left = dot_nt(panel, fit[g, 0]).astype(BF16)
            right = dot_nt(panel, fit[g, 1]).astype(BF16)
        out[g * width : (g + 1) * width, :] = dot_nt(left, right)


def exchange(fit, panels, count):
    pairs, width, pao = panels.shape
    functions = fit.shape[2]
    group = 4
    flops = 2 * pairs * (2 * functions * pao * width + functions * width * width)
    return pl.pallas_call(
        functools.partial(exchange_kernel, group, width),
        out_shape=(
            jax.ShapeDtypeStruct((pairs * width, width), F32),
            jax.ShapeDtypeStruct((pairs * width, pao), BF16),
        ),
        grid=(pairs // group,),
        in_specs=[
            pl.BlockSpec((group, 2, functions, pao), lambda i: (i, 0, 0, 0)),
            pl.BlockSpec((group, width, pao), lambda i: (i, 0, 0)),
            whole(pltpu.SMEM),
        ],
        out_specs=(
            pl.BlockSpec((group * width, width), lambda i: (i, 0)),
            pl.BlockSpec((group * width, pao), lambda i: (i, 0)),
        ),
        compiler_params=pltpu.CompilerParams(vmem_limit_bytes=VMEM_BYTES),
        cost_estimate=pl.CostEstimate(
            flops=5 * flops, bytes_accessed=fit.size * 2 + panels.size * 4, transcendentals=0
        ),
        name="exchange",
    )(fit, panels, count)


def tables_kernel(
    block, width, couplings, rounds, table, pos, fock, amps, weight_in, weight_out, block_amps
):
    total = pos.shape[0]
    occ = fock.shape[0]
    per_dev = amps.shape[0] // width
    rows = table.shape[0]
    pair_devices = total // per_dev
    pair = lax.axis_index("pair")
    first = lax.axis_index("aux") * block
    here = pos[...] == iota((total, total), 1)
    label_at = jnp.sum(jnp.where(here, iota((total, total), 0), 0), axis=0, keepdims=True)
    lanes = iota((rows, occ), 1)
    base = 3 * couplings
    hot_i = (table[:, base : base + 1] == lanes).astype(F32)
    hot_j = (table[:, base + 1 : base + 2] == lanes).astype(F32)
    fock_i = dot_nn(hot_i, fock[...], HIGHEST)
    fock_j = dot_nt(hot_j, fock[...], HIGHEST)
    weight = jnp.zeros((rows, total), F32)
    for c in range(couplings):
        hot_k = table[:, 2 * couplings + c : 2 * couplings + c + 1] == lanes
        left = jnp.sum(jnp.where(hot_k, fock_j, 0.0), axis=1, keepdims=True)
        right = jnp.sum(jnp.where(hot_k, fock_i, 0.0), axis=1, keepdims=True)
        weight += jnp.where(table[:, 2 * c : 2 * c + 1] == label_at, left, 0.0)
        weight += jnp.where(table[:, 2 * c + 1 : 2 * c + 2] == label_at, right, 0.0)
    wide = per_dev * width
    spread = (
        iota((total, wide), 0) == pair * per_dev + floor_div(iota((total, wide), 1), width)
    ).astype(F32)
    weight_out[...] = dot_nn(weight[per_dev:, :], spread, HIGHEST)
    thin = block * width
    of_row = iota((total, thin), 0)
    of_lane = floor_div(iota((total, thin), 1), width)
    for k in range(rounds + 1):
        source = lax.rem(pair + pair_devices - k, pair_devices) * per_dev + first
        spread = (of_row == source + of_lane).astype(F32)
        weight_in[k * per_dev : (k + 1) * per_dev, :] = dot_nn(
            weight[:per_dev, :], spread, HIGHEST
        )
    lane = iota((1, wide), 1)
    lane_pair = floor_div(lane, width)
    repeat = (iota((width, wide), 0) == (lane - width * lane_pair)).astype(F32).astype(BF16)
    tiled = dot_nn(amps[...], repeat)
    row_pair = floor_div(iota((wide, 1), 0), width)
    block_amps[...] = jnp.where(row_pair == lane_pair, tiled, 0.0).astype(BF16)


def tables(table, pos, fock, amps, block, width, couplings, rounds):
    wide = amps.shape[0]
    per_dev = wide // width
    return pl.pallas_call(
        functools.partial(tables_kernel, block, width, couplings, rounds),
        out_shape=(
            jax.ShapeDtypeStruct(((rounds + 1) * per_dev, block * width), F32),
            jax.ShapeDtypeStruct((table.shape[0] - per_dev, wide), F32),
            jax.ShapeDtypeStruct((wide, wide), BF16),
        ),
        in_specs=[whole()] * 4,
        out_specs=(whole(),) * 3,
        compiler_params=pltpu.CompilerParams(vmem_limit_bytes=VMEM_BYTES),
        cost_estimate=pl.CostEstimate(
            flops=2_000_000_000, bytes_accessed=4_000_000, transcendentals=0
        ),
        name="tables",
    )(table, pos, fock, amps)


def split_high_low(values):
    high = values.astype(BF16)
    return high, (values - high.astype(F32)).astype(BF16)


def couple_kernel(block, width, chunks, back, flat, *refs):
    refs = list(refs)
    sent, masked, weight_in, acc_in = refs[:4]
    refs = refs[4:]
    if back:
        block_amps, weight_out = refs[:2]
        refs = refs[2:]
    acc_out = refs.pop(0)
    if back:
        back_out = refs.pop(0)
    acc = refs.pop(0) if flat else acc_out
    if back:
        back_acc = refs.pop(0)
    thin = block * width
    pao = masked.shape[1]
    per_dev = masked.shape[0] // width
    per_chunk = pao // width
    tail = sent.shape[0] - thin
    panels = sent[:thin, :]

    row = iota((thin, 1), 0)
    row_pair = floor_div(row, width)
    row_pno = row - width * row_pair
    row_chunk = floor_div(row_pno, per_chunk)
    pick = (iota((thin, tail), 1) == row_chunk * block + row_pair).astype(F32).astype(BF16)
    picked = dot_nn(pick, sent[thin:, :])
    lane = iota((1, pao), 1)
    picked = jnp.where(
        row_pno - per_chunk * row_chunk == floor_div(lane, width), picked, 0.0
    ).astype(BF16)
    down = iota((pao, 1), 0)
    across = iota((1, thin), 1)
    across_pair = floor_div(across, width)
    fold = (
        (down - width * floor_div(down, width)) == (across - width * across_pair)
    ).astype(F32).astype(BF16)
    sent_amps = jnp.where(row_pair == across_pair, dot_nn(picked, fold), 0.0).astype(BF16)

    inter = dot_nt(masked[...], panels).astype(BF16)
    half = dot_nn(inter, sent_amps).astype(BF16).astype(F32)
    for t in range(per_dev):
        rows = slice(t * width, (t + 1) * width)
        high, low = split_high_low(half[rows, :] * weight_in[t : t + 1, :])
        mine = inter[rows, :]
        acc[rows, :] = acc_in[rows, :] - (dot_nt(high, mine) + dot_nt(low, mine))
    if flat:
        for a in range(width):
            acc_out[:, a * width : (a + 1) * width] = acc[pl.ds(a, per_dev, stride=width), :]
    if back:
        inter = dot_nt(panels, masked[...]).astype(BF16)
        half = dot_nn(inter, block_amps[...]).astype(BF16).astype(F32)
        for s in range(block):
            rows = slice(s * width, (s + 1) * width)
            high, low = split_high_low(half[rows, :] * weight_out[s : s + 1, :])
            mine = inter[rows, :]
            back_acc[rows, :] = dot_nt(high, mine) + dot_nt(low, mine)
        for a in range(width):
            back_out[:, a * width : (a + 1) * width] = back_acc[pl.ds(a, block, stride=width), :]


def couple(sent, masked, weight_in, acc, block, width, flat, back):
    pao = masked.shape[1]
    wide = masked.shape[0]
    per_dev = wide // width
    chunks = width * width // pao
    thin = block * width
    acc_shape = (per_dev, width * width) if flat else (wide, width)
    outs = [jax.ShapeDtypeStruct(acc_shape, F32)]
    scratch = [pltpu.VMEM((wide, width), F32)] if flat else []
    if back:
        outs.append(jax.ShapeDtypeStruct((block, width * width), F32))
        scratch.append(pltpu.VMEM((thin, width), F32))
    args = (sent, masked, weight_in, acc) + tuple(back or ())
    flops = 2 * thin * wide * (pao + thin) + (2 * thin * wide * (pao + wide) if back else 0)
    return pl.pallas_call(
        functools.partial(couple_kernel, block, width, chunks, bool(back), flat),
        out_shape=tuple(outs),
        in_specs=[whole()] * len(args),
        out_specs=(whole(),) * len(outs),
        scratch_shapes=scratch,
        compiler_params=pltpu.CompilerParams(vmem_limit_bytes=VMEM_BYTES),
        cost_estimate=pl.CostEstimate(flops=flops, bytes_accessed=3_000_000, transcendentals=0),
        name="couple",
    )(*args)


def senders(devices, k):
    if 2 * k != devices:
        return list(range(devices))
    return [p for p in range(devices) if (p < k) == (p % 2 == 0)]


def on_device(
    panels,
    amplitudes,
    fitted_ints,
    pno_energy,
    fock_occ,
    pno_count,
    pair_pos,
    coupling,
    coupling_lmo,
    pair_lmo,
):
    per_dev, width, pao = panels.shape
    pair_devices = lax.axis_size("pair")
    aux_devices = lax.axis_size("aux")
    block = per_dev // aux_devices
    couplings = coupling.shape[1]
    total = pair_pos.shape[0]
    rounds = pair_devices // 2
    pair = lax.axis_index("pair")
    aux = lax.axis_index("aux")

    sent = pack(panels, amplitudes, pno_count, block)
    arrived = []
    for k in range(1, rounds + 1):
        ways = [(p, (p + k) % pair_devices) for p in senders(pair_devices, k)]
        arrived.append((ways, lax.ppermute(sent, "pair", ways)))

    acc, masked = exchange(fitted_ints, panels, pno_count)

    table = jnp.concatenate([coupling.reshape(total, 2 * couplings), coupling_lmo, pair_lmo], 1)
    table = jnp.pad(table, ((0, 0), (0, 128 - table.shape[1])))
    pieces = [lax.dynamic_slice_in_dim(table, pair * per_dev, per_dev, 0)]
    for k in range(1, rounds + 1):
        source = lax.rem(pair + pair_devices - k, pair_devices) * per_dev + aux * block
        piece = lax.dynamic_slice_in_dim(table, source, block, 0)
        pieces.append(jnp.pad(piece, ((0, 8 - block), (0, 0))))
    weight_in, weight_out, block_amps = tables(
        jnp.concatenate(pieces, 0),
        pair_pos[:, None],
        fock_occ,
        amplitudes.reshape(per_dev * width, width),
        block,
        width,
        couplings,
        rounds,
    )

    own_first = aux * block
    live = iota((block, width), 1) < lax.dynamic_slice_in_dim(pno_count, own_first, block)[:, None]
    live = live[:, :, None] & live[:, None, :]
    own_energy = lax.dynamic_slice_in_dim(pno_energy, own_first, block, 0)
    own_lmo = lax.dynamic_slice_in_dim(pair_lmo, pair * per_dev + own_first, block, 0)
    occ_diag = jnp.diagonal(fock_occ)
    lmo_hot = own_lmo[:, :, None] == jnp.arange(fock_occ.shape[0], dtype=I32)
    occ_pair = jnp.sum(jnp.where(lmo_hot, occ_diag, 0.0), axis=(1, 2))
    gap = own_energy[:, :, None] + own_energy[:, None, :] - occ_pair[:, None, None]
    gap = jnp.where(live, gap, 0.0).reshape(block, width * width)
    own_amps = lax.dynamic_slice_in_dim(amplitudes, own_first, block, 0)
    own = gap * own_amps.astype(F32)

    (acc,) = couple(sent, masked, weight_in[:per_dev], acc, block, width, False, None)
    for k, (ways, block_sent) in enumerate(arrived, 1):
        acc, back = couple(
            block_sent,
            masked,
            weight_in[k * per_dev : (k + 1) * per_dev],
            acc,
            block,
            width,
            k == rounds,
            (block_amps, weight_out[(k - 1) * 8 : k * 8]),
        )
        own = own - lax.ppermute(back, "pair", [(q, p) for p, q in ways])

    left = acc.reshape(aux_devices, block, width * width)
    step = 1
    while step < aux_devices:
        bit = (aux // step) % 2
        halves = left.reshape(left.shape[0] // 2, 2, block, width * width)
        keep = lax.dynamic_index_in_dim(halves, bit, 1, False)
        give = lax.dynamic_index_in_dim(halves, 1 - bit, 1, False)
        ways = [(d, d ^ step) for d in range(aux_devices)]
        left = keep + lax.ppermute(give, "aux", ways)
        step *= 2
    return left[0] + own


def solution(mesh):
    placed = (
        P(("groups", "pair"), None, None),
        P(("groups", "pair"), None),
        P(("groups", "pair"), None, "aux", None),
        P(("groups", "pair"), None),
        P("groups", None),
        P(("groups", "pair")),
        P("groups"),
        P("groups", None, None),
        P("groups", None),
        P("groups", None),
    )
    return jax.shard_map(
        on_device,
        mesh=mesh,
        in_specs=placed,
        out_specs=P(("groups", "pair", "aux"), None),
        check_vma=False,
    )
```

time: 467 us -> 41.5 us (0.09)
  waiting for transfers between devices: 331 us -> 2.32 us
  local copies, waits for them, and re-layouts: 54.3 us -> 7.46 us
  other arithmetic: 29.6 us -> 2.4 us
  matrix products: 23.2 us -> 0 us
  Pallas kernels: 0 us -> 16.8 us
  between operations: 14.4 us -> 0.38 us
    all_to_all x2 -> x0, waiting for transfers between devices: 331 us -> none  [the longest x1 330 us: on_device(): lax.all_to_all(send_panels, 'pair', split_axis=0, concat_axis=0, tiled=True)]
    gather x12 -> x0, local copies, waits for them, and re-layouts: 39.7 us -> none  [the longest x1 15.6 us: on_device(): jnp.take(recv_panels.reshape(pair_devices * capacity, pno_width, pao_widt...]
    dot_general x6 -> x0, matrix products: 23.2 us -> none  [the longest x1 11.8 us: sandwich(): jnp.einsum(pattern_intersection, left_panels, right_panels, preferred_ele...]
    select_n x12 -> x0, other arithmetic: 21.7 us -> none  [the longest x1 14.5 us: on_device(): jnp.where(filled[:, :, None, None] > 0, send_panels, jnp.zeros_like(send_...]
    pallas_call x0 -> x6, Pallas kernels: none -> 16.8 us  [the longest x3 6.94 us: couple(): pl.pallas_call(functools.partial(couple_kernel, block, width, chunks, boo...]
    all_to_all x2 -> x0, starting transfers between devices: 13.3 us -> none  [the longest x1 6.95 us: on_device(): lax.all_to_all(send_panels, 'pair', split_axis=0, concat_axis=0, tiled=True)]
    ppermute x0 -> x6, starting transfers between devices: none -> 11.9 us  [the longest x2 7.58 us: on_device(): arrived.append((ways, lax.ppermute(sent, 'pair', ways)))]
    select_n x4 -> x0, local copies, waits for them, and re-layouts: 6.22 us -> none  [the longest x1 5.99 us: on_device(): jnp.take(recv_amps.reshape(pair_devices * capacity, pno_width * pno_width...]
  transfers between devices with their start and end apart: 3 -> 6, of which waited for: 2 -> 1; matrix products, arithmetic and copies ran while one was open for 18% -> 13% of each run, Pallas kernels for 0% -> 33%
where the time goes in v1:
time: 41.5 us; the launch traced here: 41.2 us
  Pallas kernels  16.8 us (40%)
  starting transfers between devices  11.9 us (29%)
  local copies, waits for them, and re-layouts  7.46 us (18%)
  other arithmetic  2.4 us (6%)
  waiting for transfers between devices  2.32 us (6%)
    ppermute x2, starting transfers between devices, on_device(): arrived.append((ways, lax.ppermute(sent, 'pair', ways)))  7.58 us
    pallas_call x3, Pallas kernels, couple(): pl.pallas_call(functools.partial(couple_kernel, block, width, chunks, boo...  6.94 us
    pallas_call x1, Pallas kernels, exchange(): pl.pallas_call(functools.partial(exchange_kernel, group, width), out_shap...  6.37 us
    unnamed x40, local copies, waits for them, and re-layouts  3.8 us
    ppermute x2, starting transfers between devices, on_device(): own = own - lax.ppermute(back, 'pair', [(q, p) for p, q in ways])  2.68 us
    pallas_call x1, Pallas kernels, tables(): pl.pallas_call(functools.partial(tables_kernel, block, width, couplings,...  2.62 us
    ppermute x2, waiting for transfers between devices, on_device(): own = own - lax.ppermute(back, 'pair', [(q, p) for p, q in ways])  2.31 us
    ppermute x2, starting transfers between devices, on_device(): left = keep + lax.ppermute(give, 'aux', ways)  1.63 us
  transfers between devices with their start and end apart: 6, of which 1 were waited for; matrix products, arithmetic and copies ran while one was open for 13% of the time, Pallas kernels for 33%

profile of v1, /device:TPU:0, one launch (start us, length us, event | category | flops | bytes accessed | tf_op | source)
XLA Modules:
  0.0 41.2 jit_solution(3859496029172053643)
XLA Ops:
  0.0 1.3 %copy-done.3 = bf16[16,48,768]{2,1,0:T(8,128)(2,1)S(1)} copy-done((bf16[16,48,768]{2,1,0:T(8,128)(2,1)S(1)}, bf16[16,48,768]{2,1,0:T(8,128)(2,1)}, u32[]{:S(2)}) %copy-start.3) | copy-done | bytes 1179672
  1.3 0.9 %copy-done.5 = bf16[16,2304]{1,0:T(8,128)(2,1)S(1)} copy-done((bf16[16,2304]{1,0:T(8,128)(2,1)S(1)}, bf16[16,2304]{1,0:T(8,128)(2,1)}, u32[]{:S(2)}) %copy-start.5) | copy-done | bytes 73752
  2.2 0.7 %copy-done.10 = s32[16]{0:T(128)S(1)} copy-done((s32[16]{0:T(128)S(1)}, s32[16]{0:T(128)}, u32[]{:S(2)}) %copy-start.10) | copy-done | bytes 88
  2.9 0.8 %pack.1.refs_0_ = bf16[208,768]{1,0:T(8,128)(2,1)S(1)} custom-call(bf16[16,48,768]{2,1,0:T(8,128)(2,1)S(1)} %copy-done.3, bf16[16,2304]{1,0:T(8,128)(2,1)S(1)} %copy-done.5, s32[16]{0:T(128)S(1)} %copy-done.10), custom_call_target="tpu_custom_call" | custom-call | tf_op jit(solution)/shard_map/pack/pallas_call | solution.py:74
  3.7 3.1 %collective-permute-start.1 = (bf16[208,768]{1,0:T(8,128)(2,1)S(1)}, bf16[208,768]{1,0:T(8,128)(2,1)}, u32[]{:S(2)}, u32[]{:S(2)}) collective-permute-start(bf16[208,768]{1,0:T(8,128)(2,1)S(1)} %pack.1.refs_0_), channel_id=1, source_target_pairs={{0,4},{4,8},{8,12},{12,0},{1,5},{5,9},{9,13},{13,1},{2,6},{6,10},{... | collective-permute-start | bytes 958472 | tf_op jit(solution)/shard_map/ppermute | solution.py:319
  6.8 4.5 %collective-permute-start = (bf16[208,768]{1,0:T(8,128)(2,1)S(1)}, bf16[208,768]{1,0:T(8,128)(2,1)S(1)}, u32[]{:S(2)}, u32[]{:S(2)}) collective-permute-start(bf16[208,768]{1,0:T(8,128)(2,1)S(1)} %pack.1.refs_0_), channel_id=1, source_target_pairs={{0,8},{12,4},{1,9},{13,5},{2,10},{14,6},{3,11},{15,7},{16,24},{28,... | collective-permute-start | bytes 958472 | tf_op jit(solution)/shard_map/ppermute | solution.py:319
  11.3 0.2 reshape.55.amps
  11.6 0.5 %or_bitcast_fusion = s32[64]{0:T(128)} fusion(), kind=kLoop, calls=%fused_computation.18 | loop fusion | flops 256 | bytes 256 | tf_op jit(solution)/shard_map/jit(diagonal)/cond/branch_0_fun/concatenate | solution.py:346
  12.2 0.1 copy.26
  12.3 0.1 copy.27
  12.4 0.1 copy.28.pos
  12.5 0.1 pad_add_fusion
  12.7 2.6 %tables.1 = (f32[48,192]{1,0:T(8,128)S(1)}, f32[16,768]{1,0:T(8,128)S(1)}, bf16[768,768]{1,0:T(8,128)(2,1)S(1)}) custom-call(s32[32,128]{1,0:T(8,128)S(1)} %pad_add_fusion.1.table, s32[64,1]{1,0:T(8,128)S(1)} %copy.28.pos, f32[64,64]{1,0:T(8,128)S(1)} %copy-done.1, bf16[768,48]{1,0:T(8,128)(2,1)S(1)} %reshape.55.amps), custom_call_target="tpu_custom_call" | custom-call | flops 2000000000 | bytes 4000000 | tf_op jit(solution)/shard_map/tables/pallas_call | solution.py:179
  15.3 0.6 %fusion.1 = (f32[16,192]{1,0:T(8,128)}, f32[16,192]{1,0:T(8,128)}, f32[16,192]{1,0:T(8,128)}) fusion(f32[48,192]{1,0:T(8,128)S(1)} %get-tuple-element.15), kind=kLoop, calls=%fused_computation.20 | loop fusion | bytes 73728 | tf_op jit(solution)/shard_map/slice | solution.py:354
  15.9 6.4 %exchange.1 = (f32[768,48]{1,0:T(8,128)S(1)}, bf16[768,768]{1,0:T(8,128)(2,1)S(1)}) custom-call(bf16[16,2,128,768]{3,2,1,0:T(8,128)(2,1)S(1)} %copy-done.2, bf16[16,48,768]{2,1,0:T(8,128)(2,1)S(1)} %copy-done.4, s32[16]{0:T(128)S(1)} %copy-done.11), custom_call_target="tpu_custom_call" | custom-call | flops 1557135360 | bytes 8650752 | tf_op jit(solution)/shard_map/exchange/pallas_call | solution.py:105
  22.3 1.5 %gather_fusion = f32[64]{0:T(128)} fusion(f32[64,64]{1,0:T(8,128)S(1)} %copy-done.1, s32[64]{0:T(128)} %or_bitcast_fusion), kind=kCustom, calls=%fused_computation | custom fusion | bytes 1024 | tf_op jit(solution)/shard_map/jit(diagonal)/cond/branch_0_fun/gather | solution.py:346
  23.8 0.7 %dynamic_slice.36 = s32[4]{0:T(128)S(1)} dynamic-slice(s32[16]{0:T(128)} %count.3, s32[]{:T(128)S(6)} %select_n.70), dynamic_slice_sizes={4} | dynamic-slice | bytes 36 | tf_op jit(solution)/shard_map/dynamic_slice | solution.py:342
  24.6 0.7 %broadcast_and_fusion = pred[4,48,48]{2,1,0:T(8,128)(4,1)} fusion(pred[4,48]{1,0:T(4,128)(4,1)S(1)} %iota_compare_fusion.1), kind=kLoop, calls=%fused_computation.4 | loop fusion | flops 9216 | bytes 9408 | tf_op jit(solution)/shard_map/and | solution.py:343
  25.3 0.7 %copy-done.9 = f32[16,192]{1,0:T(8,128)S(1)} copy-done((f32[16,192]{1,0:T(8,128)S(1)}, f32[16,192]{1,0:T(8,128)}, u32[]{:S(2)}) %copy-start.9) | copy-done | bytes 12312
  26.1 1.4 %couple.3.refs_3_ = f32[768,48]{1,0:T(8,128)S(1)} custom-call(bf16[208,768]{1,0:T(8,128)(2,1)S(1)} %pack.1.refs_0_, bf16[768,768]{1,0:T(8,128)(2,1)S(1)} %get-tuple-element.14.refs_1_, f32[16,192]{1,0:T(8,128)S(1)} %copy-done.9, f32[768,48]{1,0:T(8,128)S(1)} %get-tuple-element.16.refs_3_), custom_call_target="tpu_custom_call" | custom-call | flops 283115520 | bytes 3000000 | tf_op jit(solution)/shard_map/couple/pallas_call | solution.py:275
  27.4 0.1 broadcast_add_fusion
  27.6 3.3 %couple.4 = (f32[768,48]{1,0:T(8,128)S(1)}, f32[4,2304]{1,0:T(4,128)S(1)}) custom-call(bf16[208,768]{1,0:T(8,128)(2,1)} %collective-permute-done.1.refs_0_, bf16[768,768]{1,0:T(8,128)(2,1)S(1)} %get-tuple-element.14.refs_1_, f32[16,192]{1,0:T(8,128)S(1)} %copy-done.8, f32[768,48]{1,0:T(8,128)S(1)} %couple.3.refs_3_, ...), custom_call_target="tpu_custom_call" | custom-call | flops 736100352 | bytes 3000000 | tf_op jit(solution)/shard_map/couple/pallas_call | solution.py:275
  30.9 2.3 %couple.5 = (f32[16,2304]{1,0:T(8,128)S(1)}, f32[4,2304]{1,0:T(4,128)S(1)}) custom-call(bf16[208,768]{1,0:T(8,128)(2,1)S(1)} %collective-permute-done.refs_0_, bf16[768,768]{1,0:T(8,128)(2,1)S(1)} %get-tuple-element.14.refs_1_, f32[16,192]{1,0:T(8,128)S(1)} %copy-done.7, f32[768,48]{1,0:T(8,128)S(1)} %get-tuple-element.19.refs_3_, ...), custom_call_target="tpu_custom_call" | custom-call | flops 736100352 | bytes 3000000 | tf_op jit(solution)/shard_map/couple/pallas_call | solution.py:275
  33.4 0.1 constant_dynamic-slice_fusion
  33.4 1.3 %collective-permute-start.5 = (f32[4,2304]{1,0:T(4,128)S(1)}, f32[4,2304]{1,0:T(4,128)S(1)}, u32[]{:S(2)}, u32[]{:S(2)}) collective-permute-start(f32[4,2304]{1,0:T(4,128)S(1)} %get-tuple-element.22), channel_id=1, source_target_pairs={{8,0},{4,12},{9,1},{5,13},{10,2},{6,14},{11,3},{7,15},{24,16},{20,... | collective-permute-start | bytes 110600 | tf_op jit(solution)/shard_map/ppermute | solution.py:366
  34.7 1.4 %collective-permute-start.4 = (f32[4,2304]{1,0:T(4,128)S(1)}, f32[4,2304]{1,0:T(4,128)S(1)}, u32[]{:S(2)}, u32[]{:S(2)}) collective-permute-start(f32[4,2304]{1,0:T(4,128)S(1)} %get-tuple-element.21), channel_id=1, source_target_pairs={{4,0},{8,4},{12,8},{0,12},{5,1},{9,5},{13,9},{1,13},{6,2},{10,6},{... | collective-permute-start | bytes 110600 | tf_op jit(solution)/shard_map/ppermute | solution.py:366
  36.2 1.6 %collective-permute-start.3 = (f32[1,4,2304]{2,1,0:T(4,128)S(1)}, f32[1,4,2304]{2,1,0:T(4,128)S(1)}, u32[]{:S(2)}, u32[]{:S(2)}) collective-permute-start(f32[1,4,2304]{2,1,0:T(4,128)S(1)} %constant_dynamic-slice_fusion.2), channel_id=1, source_target_pairs={{0,2},{1,3},{2,0},{3,1},{4,6},{5,7},{6,4},{7,5},{8,10},{9,11},{10,... | collective-permute-start | bytes 110600 | tf_op jit(solution)/shard_map/ppermute | solution.py:376
  37.7 0.2 select_reduce_fusion
  37.9 0.1 add.112
  38.0 0.1 and.43
  38.2 2.3 %collective-permute-done.5 = f32[4,2304]{1,0:T(4,128)S(1)} collective-permute-done((f32[4,2304]{1,0:T(4,128)S(1)}, f32[4,2304]{1,0:T(4,128)S(1)}, u32[]{:S(2)}, u32[]{:S(2)}) %collective-permute-start.5) | collective-permute-done | bytes 36896 | tf_op jit(solution)/shard_map/ppermute | solution.py:366
  40.5 0.7 %bitcast_add_fusion.1 = f32[4,2304]{1,0:T(4,128)} fusion(f32[4,2304]{1,0:T(4,128)S(1)} %collective-permute-done.5, f32[4,2304]{1,0:T(4,128)S(1)} %collective-permute-done.4, pred[4,2304]{1,0:T(4,128)(4,1)S(1)} %and.43, f32[4,2304]{1,0:T(4,128)S(1)} %add.112, f32[1,4,2304]{2,1,0:T(4,128)S(1)} %collective-permute-done.3, f32[2,4,2304]{2,1,0:T(4,128)S(1)} %bitcast_add_fusion, ...), kind=kLoop, calls=%fused_computation.5 | loop fusion | flops 73728 | bytes 248856 | tf_op jit(solution)/shard_map/add | solution.py:378
  (51 shorter events, 0.5 us)
Async XLA Ops:
  0.0 25.3 %copy-start = (f32[16,48]{1,0:T(8,128)S(1)}, f32[16,48]{1,0:T(8,128)}, u32[]{:S(2)}) copy-start(f32[16,48]{1,0:T(8,128)} %param.13) | copy-start | bytes 9220
  0.0 12.6 %copy-start.1 = (f32[64,64]{1,0:T(8,128)S(1)}, f32[64,64]{1,0:T(8,128)}, u32[]{:S(2)}) copy-start(f32[64,64]{1,0:T(8,128)} %fock.1) | copy-start | bytes 49156
  0.0 1.3 %copy-start.3 = (bf16[16,48,768]{2,1,0:T(8,128)(2,1)S(1)}, bf16[16,48,768]{2,1,0:T(8,128)(2,1)}, u32[]{:S(2)}) copy-start(bf16[16,48,768]{2,1,0:T(8,128)(2,1)} %panels.3) | copy-start | bytes 3538948
  1.3 0.9 %copy-start.5 = (bf16[16,2304]{1,0:T(8,128)(2,1)S(1)}, bf16[16,2304]{1,0:T(8,128)(2,1)}, u32[]{:S(2)}) copy-start(bf16[16,2304]{1,0:T(8,128)(2,1)} %amps.1) | copy-start | bytes 221188
  2.2 0.7 %copy-start.10 = (s32[16]{0:T(128)S(1)}, s32[16]{0:T(128)}, u32[]{:S(2)}) copy-start(s32[16]{0:T(128)} %count.3) | copy-start | bytes 196
  2.8 8.5 %copy-start.6 = (bf16[16,2304]{1,0:T(8,128)(2,1)S(1)}, bf16[16,2304]{1,0:T(8,128)(2,1)}, u32[]{:S(2)}) copy-start(bf16[16,2304]{1,0:T(8,128)(2,1)} %amps.1) | copy-start | bytes 221188
  2.8 9.3 %copy-start.13 = (s32[64,28,2]{0,2,1:T(2,128)S(1)}, s32[64,28,2]{0,2,1:T(2,128)}, u32[]{:S(2)}) copy-start(s32[64,28,2]{0,2,1:T(2,128)} %param.17) | copy-start | bytes 43012
  2.8 9.3 %copy-start.14 = (s32[64,28]{0,1:T(8,128)S(1)}, s32[64,28]{0,1:T(8,128)}, u32[]{:S(2)}) copy-start(s32[64,28]{0,1:T(8,128)} %param.18) | copy-start | bytes 21508
  2.8 9.4 %copy-start.15 = (s32[64,2]{0,1:T(2,128)S(1)}, s32[64,2]{0,1:T(2,128)}, u32[]{:S(2)}) copy-start(s32[64,2]{0,1:T(2,128)} %param.19) | copy-start | bytes 1540
  2.9 9.5 %copy-start.18 = (s32[64]{0:T(128)S(1)}, s32[64]{0:T(128)}, u32[]{:S(2)}) copy-start(s32[64]{0:T(128)} %param.16) | copy-start | bytes 772
  3.7 23.8 %collective-permute-start.1 = (bf16[208,768]{1,0:T(8,128)(2,1)S(1)}, bf16[208,768]{1,0:T(8,128)(2,1)}, u32[]{:S(2)}, u32[]{:S(2)}) collective-permute-start(bf16[208,768]{1,0:T(8,128)(2,1)S(1)} %pack.1.refs_0_), channel_id=1, source_target_pairs={{0,4},{4,8},{8,12},{12,0},{1,5},{5,9},{9,13},{13,1},{2,6},{6,10},{... | collective-permute-start | bytes 958472 | tf_op jit(solution)/shard_map/ppermute | solution.py:319
  6.8 24.1 %collective-permute-start = (bf16[208,768]{1,0:T(8,128)(2,1)S(1)}, bf16[208,768]{1,0:T(8,128)(2,1)S(1)}, u32[]{:S(2)}, u32[]{:S(2)}) collective-permute-start(bf16[208,768]{1,0:T(8,128)(2,1)S(1)} %pack.1.refs_0_), channel_id=1, source_target_pairs={{0,8},{12,4},{1,9},{13,5},{2,10},{14,6},{3,11},{15,7},{16,24},{28,... | collective-permute-start | bytes 958472 | tf_op jit(solution)/shard_map/ppermute | solution.py:319
  12.6 3.3 %copy-start.2 = (bf16[16,2,128,768]{3,2,1,0:T(8,128)(2,1)S(1)}, bf16[16,2,128,768]{3,2,1,0:T(8,128)(2,1)}, u32[]{:S(2)}) copy-start(bf16[16,2,128,768]{3,2,1,0:T(8,128)(2,1)} %fit.1) | copy-start | bytes 18874372
  12.6 3.3 %copy-start.4 = (bf16[16,48,768]{2,1,0:T(8,128)(2,1)S(1)}, bf16[16,48,768]{2,1,0:T(8,128)(2,1)}, u32[]{:S(2)}) copy-start(bf16[16,48,768]{2,1,0:T(8,128)(2,1)} %panels.3) | copy-start | bytes 3538948
  12.7 3.3 %copy-start.11 = (s32[16]{0:T(128)S(1)}, s32[16]{0:T(128)}, u32[]{:S(2)}) copy-start(s32[16]{0:T(128)} %count.3) | copy-start | bytes 196
  25.3 0.7 %copy-start.9 = (f32[16,192]{1,0:T(8,128)S(1)}, f32[16,192]{1,0:T(8,128)}, u32[]{:S(2)}) copy-start(f32[16,192]{1,0:T(8,128)} %get-tuple-element.25.refs_2_) | copy-start | bytes 36868
  26.1 1.5 %copy-start.8 = (f32[16,192]{1,0:T(8,128)S(1)}, f32[16,192]{1,0:T(8,128)}, u32[]{:S(2)}) copy-start(f32[16,192]{1,0:T(8,128)} %get-tuple-element.26.refs_2_) | copy-start | bytes 36868
  27.6 3.3 %copy-start.7 = (f32[16,192]{1,0:T(8,128)S(1)}, f32[16,192]{1,0:T(8,128)}, u32[]{:S(2)}) copy-start(f32[16,192]{1,0:T(8,128)} %get-tuple-element.27.refs_2_) | copy-start | bytes 36868
  30.9 2.5 %copy-start.16 = (s32[64,2]{0,1:T(2,128)S(1)}, s32[64,2]{0,1:T(2,128)}, u32[]{:S(2)}) copy-start(s32[64,2]{0,1:T(2,128)} %param.19) | copy-start | bytes 1540
  30.9 6.9 %copy-start.17 = (f32[64]{0:T(128)S(1)}, f32[64]{0:T(128)}, u32[]{:S(2)}) copy-start(f32[64]{0:T(128)} %gather_fusion) | copy-start | bytes 772
  30.9 7.2 %copy-start.12 = (pred[4,48,48]{2,1,0:T(8,128)(4,1)S(1)}, pred[4,48,48]{2,1,0:T(8,128)(4,1)}, u32[]{:S(2)}) copy-start(pred[4,48,48]{2,1,0:T(8,128)(4,1)} %broadcast_and_fusion) | copy-start | bytes 27652
  33.3 2.9 %collective-permute-start.2 = (f32[2,4,2304]{2,1,0:T(4,128)S(1)}, f32[2,4,2304]{2,1,0:T(4,128)S(1)}, u32[]{:S(2)}, u32[]{:S(2)}) collective-permute-start(f32[2,4,2304]{2,1,0:T(4,128)S(1)} %dynamic-slice_bitcast_fusion), channel_id=1, source_target_pairs={{0,1},{1,0},{2,3},{3,2},{4,5},{5,4},{6,7},{7,6},{8,9},{9,8},{10,11... | collective-permute-start | bytes 221192 | tf_op jit(solution)/shard_map/ppermute | solution.py:376
  33.4 7.0 %collective-permute-start.5 = (f32[4,2304]{1,0:T(4,128)S(1)}, f32[4,2304]{1,0:T(4,128)S(1)}, u32[]{:S(2)}, u32[]{:S(2)}) collective-permute-start(f32[4,2304]{1,0:T(4,128)S(1)} %get-tuple-element.22), channel_id=1, source_target_pairs={{8,0},{4,12},{9,1},{5,13},{10,2},{6,14},{11,3},{7,15},{24,16},{20,... | collective-permute-start | bytes 110600 | tf_op jit(solution)/shard_map/ppermute | solution.py:366
  34.7 5.8 %collective-permute-start.4 = (f32[4,2304]{1,0:T(4,128)S(1)}, f32[4,2304]{1,0:T(4,128)S(1)}, u32[]{:S(2)}, u32[]{:S(2)}) collective-permute-start(f32[4,2304]{1,0:T(4,128)S(1)} %get-tuple-element.21), channel_id=1, source_target_pairs={{4,0},{8,4},{12,8},{0,12},{5,1},{9,5},{13,9},{1,13},{6,2},{10,6},{... | collective-permute-start | bytes 110600 | tf_op jit(solution)/shard_map/ppermute | solution.py:366
  36.2 4.3 %collective-permute-start.3 = (f32[1,4,2304]{2,1,0:T(4,128)S(1)}, f32[1,4,2304]{2,1,0:T(4,128)S(1)}, u32[]{:S(2)}, u32[]{:S(2)}) collective-permute-start(f32[1,4,2304]{2,1,0:T(4,128)S(1)} %constant_dynamic-slice_fusion.2), channel_id=1, source_target_pairs={{0,2},{1,3},{2,0},{3,1},{4,6},{5,7},{6,4},{7,5},{8,10},{9,11},{10,... | collective-permute-start | bytes 110600 | tf_op jit(solution)/shard_map/ppermute | solution.py:376

commit v2 on v0

v2 whole, which is shorter than its diff:
```python
import functools

import jax
import jax.numpy as jnp
from jax import lax
from jax.experimental import pallas as pl
from jax.experimental.pallas import tpu as pltpu
from jax.sharding import PartitionSpec as P

BF16 = jnp.bfloat16
F32 = jnp.float32
I32 = jnp.int32
HIGHEST = lax.Precision.HIGHEST
VMEM_BYTES = 48 * 1024 * 1024
PACK_VMEM_BYTES = 61 * 1024 * 1024
LOCAL_VMEM_BYTES = 48 * 1024 * 1024


def dot_nn(a, b, precision=None):
    return lax.dot_general(
        a, b, (((1,), (0,)), ((), ())), precision=precision, preferred_element_type=F32
    )


def dot_nt(a, b, precision=None):
    return lax.dot_general(
        a, b, (((1,), (1,)), ((), ())), precision=precision, preferred_element_type=F32
    )


def iota(shape, dim):
    return lax.broadcasted_iota(I32, shape, dim)


def floor_div(values, by):
    return jnp.floor((values.astype(F32) + 0.5) * (1.0 / by)).astype(I32)


def whole(memory_space=pltpu.VMEM):
    return pl.BlockSpec(memory_space=memory_space)


def lane_in(width, lanes):
    lane = iota((1, lanes), 1)
    block = floor_div(lane, width)
    return block, lane - width * block


def row_in(width, rows):
    row = iota((rows, 1), 0)
    block = floor_div(row, width)
    return block, row - width * block


def fold_diagonal(square, width):
    lanes = square.shape[1]
    block, _ = lane_in(width, lanes)
    out = jnp.zeros((width, lanes), F32)
    for n in range(lanes // width):
        out += jnp.where(block == n, square[n * width : (n + 1) * width, :], 0.0)
    return out


def tail_rows(block, chunks):
    return -(-(block * chunks) // 16) * 16


def masked_rows(panel, count):
    live = iota(panel.shape, 0) < count
    return jnp.where(live, panel.astype(F32), 0.0).astype(BF16)


def split_high_low(values):
    high = values.astype(BF16)
    return high, (values - high.astype(F32)).astype(BF16)


def pack_kernel(block, width, chunks, panels, amps, count, out, held, amps_held, count_held, sems):
    first = lax.axis_index("aux") * block
    copies = [
        pltpu.make_async_copy(panels.at[pl.ds(first, block)], held, sems.at[0]),
        pltpu.make_async_copy(amps, amps_held, sems.at[1]),
        pltpu.make_async_copy(count, count_held, sems.at[2]),
    ]
    for copy in copies:
        copy.start()
    pao = held.shape[2]
    pairs = amps_held.shape[0]
    tail = tail_rows(block, chunks)
    row = iota((tail, pairs), 0)
    source = iota((tail, pairs), 1)
    for copy in copies:
        copy.wait()
    rows = jnp.zeros((tail, pao), F32)
    for chunk in range(chunks):
        inside = (row >= chunk * block) & (row < (chunk + 1) * block)
        hot = (inside & (source == first + row - chunk * block)).astype(F32).astype(BF16)
        rows += dot_nn(hot, amps_held[:, chunk * pao : (chunk + 1) * pao])
    out[block * width :, :] = rows.astype(BF16)
    for j in range(block):
        out[j * width : (j + 1) * width, :] = masked_rows(held[j], count_held[first + j])


def pack(panels, amps, count, block):
    pairs, width, pao = panels.shape
    chunks = width * width // pao
    rows = block * width + tail_rows(block, chunks)
    return pl.pallas_call(
        functools.partial(pack_kernel, block, width, chunks),
        out_shape=jax.ShapeDtypeStruct((rows, pao), BF16),
        in_specs=[whole(pltpu.HBM)] * 3,
        out_specs=whole(),
        scratch_shapes=[
            pltpu.VMEM((block, width, pao), BF16),
            pltpu.VMEM(amps.shape, BF16),
            pltpu.SMEM(count.shape, I32),
            pltpu.SemaphoreType.DMA((3,)),
        ],
        compiler_params=pltpu.CompilerParams(vmem_limit_bytes=PACK_VMEM_BYTES),
        name="pack",
    )(panels, amps, count)


def local_kernel(
    block,
    width,
    ways,
    coupling,
    orbital,
    lmo,
    pos,
    fock,
    amps,
    energy,
    count,
    fit,
    panels,
    weight_in,
    weight_out,
    block_amps,
    own,
    masked,
    out,
    weight,
    fock_of,
    held,
    panels_held,
    count_held,
    both,
    sems,
):
    copies = [
        pltpu.make_async_copy(count, count_held, sems.at[0]),
        pltpu.make_async_copy(panels, panels_held, sems.at[1]),
    ]
    groups = fit.shape[0] // block
    fits = []
    for group in range(groups):
        part = pl.ds(group * block, block)
        fits.append(pltpu.make_async_copy(fit.at[part], held.at[part], sems.at[2 + group]))
    for copy in copies + fits:
        copy.start()
    total = pos.shape[1]
    occ = fock.shape[0]
    couplings = orbital.shape[0]
    per_dev = energy.shape[0]
    pair_devices = total // per_dev
    pair = lax.axis_index("pair")
    first = lax.axis_index("aux") * block
    here = pos[...] == iota((total, total), 0)
    label_at = jnp.sum(jnp.where(here, iota((total, total), 1), 0), axis=1, keepdims=True)
    level = iota((occ, total), 0)
    hot_i = (lmo[0:1, :] == level).astype(F32)
    hot_j = (lmo[1:2, :] == level).astype(F32)
    fock_of[0] = dot_nn(fock[...], hot_j, HIGHEST)
    fock_of[1] = lax.dot_general(
        fock[...], hot_i, (((0,), (0,)), ((), ())), precision=HIGHEST, preferred_element_type=F32
    )
    weight[...] = jnp.zeros_like(weight)

    def add(c, carry):
        hot_k = orbital[pl.ds(c, 1), :] == level
        for h in range(2):
            value = jnp.sum(jnp.where(hot_k, fock_of[h], 0.0), axis=0, keepdims=True)
            named = coupling[pl.ds(2 * c + h, 1), :] == label_at
            weight[...] += jnp.where(named, value, 0.0)
        return carry

    lax.fori_loop(0, couplings, add, 0, unroll=4)

    def of_pairs(rows, start):
        hot = (iota((rows, total), 1) == start + iota((rows, total), 0)).astype(F32)
        return dot_nt(hot, weight[...], HIGHEST)

    wide = per_dev * width
    thin = block * width
    wide_pair, wide_pno = lane_in(width, wide)
    thin_pair, _ = lane_in(width, thin)
    mine = of_pairs(per_dev, pair * per_dev)
    local = (iota((total, wide), 0) == pair * per_dev + wide_pair).astype(F32)
    for k in range(len(ways) + 1):
        start = pair
        if k > 0:
            start = jnp.int32(-pair_devices)
            for sender, receiver in ways[k - 1]:
                start = jnp.where(pair == receiver, sender, start)
        source = start * per_dev + first
        spread = (iota((total, thin), 0) == source + thin_pair).astype(F32)
        weight_in[k] = dot_nn(mine, spread, HIGHEST)
        if k > 0:
            weight_out[k - 1] = dot_nn(of_pairs(8, source), local, HIGHEST)

    repeat = (iota((width, wide), 0) == wide_pno).astype(F32).astype(BF16)
    tiled = dot_nn(amps[...], repeat)
    row_pair, _ = row_in(width, wide)
    block_amps[...] = jnp.where(row_pair == wide_pair, tiled, 0.0).astype(BF16)

    for copy in copies:
        copy.wait()
    across = iota((occ, occ), 0) == iota((occ, occ), 1)
    diagonal = jnp.sum(jnp.where(across, fock[...], 0.0), axis=1, keepdims=True)
    gap_of = jnp.sum((hot_i + hot_j) * diagonal, axis=0, keepdims=True)
    row = iota((width, width), 0)
    column = iota((width, width), 1)
    for j in range(block):
        at = iota((1, total), 1) == pair * per_dev + first + j
        gap = jnp.sum(jnp.where(at, gap_of, 0.0), axis=1, keepdims=True)
        flat = energy[pl.ds(first + j, 1), :]
        upright = jnp.sum(jnp.where(row == column, flat, 0.0), axis=1, keepdims=True)
        live = count_held[first + j]
        values = amps[pl.ds((first + j) * width, width), :].astype(F32)
        term = (upright + flat - gap) * values
        own[:, j * width : (j + 1) * width] = jnp.where((row < live) & (column < live), term, 0.0)

    functions = held.shape[2]
    pao = held.shape[3]
    for p in range(per_dev):
        masked[p * width : (p + 1) * width, :] = masked_rows(panels_held[p], count_held[p])
    for group in range(groups):
        fits[group].wait()
        for p in range(group * block, (group + 1) * block):
            rows = slice(p * width, (p + 1) * width)
            if functions % 128 == 0:
                fitted = dot_nt(masked[rows, :], held[p].reshape(2 * functions, pao)).astype(BF16)
                both[0, rows, :] = fitted[:, :functions]
                both[1, rows, :] = fitted[:, functions:]
            else:
                for h in range(2):
                    both[h, rows, :] = dot_nt(masked[rows, :], held[p, h]).astype(BF16)
        rows = slice(group * thin, (group + 1) * thin)
        out[group] = fold_diagonal(dot_nt(both[0, rows, :], both[1, rows, :]), width)


def local(coupling, orbital, lmo, pos, fock, amps, energy, count, fit, panels, block, ways):
    rounds = len(ways)
    wide, width = amps.shape
    per_dev, _, pao = panels.shape
    total = pos.shape[1]
    occ = fock.shape[0]
    groups = per_dev // block
    thin = block * width
    return pl.pallas_call(
        functools.partial(local_kernel, block, width, ways),
        out_shape=(
            jax.ShapeDtypeStruct((rounds + 1, per_dev, thin), F32),
            jax.ShapeDtypeStruct((rounds, 8, wide), F32),
            jax.ShapeDtypeStruct((wide, wide), BF16),
            jax.ShapeDtypeStruct((width, thin), F32),
            jax.ShapeDtypeStruct((wide, pao), BF16),
            jax.ShapeDtypeStruct((groups, width, thin), F32),
        ),
        in_specs=[whole()] * 7 + [whole(pltpu.HBM)] * 3,
        out_specs=(whole(),) * 6,
        scratch_shapes=[
            pltpu.VMEM((total, total), F32),
            pltpu.VMEM((2, occ, total), F32),
            pltpu.VMEM(fit.shape, BF16),
            pltpu.VMEM(panels.shape, BF16),
            pltpu.SMEM(count.shape, I32),
            pltpu.VMEM((2, wide, fit.shape[2]), BF16),
            pltpu.SemaphoreType.DMA((2 + groups,)),
        ],
        compiler_params=pltpu.CompilerParams(vmem_limit_bytes=LOCAL_VMEM_BYTES),
        cost_estimate=pl.CostEstimate(
            flops=6_000_000_000, bytes_accessed=fit.size * 2, transcendentals=0
        ),
        name="local",
    )(coupling, orbital, lmo, pos, fock, amps, energy, count, fit, panels)


def unpack_amps(sent, block, width):
    thin = block * width
    pao = sent.shape[1]
    per_chunk = pao // width
    row_pair, row_pno = row_in(width, thin)
    row_chunk = floor_div(row_pno, per_chunk)
    tail = sent.shape[0] - thin
    pick = (iota((thin, tail), 1) == row_chunk * block + row_pair).astype(F32).astype(BF16)
    picked = dot_nn(pick, sent[thin:, :])
    lane_block, _ = lane_in(width, pao)
    at = row_pno - per_chunk * row_chunk == lane_block
    picked = jnp.where(at, picked, 0.0).astype(BF16)
    _, down_pno = row_in(width, pao)
    across_pair, across_pno = lane_in(width, thin)
    fold = (down_pno == across_pno).astype(F32).astype(BF16)
    return jnp.where(row_pair == across_pair, dot_nn(picked, fold), 0.0).astype(BF16)


def add_in(block, width, masked, parts, put):
    thin = block * width
    inters, halves = [], []
    for sent, _ in parts:
        inter = dot_nt(masked[...], sent[:thin, :]).astype(BF16)
        half = dot_nn(inter, unpack_amps(sent, block, width)).astype(BF16).astype(F32)
        inters.append(inter)
        halves.append(half)
    for group in range(masked.shape[0] // thin):
        square = jnp.zeros((thin, thin), F32)
        for (_, weight_in), inter, half in zip(parts, inters, halves):
            scaled = []
            for t in range(group * block, (group + 1) * block):
                scaled.append(half[t * width : (t + 1) * width, :] * weight_in[t : t + 1, :])
            high, low = split_high_low(jnp.concatenate(scaled, 0))
            mine = inter[group * thin : (group + 1) * thin, :]
            square += dot_nt(high, mine) + dot_nt(low, mine)
        put(group, fold_diagonal(square, width))


def add_back(block, width, sent, masked, block_amps, weight_out):
    thin = block * width
    inter = dot_nt(sent[:thin, :], masked[...]).astype(BF16)
    half = dot_nn(inter, block_amps[...]).astype(BF16).astype(F32)
    parts = []
    for s in range(block):
        parts.append(half[s * width : (s + 1) * width, :] * weight_out[s : s + 1, :])
    high, low = split_high_low(jnp.concatenate(parts, 0))
    return fold_diagonal(dot_nt(high, inter) + dot_nt(low, inter), width)


def back_kernel(block, width, sent, masked, block_amps, weight_out, out):
    out[...] = as_sent(add_back(block, width, sent, masked, block_amps, weight_out)).astype(BF16)


def both_kernel(block, width, *refs):
    masked, block_amps, acc, sent, weight_in, weight_out = refs[:6]
    out, back = refs[-2:]
    parts = [(sent, weight_in)] + ([refs[6:8]] if len(refs) > 8 else [])

    def put(group, value):
        out[group] = acc[group] - value

    back[...] = as_sent(add_back(block, width, sent, masked, block_amps, weight_out)).astype(BF16)
    add_in(block, width, masked, parts, put)


def last_kernel(block, width, returned, sent, masked, weight_in, acc, own, *refs):
    backs, outs, held = refs[:returned], refs[returned:-1], refs[-1]

    def put(group, value):
        held[group] = acc[group] - value

    add_in(block, width, masked, [(sent, weight_in)], put)
    aux = lax.axis_index("aux")
    mine = as_sent(held[aux] + own[...])
    for back in backs:
        mine -= back[...].astype(F32)
    outs[0][...] = mine
    for k in range(1, len(outs)):
        outs[k][...] = as_sent(held[lax.bitwise_xor(aux, k)]).astype(BF16)


def finish_kernel(block, width, count, *refs):
    parts, out, held = refs[:count], refs[count], refs[count + 1]
    total = parts[0][...]
    for part in parts[1:-1]:
        total += part[...].astype(F32)
    total -= parts[-1][...].astype(F32)
    for s in range(block):
        for r in range(0, width, 16):
            lane = r // 16 * block * width + s * width
            held[s * width + r : s * width + r + 16, :] = total[:, lane : lane + width]
    for a in range(width):
        out[:, a * width : (a + 1) * width] = held[pl.ds(a, block, stride=width), :]


def as_sent(values):
    rows = values.shape[0]
    return jnp.concatenate([values[r : r + 16, :] for r in range(0, rows, 16)], 1)


def call(kernel, name, out_shape, args, flops, scratch=()):
    many = isinstance(out_shape, tuple)
    return pl.pallas_call(
        kernel,
        out_shape=out_shape,
        in_specs=[whole()] * len(args),
        out_specs=(whole(),) * len(out_shape) if many else whole(),
        scratch_shapes=list(scratch),
        compiler_params=pltpu.CompilerParams(vmem_limit_bytes=VMEM_BYTES),
        cost_estimate=pl.CostEstimate(flops=flops, bytes_accessed=3_000_000, transcendentals=0),
        name=name,
    )(*args)


def schedule(devices):
    if devices == 4:
        return [[(0, 2), (3, 1), (2, 3), (1, 0)], [(1, 2), (3, 0)]]
    rounds = []
    for k in range(1, devices // 2 + 1):
        whole_way = [(p, (p + k) % devices) for p in range(devices)]
        if 2 * k == devices:
            whole_way = [way for way in whole_way if (way[0] < k) == (way[0] % 2 == 0)]
        rounds.append(whole_way)
    return rounds


def completed(way, devices):
    idle = sorted(set(range(devices)) - {p for p, _ in way})
    open_ends = sorted(set(range(devices)) - {q for _, q in way})
    return way + list(zip(idle, open_ends))


def on_device(
    panels,
    amplitudes,
    fitted_ints,
    pno_energy,
    fock_occ,
    pno_count,
    pair_pos,
    coupling,
    coupling_lmo,
    pair_lmo,
):
    per_dev, width, pao = panels.shape
    pair_devices = lax.axis_size("pair")
    aux_devices = lax.axis_size("aux")
    block = per_dev // aux_devices
    thin = block * width
    couplings = coupling.shape[1]
    total = pair_pos.shape[0]
    ways = schedule(pair_devices)
    rounds = len(ways)
    back_ways = [completed([(q, p) for p, q in way], pair_devices) for way in ways]

    sent = pack(panels, amplitudes, pno_count, block)
    arrived = [lax.ppermute(sent, "pair", way) for way in ways]
    weight_in, weight_out, block_amps, own, masked, acc = local(
        coupling.transpose(1, 2, 0).reshape(2 * couplings, total),
        coupling_lmo.T,
        pair_lmo.T,
        pair_pos[None, :],
        fock_occ,
        amplitudes.reshape(per_dev * width, width),
        pno_energy,
        pno_count,
        fitted_ints,
        panels,
        block,
        ways,
    )

    acc_shape = jax.ShapeDtypeStruct(acc.shape, F32)
    own_shape = jax.ShapeDtypeStruct((16, width // 16 * thin), F32)
    block_shape = jax.ShapeDtypeStruct(own_shape.shape, BF16)
    flops = 1_000_000_000
    returned = []
    for k in range(1, rounds):
        args = (masked, block_amps, acc, arrived[k - 1], weight_in[k], weight_out[k - 1])
        if k == 1:
            args += (sent, weight_in[0])
        acc, back = call(
            functools.partial(both_kernel, block, width),
            "couple",
            (acc_shape, block_shape),
            args,
            2 * flops,
        )
        returned.append(lax.ppermute(back, "pair", back_ways[k - 1]))
    back = call(
        functools.partial(back_kernel, block, width),
        "couple_back",
        block_shape,
        (arrived[-1], masked, block_amps, weight_out[-1]),
        flops,
    )
    last_back = lax.ppermute(back, "pair", back_ways[-1])
    parts = call(
        functools.partial(last_kernel, block, width, len(returned)),
        "couple_last",
        (own_shape,) + (block_shape,) * (aux_devices - 1),
        (arrived[-1], masked, weight_in[rounds], acc, own, *returned),
        flops,
        [pltpu.VMEM(acc.shape, F32)],
    )
    sums = [parts[0]]
    for k in range(1, aux_devices):
        sums.append(lax.ppermute(parts[k], "aux", [(d, d ^ k) for d in range(aux_devices)]))
    sums.append(last_back)
    return call(
        functools.partial(finish_kernel, block, width, len(sums)),
        "finish",
        jax.ShapeDtypeStruct((block, width * width), F32),
        tuple(sums),
        1_000_000,
        [pltpu.VMEM((thin, width), F32)],
    )


def solution(mesh):
    placed = (
        P(("groups", "pair"), None, None),
        P(("groups", "pair"), None),
        P(("groups", "pair"), None, "aux", None),
        P(("groups", "pair"), None),
        P("groups", None),
        P(("groups", "pair")),
        P("groups"),
        P("groups", None, None),
        P("groups", None),
        P("groups", None),
    )
    return jax.shard_map(
        on_device,
        mesh=mesh,
        in_specs=placed,
        out_specs=P(("groups", "pair", "aux"), None),
        check_vma=False,
    )
```

time: 467 us -> 30.6 us (0.07)
  waiting for transfers between devices: 331 us -> 5.25 us
  local copies, waits for them, and re-layouts: 54.3 us -> 0.27 us
  other arithmetic: 29.6 us -> 0 us
  matrix products: 23.2 us -> 0 us
  Pallas kernels: 0 us -> 14.5 us
  between operations: 14.4 us -> 0.22 us
    all_to_all x2 -> x0, waiting for transfers between devices: 331 us -> none  [the longest x1 330 us: on_device(): lax.all_to_all(send_panels, 'pair', split_axis=0, concat_axis=0, tiled=True)]
    gather x13 -> x0, local copies, waits for them, and re-layouts: 40.6 us -> none  [the longest x1 15.6 us: on_device(): jnp.take(recv_panels.reshape(pair_devices * capacity, pno_width, pao_widt...]
    dot_general x6 -> x0, matrix products: 23.2 us -> none  [the longest x1 11.8 us: sandwich(): jnp.einsum(pattern_intersection, left_panels, right_panels, preferred_ele...]
    select_n x12 -> x0, other arithmetic: 21.7 us -> none  [the longest x1 14.5 us: on_device(): jnp.where(filled[:, :, None, None] > 0, send_panels, jnp.zeros_like(send_...]
    pallas_call x0 -> x6, Pallas kernels: none -> 14.5 us  [the longest x4 6.5 us: call(): pl.pallas_call(kernel, out_shape=out_shape, in_specs=[whole()] * len(args...]
    all_to_all x2 -> x0, starting transfers between devices: 13.3 us -> none  [the longest x1 6.95 us: on_device(): lax.all_to_all(send_panels, 'pair', split_axis=0, concat_axis=0, tiled=True)]
    ppermute x0 -> x7, starting transfers between devices: none -> 10.2 us  [the longest x2 5.38 us: on_device(): arrived = [lax.ppermute(sent, 'pair', way) for way in ways]]
    select_n x4 -> x0, local copies, waits for them, and re-layouts: 6.22 us -> none  [the longest x1 5.99 us: on_device(): jnp.take(recv_amps.reshape(pair_devices * capacity, pno_width * pno_width...]
  transfers between devices with their start and end apart: 3 -> 7, of which waited for: 2 -> 4; matrix products, arithmetic and copies ran while one was open for 18% -> 1% of each run, Pallas kernels for 0% -> 38%
where the time goes in v2:
time: 30.6 us; the launch traced here: 30.5 us
  Pallas kernels  14.5 us (47%)
  starting transfers between devices  10.2 us (33%)
  waiting for transfers between devices  5.25 us (17%)
    pallas_call x4, Pallas kernels, call(): pl.pallas_call(kernel, out_shape=out_shape, in_specs=[whole()] * len(args...  6.5 us
    pallas_call x1, Pallas kernels, local(): pl.pallas_call(functools.partial(local_kernel, block, width, ways), out_s...  5.98 us
    ppermute x2, starting transfers between devices, on_device(): arrived = [lax.ppermute(sent, 'pair', way) for way in ways]  5.38 us
    ppermute x1, starting transfers between devices, on_device(): returned.append(lax.ppermute(back, 'pair', back_ways[k - 1]))  2.92 us
    ppermute x3, waiting for transfers between devices, on_device(): lax.ppermute(parts[k], 'aux', [(d, d ^ k) for d in range(aux_devices)])  2.39 us
    ppermute x2, waiting for transfers between devices, on_device(): arrived = [lax.ppermute(sent, 'pair', way) for way in ways]  2.35 us
    pallas_call x1, Pallas kernels, pack(): pl.pallas_call(functools.partial(pack_kernel, block, width, chunks), out_...  1.99 us
    ppermute x3, starting transfers between devices, on_device(): lax.ppermute(parts[k], 'aux', [(d, d ^ k) for d in range(aux_devices)])  1.93 us
  transfers between devices with their start and end apart: 7, of which 4 were waited for; matrix products, arithmetic and copies ran while one was open for 1% of the time, Pallas kernels for 38%

profile of v2, /device:TPU:0, one launch (start us, length us, event | category | flops | bytes accessed | tf_op | source)
XLA Modules:
  0.0 30.5 jit_solution(5059838544864458825)
XLA Ops:
  0.0 0.0 copy-start.7
  0.0 0.0 copy-start.8
  0.1 2.0 %pack.1.refs_6_ = bf16[208,768]{1,0:T(8,128)(2,1)} custom-call(bf16[16,48,768]{2,1,0:T(8,128)(2,1)} %panels.3, bf16[16,2304]{1,0:T(8,128)(2,1)} %amps.1, s32[16]{0:T(128)} %count.3), custom_call_target="tpu_custom_call" | custom-call | tf_op jit(solution)/shard_map/pack/pallas_call | solution.py:108
  2.1 4.1 %collective-permute-start.1 = (bf16[208,768]{1,0:T(8,128)(2,1)}, bf16[208,768]{1,0:T(8,128)(2,1)S(1)}, u32[]{:S(2)}, u32[]{:S(2)}) collective-permute-start(bf16[208,768]{1,0:T(8,128)(2,1)} %pack.1.refs_6_), channel_id=1, source_target_pairs={{0,8},{12,4},{8,12},{4,0},{1,9},{13,5},{9,13},{5,1},{2,10},{14,6},... | collective-permute-start | bytes 958472 | tf_op jit(solution)/shard_map/ppermute | solution.py:447
  6.2 1.3 %collective-permute-start = (bf16[208,768]{1,0:T(8,128)(2,1)}, bf16[208,768]{1,0:T(8,128)(2,1)S(1)}, u32[]{:S(2)}, u32[]{:S(2)}) collective-permute-start(bf16[208,768]{1,0:T(8,128)(2,1)} %pack.1.refs_6_), channel_id=1, source_target_pairs={{4,8},{12,0},{5,9},{13,1},{6,10},{14,2},{7,11},{15,3},{20,24},{28,... | collective-permute-start | bytes 958472 | tf_op jit(solution)/shard_map/ppermute | solution.py:447
  7.5 0.2 reshape.7.amps
  7.7 0.0 copy-done
  7.7 0.0 copy-done.2
  7.7 0.0 copy-done.4
  7.7 0.0 copy-done.5
  7.7 0.0 copy-done.7
  7.7 0.0 copy-done.8
  7.7 0.0 copy-done.6
  7.7 0.0 copy-done.3
  7.8 0.0 copy-start.1
  7.8 6.0 %local.1 = (f32[3,16,192]{2,1,0:T(8,128)S(1)}, f32[2,8,768]{2,1,0:T(8,128)S(1)}, bf16[768,768]{1,0:T(8,128)(2,1)S(1)}, f32[48,192]{1,0:T(8,128)S(1)}, bf16[768,7...) custom-call(s32[56,64]{1,0:T(8,128)S(1)} %bitcast.16, s32[28,64]{1,0:T(8,128)S(1)} %bitcast.17, s32[2,64]{1,0:T(2,128)S(1)} %bitcast.18, ...), custom_call_target="tpu_custom_call" | custom-call | flops 6000000000 | bytes 6291456 | tf_op jit(solution)/shard_map/local/pallas_call | solution.py:262
  13.8 0.0 collective-permute-done.1.refs_3_
  13.8 3.0 %couple.1 = (f32[4,48,192]{2,1,0:T(8,128)S(1)}, bf16[16,576]{1,0:T(8,128)(2,1)S(1)}) custom-call(bf16[768,768]{1,0:T(8,128)(2,1)S(1)} %get-tuple-element.17.refs_0_.masked, bf16[768,768]{1,0:T(8,128)(2,1)S(1)} %get-tuple-element.19.refs_1_.block_amps, f32[4,48,192]{2,1,0:T(8,128)S(1)} %get-tuple-element.20.refs_2_, ...), custom_call_target="tpu_custom_call" | custom-call | flops 2000000000 | bytes 3000000 | tf_op jit(solution)/shard_map/couple/pallas_call | solution.py:393
  16.8 2.9 %collective-permute-start.2 = (bf16[16,576]{1,0:T(8,128)(2,1)S(1)}, bf16[16,576]{1,0:T(8,128)(2,1)S(1)}, u32[]{:S(2)}, u32[]{:S(2)}) collective-permute-start(bf16[16,576]{1,0:T(8,128)(2,1)S(1)} %get-tuple-element.24), channel_id=1, source_target_pairs={{8,0},{4,12},{12,8},{0,4},{9,1},{5,13},{13,9},{1,5},{10,2},{6,14},... | collective-permute-start | bytes 55304 | tf_op jit(solution)/shard_map/ppermute | solution.py:479
  19.7 2.4 %collective-permute-done.sent = bf16[208,768]{1,0:T(8,128)(2,1)S(1)} collective-permute-done((bf16[208,768]{1,0:T(8,128)(2,1)}, bf16[208,768]{1,0:T(8,128)(2,1)S(1)}, u32[]{:S(2)}, u32[]{:S(2)}) %collective-permute-start) | collective-permute-done | bytes 319520 | tf_op jit(solution)/shard_map/ppermute | solution.py:447
  22.0 1.4 %couple_back.1 = bf16[16,576]{1,0:T(8,128)(2,1)S(1)} custom-call(bf16[208,768]{1,0:T(8,128)(2,1)S(1)} %collective-permute-done.sent, bf16[768,768]{1,0:T(8,128)(2,1)S(1)} %get-tuple-element.17.refs_0_.masked, bf16[768,768]{1,0:T(8,128)(2,1)S(1)} %get-tuple-element.19.refs_1_.block_amps, f32[8,768]{1,0:T(8,128)S(1)} %get-tuple-element.29.weight_out), custom_call_target="tpu_custom_call" | custom-call | flops 1000000000 | bytes 3000000 | tf_op jit(solution)/shard_map/couple_back/pallas_call | solution.py:393
  23.4 0.0 collective-permute-start.6
  23.5 0.0 collective-permute-done.2.refs_0_
  23.5 1.3 %couple_last.1 = (f32[16,576]{1,0:T(8,128)S(1)}, bf16[16,576]{1,0:T(8,128)(2,1)S(1)}, bf16[16,576]{1,0:T(8,128)(2,1)S(1)}, bf16[16,576]{1,0:T(8,128)(2,1)S(1)}) custom-call(bf16[208,768]{1,0:T(8,128)(2,1)S(1)} %collective-permute-done.sent, bf16[768,768]{1,0:T(8,128)(2,1)S(1)} %get-tuple-element.17.refs_0_.masked, ...), custom_call_target="tpu_custom_call" | custom-call | flops 1000000000 | bytes 3000000 | tf_op jit(solution)/shard_map/couple_last/pallas_call | solution.py:393
  24.8 0.1 collective-permute-start.3
  24.9 1.6 %collective-permute-start.4 = (bf16[16,576]{1,0:T(8,128)(2,1)S(1)}, bf16[16,576]{1,0:T(8,128)(2,1)S(1)}, u32[]{:S(2)}, u32[]{:S(2)}) collective-permute-start(bf16[16,576]{1,0:T(8,128)(2,1)S(1)} %get-tuple-element.27), channel_id=1, source_target_pairs={{0,2},{1,3},{2,0},{3,1},{4,6},{5,7},{6,4},{7,5},{8,10},{9,11},{10,... | collective-permute-start | bytes 55304 | tf_op jit(solution)/shard_map/ppermute | solution.py:498
  26.4 0.3 %collective-permute-start.5 = (bf16[16,576]{1,0:T(8,128)(2,1)S(1)}, bf16[16,576]{1,0:T(8,128)(2,1)S(1)}, u32[]{:S(2)}, u32[]{:S(2)}) collective-permute-start(bf16[16,576]{1,0:T(8,128)(2,1)S(1)} %get-tuple-element.28), channel_id=1, source_target_pairs={{0,3},{1,2},{2,1},{3,0},{4,7},{5,6},{6,5},{7,4},{8,11},{9,10},{10,... | collective-permute-start | bytes 55304 | tf_op jit(solution)/shard_map/ppermute | solution.py:498
  26.7 0.5 %collective-permute-done.6.refs_4_ = bf16[16,576]{1,0:T(8,128)(2,1)S(1)} collective-permute-done((bf16[16,576]{1,0:T(8,128)(2,1)S(1)}, bf16[16,576]{1,0:T(8,128)(2,1)S(1)}, u32[]{:S(2)}, u32[]{:S(2)}) %collective-permute-start.6) | collective-permute-done | bytes 18464 | tf_op jit(solution)/shard_map/ppermute | solution.py:487
  27.2 0.0 collective-permute-done.3.refs_1_
  27.2 1.5 %collective-permute-done.4.refs_2_ = bf16[16,576]{1,0:T(8,128)(2,1)S(1)} collective-permute-done((bf16[16,576]{1,0:T(8,128)(2,1)S(1)}, bf16[16,576]{1,0:T(8,128)(2,1)S(1)}, u32[]{:S(2)}, u32[]{:S(2)}) %collective-permute-start.4) | collective-permute-done | bytes 18464 | tf_op jit(solution)/shard_map/ppermute | solution.py:498
  28.7 0.9 %collective-permute-done.5.refs_3_ = bf16[16,576]{1,0:T(8,128)(2,1)S(1)} collective-permute-done((bf16[16,576]{1,0:T(8,128)(2,1)S(1)}, bf16[16,576]{1,0:T(8,128)(2,1)S(1)}, u32[]{:S(2)}, u32[]{:S(2)}) %collective-permute-start.5) | collective-permute-done | bytes 18464 | tf_op jit(solution)/shard_map/ppermute | solution.py:498
  29.6 0.8 %finish.1 = f32[4,2304]{1,0:T(4,128)} custom-call(f32[16,576]{1,0:T(8,128)S(1)} %get-tuple-element.25.refs_0_, bf16[16,576]{1,0:T(8,128)(2,1)S(1)} %collective-permute-done.3.refs_1_, bf16[16,576]{1,0:T(8,128)(2,1)S(1)} %collective-permute-done.4.refs_2_, bf16[16,576]{1,0:T(8,128)(2,1)S(1)} %collective-permute-done.5.refs_3_, ...), custom_call_target="tpu_custom_call" | custom-call | flops 1000000 | bytes 3000000 | tf_op jit(solution)/shard_map/finish/pallas_call | solution.py:393
  (11 shorter events, 0.0 us)
Async XLA Ops:
  0.0 7.4 %copy-start.9 = (bf16[16,2304]{1,0:T(8,128)(2,1)S(1)}, bf16[16,2304]{1,0:T(8,128)(2,1)}, u32[]{:S(2)}) copy-start(bf16[16,2304]{1,0:T(8,128)(2,1)} %amps.1) | copy-start | bytes 221188
  0.0 7.7 %copy-start = (bf16[16,48,768]{2,1,0:T(8,128)(2,1)S(1)}, bf16[16,48,768]{2,1,0:T(8,128)(2,1)}, u32[]{:S(2)}) copy-start(bf16[16,48,768]{2,1,0:T(8,128)(2,1)} %panels.3) | copy-start | bytes 3538948
  0.0 7.7 %copy-start.2 = (s32[16]{0:T(128)S(1)}, s32[16]{0:T(128)}, u32[]{:S(2)}) copy-start(s32[16]{0:T(128)} %count.3) | copy-start | bytes 196
  0.0 7.7 %copy-start.4 = (s32[64,28,2]{0,2,1:T(2,128)S(1)}, s32[64,28,2]{0,2,1:T(2,128)}, u32[]{:S(2)}) copy-start(s32[64,28,2]{0,2,1:T(2,128)} %param.17) | copy-start | bytes 43012
  0.0 7.7 %copy-start.5 = (s32[64,28]{0,1:T(8,128)S(1)}, s32[64,28]{0,1:T(8,128)}, u32[]{:S(2)}) copy-start(s32[64,28]{0,1:T(8,128)} %param.18) | copy-start | bytes 21508
  0.0 7.7 %copy-start.7 = (s32[64,2]{0,1:T(2,128)S(1)}, s32[64,2]{0,1:T(2,128)}, u32[]{:S(2)}) copy-start(s32[64,2]{0,1:T(2,128)} %param.19) | copy-start | bytes 1540
  0.0 7.7 %copy-start.8 = (s32[64]{0:T(128)S(1)}, s32[64]{0:T(128)}, u32[]{:S(2)}) copy-start(s32[64]{0:T(128)} %param.16) | copy-start | bytes 772
  0.0 7.7 %copy-start.6 = (f32[16,48]{1,0:T(8,128)S(1)}, f32[16,48]{1,0:T(8,128)}, u32[]{:S(2)}) copy-start(f32[16,48]{1,0:T(8,128)} %energy.1) | copy-start | bytes 9220
  0.0 7.7 %copy-start.3 = (f32[64,64]{1,0:T(8,128)S(1)}, f32[64,64]{1,0:T(8,128)}, u32[]{:S(2)}) copy-start(f32[64,64]{1,0:T(8,128)} %fock.1) | copy-start | bytes 49156
  2.1 11.7 %collective-permute-start.1 = (bf16[208,768]{1,0:T(8,128)(2,1)}, bf16[208,768]{1,0:T(8,128)(2,1)S(1)}, u32[]{:S(2)}, u32[]{:S(2)}) collective-permute-start(bf16[208,768]{1,0:T(8,128)(2,1)} %pack.1.refs_6_), channel_id=1, source_target_pairs={{0,8},{12,4},{8,12},{4,0},{1,9},{13,5},{9,13},{5,1},{2,10},{14,6},... | collective-permute-start | bytes 958472 | tf_op jit(solution)/shard_map/ppermute | solution.py:447
  6.2 15.9 %collective-permute-start = (bf16[208,768]{1,0:T(8,128)(2,1)}, bf16[208,768]{1,0:T(8,128)(2,1)S(1)}, u32[]{:S(2)}, u32[]{:S(2)}) collective-permute-start(bf16[208,768]{1,0:T(8,128)(2,1)} %pack.1.refs_6_), channel_id=1, source_target_pairs={{4,8},{12,0},{5,9},{13,1},{6,10},{14,2},{7,11},{15,3},{20,24},{28,... | collective-permute-start | bytes 958472 | tf_op jit(solution)/shard_map/ppermute | solution.py:447
  7.8 6.0 %copy-start.1 = (bf16[208,768]{1,0:T(8,128)(2,1)S(1)}, bf16[208,768]{1,0:T(8,128)(2,1)}, u32[]{:S(2)}) copy-start(bf16[208,768]{1,0:T(8,128)(2,1)} %pack.1.refs_6_) | copy-start | bytes 958468
  16.8 6.7 %collective-permute-start.2 = (bf16[16,576]{1,0:T(8,128)(2,1)S(1)}, bf16[16,576]{1,0:T(8,128)(2,1)S(1)}, u32[]{:S(2)}, u32[]{:S(2)}) collective-permute-start(bf16[16,576]{1,0:T(8,128)(2,1)S(1)} %get-tuple-element.24), channel_id=1, source_target_pairs={{8,0},{4,12},{12,8},{0,4},{9,1},{5,13},{13,9},{1,5},{10,2},{6,14},... | collective-permute-start | bytes 55304 | tf_op jit(solution)/shard_map/ppermute | solution.py:479
  23.4 3.8 %collective-permute-start.6 = (bf16[16,576]{1,0:T(8,128)(2,1)S(1)}, bf16[16,576]{1,0:T(8,128)(2,1)S(1)}, u32[]{:S(2)}, u32[]{:S(2)}) collective-permute-start(bf16[16,576]{1,0:T(8,128)(2,1)S(1)} %couple_back.1), channel_id=1, source_target_pairs={{8,4},{0,12},{4,0},{12,8},{9,5},{1,13},{5,1},{13,9},{10,6},{2,14},... | collective-permute-start | bytes 55304 | tf_op jit(solution)/shard_map/ppermute | solution.py:487
  24.8 2.5 %collective-permute-start.3 = (bf16[16,576]{1,0:T(8,128)(2,1)S(1)}, bf16[16,576]{1,0:T(8,128)(2,1)S(1)}, u32[]{:S(2)}, u32[]{:S(2)}) collective-permute-start(bf16[16,576]{1,0:T(8,128)(2,1)S(1)} %get-tuple-element.26), channel_id=1, source_target_pairs={{0,1},{1,0},{2,3},{3,2},{4,5},{5,4},{6,7},{7,6},{8,9},{9,8},{10,11... | collective-permute-start | bytes 55304 | tf_op jit(solution)/shard_map/ppermute | solution.py:498
  24.9 3.8 %collective-permute-start.4 = (bf16[16,576]{1,0:T(8,128)(2,1)S(1)}, bf16[16,576]{1,0:T(8,128)(2,1)S(1)}, u32[]{:S(2)}, u32[]{:S(2)}) collective-permute-start(bf16[16,576]{1,0:T(8,128)(2,1)S(1)} %get-tuple-element.27), channel_id=1, source_target_pairs={{0,2},{1,3},{2,0},{3,1},{4,6},{5,7},{6,4},{7,5},{8,10},{9,11},{10,... | collective-permute-start | bytes 55304 | tf_op jit(solution)/shard_map/ppermute | solution.py:498
  26.4 3.2 %collective-permute-start.5 = (bf16[16,576]{1,0:T(8,128)(2,1)S(1)}, bf16[16,576]{1,0:T(8,128)(2,1)S(1)}, u32[]{:S(2)}, u32[]{:S(2)}) collective-permute-start(bf16[16,576]{1,0:T(8,128)(2,1)S(1)} %get-tuple-element.28), channel_id=1, source_target_pairs={{0,3},{1,2},{2,1},{3,0},{4,7},{5,6},{6,5},{7,4},{8,11},{9,10},{10,... | collective-permute-start | bytes 55304 | tf_op jit(solution)/shard_map/ppermute | solution.py:498

commit v3 on v2

--- a/solution.py
+++ b/solution.py
@@ -75,30 +75,46 @@
     return high, (values - high.astype(F32)).astype(BF16)
 
 
-def pack_kernel(block, width, chunks, panels, amps, count, out, held, amps_held, count_held, sems):
+def pack_kernel(block, width, chunks, panels, amps, count, out, held, amps_held, count_held, made, sems):
     first = lax.axis_index("aux") * block
-    copies = [
-        pltpu.make_async_copy(panels.at[pl.ds(first, block)], held, sems.at[0]),
-        pltpu.make_async_copy(amps, amps_held, sems.at[1]),
-        pltpu.make_async_copy(count, count_held, sems.at[2]),
+    coming = [
+        pltpu.make_async_copy(amps, amps_held, sems.at[0]),
+        pltpu.make_async_copy(count, count_held, sems.at[1]),
     ]
-    for copy in copies:
+    for j in range(block):
+        coming.append(pltpu.make_async_copy(panels.at[first + j], held.at[j], sems.at[2 + j]))
+    for copy in coming:
         copy.start()
     pao = held.shape[2]
     pairs = amps_held.shape[0]
     tail = tail_rows(block, chunks)
     row = iota((tail, pairs), 0)
     source = iota((tail, pairs), 1)
-    for copy in copies:
-        copy.wait()
-    rows = jnp.zeros((tail, pao), F32)
+    hots = []
     for chunk in range(chunks):
         inside = (row >= chunk * block) & (row < (chunk + 1) * block)
-        hot = (inside & (source == first + row - chunk * block)).astype(F32).astype(BF16)
+        hots.append((inside & (source == first + row - chunk * block)).astype(F32).astype(BF16))
+    going = []
+
+    def send(start, rows):
+        part = pl.ds(start, rows)
+        sem = sems.at[2 + block + len(going)]
+        going.append(pltpu.make_async_copy(made.at[part], out.at[part], sem))
+        going[-1].start()
+
+    coming[0].wait()
+    rows = jnp.zeros((tail, pao), F32)
+    for chunk, hot in enumerate(hots):
         rows += dot_nn(hot, amps_held[:, chunk * pao : (chunk + 1) * pao])
-    out[block * width :, :] = rows.astype(BF16)
+    made[block * width :, :] = rows.astype(BF16)
+    send(block * width, tail)
+    coming[1].wait()
     for j in range(block):
-        out[j * width : (j + 1) * width, :] = masked_rows(held[j], count_held[first + j])
+        coming[2 + j].wait()
+        made[j * width : (j + 1) * width, :] = masked_rows(held[j], count_held[first + j])
+        send(j * width, width)
+    for copy in going:
+        copy.wait()
 
 
 def pack(panels, amps, count, block):
@@ -109,12 +125,13 @@
         functools.partial(pack_kernel, block, width, chunks),
         out_shape=jax.ShapeDtypeStruct((rows, pao), BF16),
         in_specs=[whole(pltpu.HBM)] * 3,
-        out_specs=whole(),
+        out_specs=whole(pltpu.HBM),
         scratch_shapes=[
             pltpu.VMEM((block, width, pao), BF16),
             pltpu.VMEM(amps.shape, BF16),
             pltpu.SMEM(count.shape, I32),
-            pltpu.SemaphoreType.DMA((3,)),
+            pltpu.VMEM((rows, pao), BF16),
+            pltpu.SemaphoreType.DMA((3 + 2 * block,)),
         ],
         compiler_params=pltpu.CompilerParams(vmem_limit_bytes=PACK_VMEM_BYTES),
         name="pack",
@@ -206,7 +223,10 @@
                 start = jnp.where(pair == receiver, sender, start)
         source = start * per_dev + first
         spread = (iota((total, thin), 0) == source + thin_pair).astype(F32)
-        weight_in[k] = dot_nn(mine, spread, HIGHEST)
+        spread = dot_nn(mine, spread, HIGHEST)
+        for group in range(groups):
+            part = slice(group * block, (group + 1) * block)
+            weight_in[k, group, :block, :] = spread[part, :]
         if k > 0:
             weight_out[k - 1] = dot_nn(of_pairs(8, source), local, HIGHEST)
 
@@ -262,7 +282,7 @@
     return pl.pallas_call(
         functools.partial(local_kernel, block, width, ways),
         out_shape=(
-            jax.ShapeDtypeStruct((rounds + 1, per_dev, thin), F32),
+            jax.ShapeDtypeStruct((rounds + 1, groups, 8, thin), F32),
             jax.ShapeDtypeStruct((rounds, 8, wide), F32),
             jax.ShapeDtypeStruct((wide, wide), BF16),
             jax.ShapeDtypeStruct((width, thin), F32),
@@ -306,6 +326,13 @@
     return jnp.where(row_pair == across_pair, dot_nn(picked, fold), 0.0).astype(BF16)
 
 
+def scaled(half, weight, width):
+    rows = half.shape[0] // width
+    return jnp.concatenate(
+        [half[t * width : (t + 1) * width, :] * weight[t : t + 1, :] for t in range(rows)], 0
+    )
+
+
 def add_in(block, width, masked, parts, put):
     thin = block * width
     inters, halves = [], []
@@ -315,30 +342,29 @@
         inters.append(inter)
         halves.append(half)
     for group in range(masked.shape[0] // thin):
+        rows = slice(group * thin, (group + 1) * thin)
         square = jnp.zeros((thin, thin), F32)
         for (_, weight_in), inter, half in zip(parts, inters, halves):
-            scaled = []
-            for t in range(group * block, (group + 1) * block):
-                scaled.append(half[t * width : (t + 1) * width, :] * weight_in[t : t + 1, :])
-            high, low = split_high_low(jnp.concatenate(scaled, 0))
-            mine = inter[group * thin : (group + 1) * thin, :]
-            square += dot_nt(high, mine) + dot_nt(low, mine)
+            high, low = split_high_low(scaled(half[rows, :], weight_in[group], width))
+            square += dot_nt(high, inter[rows, :]) + dot_nt(low, inter[rows, :])
         put(group, fold_diagonal(square, width))
+
+
+def add_in_group(block, width, masked, sent, amps, weight_in, group):
+    thin = block * width
+    rows = pl.ds(pl.multiple_of(group * thin, thin), thin)
+    inter = dot_nt(masked[rows, :], sent[:thin, :]).astype(BF16)
+    half = dot_nn(inter, amps).astype(BF16).astype(F32)
+    high, low = split_high_low(scaled(half, weight_in[group], width))
+    return fold_diagonal(dot_nt(high, inter) + dot_nt(low, inter), width)
 
 
 def add_back(block, width, sent, masked, block_amps, weight_out):
     thin = block * width
     inter = dot_nt(sent[:thin, :], masked[...]).astype(BF16)
     half = dot_nn(inter, block_amps[...]).astype(BF16).astype(F32)
-    parts = []
-    for s in range(block):
-        parts.append(half[s * width : (s + 1) * width, :] * weight_out[s : s + 1, :])
-    high, low = split_high_low(jnp.concatenate(parts, 0))
+    high, low = split_high_low(scaled(half, weight_out, width))
     return fold_diagonal(dot_nt(high, inter) + dot_nt(low, inter), width)
-
-
-def back_kernel(block, width, sent, masked, block_amps, weight_out, out):
-    out[...] = as_sent(add_back(block, width, sent, masked, block_amps, weight_out)).astype(BF16)
 
 
 def both_kernel(block, width, *refs):
@@ -353,28 +379,41 @@
     add_in(block, width, masked, parts, put)
 
 
-def last_kernel(block, width, returned, sent, masked, weight_in, acc, own, *refs):
-    backs, outs, held = refs[:returned], refs[returned:-1], refs[-1]
-
-    def put(group, value):
-        held[group] = acc[group] - value
-
-    add_in(block, width, masked, [(sent, weight_in)], put)
+NEAR = 2
+
+
+def far_kernel(block, width, sent, masked, block_amps, weight_out, weight_in, acc, back, *outs):
+    amps = unpack_amps(sent, block, width)
     aux = lax.axis_index("aux")
-    mine = as_sent(held[aux] + own[...])
-    for back in backs:
-        mine -= back[...].astype(F32)
-    outs[0][...] = mine
-    for k in range(1, len(outs)):
-        outs[k][...] = as_sent(held[lax.bitwise_xor(aux, k)]).astype(BF16)
+    back[...] = as_sent(add_back(block, width, sent, masked, block_amps, weight_out)).astype(BF16)
+    for k, out in enumerate(outs, NEAR):
+        group = lax.bitwise_xor(aux, k)
+        added = add_in_group(block, width, masked, sent, amps, weight_in, group)
+        out[...] = as_sent(acc[group] - added).astype(BF16)
+
+
+def near_kernel(block, width, returned, sent, masked, weight_in, acc, own, *refs):
+    backs, outs = refs[:returned], refs[returned:]
+    amps = unpack_amps(sent, block, width)
+    aux = lax.axis_index("aux")
+    for k, out in enumerate(outs):
+        group = lax.bitwise_xor(aux, k)
+        added = add_in_group(block, width, masked, sent, amps, weight_in, group)
+        if k > 0:
+            out[...] = as_sent(acc[group] - added).astype(BF16)
+        else:
+            mine = as_sent(acc[group] - added + own[...])
+            for back in backs:
+                mine -= back[...].astype(F32)
+            out[...] = mine
 
 
 def finish_kernel(block, width, count, *refs):
     parts, out, held = refs[:count], refs[count], refs[count + 1]
     total = parts[0][...]
-    for part in parts[1:-1]:
-        total += part[...].astype(F32)
-    total -= parts[-1][...].astype(F32)
+    for n, part in enumerate(parts[1:]):
+        value = part[...].astype(F32)
+        total = total - value if n == 0 else total + value
     for s in range(block):
         for r in range(0, width, 16):
             lane = r // 16 * block * width + s * width
@@ -477,26 +516,28 @@
             2 * flops,
         )
         returned.append(lax.ppermute(back, "pair", back_ways[k - 1]))
-    back = call(
-        functools.partial(back_kernel, block, width),
-        "couple_back",
-        block_shape,
-        (arrived[-1], masked, block_amps, weight_out[-1]),
+    back, *far = call(
+        functools.partial(far_kernel, block, width),
+        "couple_far",
+        (block_shape,) * (1 + aux_devices - NEAR),
+        (arrived[-1], masked, block_amps, weight_out[-1], weight_in[rounds], acc),
         flops,
     )
     last_back = lax.ppermute(back, "pair", back_ways[-1])
-    parts = call(
-        functools.partial(last_kernel, block, width, len(returned)),
-        "couple_last",
-        (own_shape,) + (block_shape,) * (aux_devices - 1),
+    near = call(
+        functools.partial(near_kernel, block, width, len(returned)),
+        "couple_near",
+        (own_shape,) + (block_shape,) * (NEAR - 1),
         (arrived[-1], masked, weight_in[rounds], acc, own, *returned),
         flops,
-        [pltpu.VMEM(acc.shape, F32)],
-    )
-    sums = [parts[0]]
+    )
+    parts = list(near) + far
+    sums = {0: last_back}
     for k in range(1, aux_devices):
-        sums.append(lax.ppermute(parts[k], "aux", [(d, d ^ k) for d in range(aux_devices)]))
-    sums.append(last_back)
+        sums[k] = lax.ppermute(parts[k], "aux", [(d, d ^ k) for d in range(aux_devices)])
+    order = [0, 2, 3]
+    order += [k for k in range(1, aux_devices) if k not in order]
+    sums = [parts[0]] + [sums[k] for k in order]
     return call(
         functools.partial(finish_kernel, block, width, len(sums)),
         "finish",

time: 30.6 us -> 29.6 us (0.967)
  waiting for transfers between devices: 5.25 us -> 3.74 us
    ppermute x3, waiting for transfers between devices: 2.39 us -> 0.99 us  [on_device(): lax.ppermute(parts[k], 'aux', [(d, d ^ k) for d in range(aux_devices)])]
  transfers between devices with their start and end apart: 7 -> 7, of which waited for: 4 -> 4; matrix products, arithmetic and copies ran while one was open for 1% -> 1% of each run, Pallas kernels for 38% -> 40%
where the time goes in v3:
time: 29.6 us; the launch traced here: 29.4 us
  Pallas kernels  14.7 us (50%)
  starting transfers between devices  10.5 us (35%)
  waiting for transfers between devices  3.74 us (13%)
    pallas_call x4, Pallas kernels, call(): pl.pallas_call(kernel, out_shape=out_shape, in_specs=[whole()] * len(args...  6.75 us
    pallas_call x1, Pallas kernels, local(): pl.pallas_call(functools.partial(local_kernel, block, width, ways), out_s...  5.98 us
    ppermute x2, starting transfers between devices, on_device(): arrived = [lax.ppermute(sent, 'pair', way) for way in ways]  5.38 us
    ppermute x1, starting transfers between devices, on_device(): returned.append(lax.ppermute(back, 'pair', back_ways[k - 1]))  2.92 us
    ppermute x2, waiting for transfers between devices, on_device(): arrived = [lax.ppermute(sent, 'pair', way) for way in ways]  2.35 us
    ppermute x3, starting transfers between devices, on_device(): lax.ppermute(parts[k], 'aux', [(d, d ^ k) for d in range(aux_devices)])  2.23 us
    pallas_call x1, Pallas kernels, pack(): pl.pallas_call(functools.partial(pack_kernel, block, width, chunks), out_...  1.97 us
    ppermute x3, waiting for transfers between devices, on_device(): lax.ppermute(parts[k], 'aux', [(d, d ^ k) for d in range(aux_devices)])  0.99 us
  transfers between devices with their start and end apart: 7, of which 4 were waited for; matrix products, arithmetic and copies ran while one was open for 1% of the time, Pallas kernels for 40%

profile of v3, /device:TPU:0, one launch (start us, length us, event | category | flops | bytes accessed | tf_op | source)
XLA Modules:
  0.0 29.4 jit_solution(11103658662686762090)
XLA Ops:
  0.0 0.0 copy-start.7
  0.0 0.0 copy-start.8
  0.0 0.0 copy-start.6
  0.0 0.0 copy-start.3
  0.1 2.0 %pack.1.refs_6_ = bf16[208,768]{1,0:T(8,128)(2,1)} custom-call(bf16[16,48,768]{2,1,0:T(8,128)(2,1)} %panels.3, bf16[16,2304]{1,0:T(8,128)(2,1)} %amps.1, s32[16]{0:T(128)} %count.3), custom_call_target="tpu_custom_call" | custom-call | tf_op jit(solution)/shard_map/pack/pallas_call | solution.py:124
  2.0 4.1 %collective-permute-start.1 = (bf16[208,768]{1,0:T(8,128)(2,1)}, bf16[208,768]{1,0:T(8,128)(2,1)S(1)}, u32[]{:S(2)}, u32[]{:S(2)}) collective-permute-start(bf16[208,768]{1,0:T(8,128)(2,1)} %pack.1.refs_6_), channel_id=1, source_target_pairs={{0,8},{12,4},{8,12},{4,0},{1,9},{13,5},{9,13},{5,1},{2,10},{14,6},... | collective-permute-start | bytes 958472 | tf_op jit(solution)/shard_map/ppermute | solution.py:486
  6.1 1.3 %collective-permute-start = (bf16[208,768]{1,0:T(8,128)(2,1)}, bf16[208,768]{1,0:T(8,128)(2,1)S(1)}, u32[]{:S(2)}, u32[]{:S(2)}) collective-permute-start(bf16[208,768]{1,0:T(8,128)(2,1)} %pack.1.refs_6_), channel_id=1, source_target_pairs={{4,8},{12,0},{5,9},{13,1},{6,10},{14,2},{7,11},{15,3},{20,24},{28,... | collective-permute-start | bytes 958472 | tf_op jit(solution)/shard_map/ppermute | solution.py:486
  7.4 0.0 copy-done.9
  7.4 0.2 reshape.7.amps
  7.7 0.0 copy-done
  7.7 0.0 copy-done.2
  7.7 0.0 copy-done.4
  7.7 0.0 copy-done.5
  7.7 0.0 copy-done.7
  7.7 0.0 copy-done.8
  7.7 6.0 %local.1 = (f32[3,4,8,192]{3,2,1,0:T(8,128)S(1)}, f32[2,8,768]{2,1,0:T(8,128)S(1)}, bf16[768,768]{1,0:T(8,128)(2,1)S(1)}, f32[48,192]{1,0:T(8,128)S(1)}, bf16[76...) custom-call(s32[56,64]{1,0:T(8,128)S(1)} %bitcast.16, s32[28,64]{1,0:T(8,128)S(1)} %bitcast.17, s32[2,64]{1,0:T(2,128)S(1)} %bitcast.18, ...), custom_call_target="tpu_custom_call" | custom-call | flops 6000000000 | bytes 6291456 | tf_op jit(solution)/shard_map/local/pallas_call | solution.py:282
  13.8 0.0 collective-permute-done.1.refs_3_
  13.8 3.0 %couple.1 = (f32[4,48,192]{2,1,0:T(8,128)S(1)}, bf16[16,576]{1,0:T(8,128)(2,1)S(1)}) custom-call(bf16[768,768]{1,0:T(8,128)(2,1)S(1)} %get-tuple-element.18.refs_0_.masked, bf16[768,768]{1,0:T(8,128)(2,1)S(1)} %get-tuple-element.20.refs_1_.block_amps, f32[4,48,192]{2,1,0:T(8,128)S(1)} %get-tuple-element.21.refs_2_, ...), custom_call_target="tpu_custom_call" | custom-call | flops 2000000000 | bytes 3000000 | tf_op jit(solution)/shard_map/couple/pallas_call | solution.py:432
  16.8 2.9 %collective-permute-start.2 = (bf16[16,576]{1,0:T(8,128)(2,1)S(1)}, bf16[16,576]{1,0:T(8,128)(2,1)S(1)}, u32[]{:S(2)}, u32[]{:S(2)}) collective-permute-start(bf16[16,576]{1,0:T(8,128)(2,1)S(1)} %get-tuple-element.25), channel_id=1, source_target_pairs={{8,0},{4,12},{12,8},{0,4},{9,1},{5,13},{13,9},{1,5},{10,2},{6,14},... | collective-permute-start | bytes 55304 | tf_op jit(solution)/shard_map/ppermute | solution.py:518
  19.7 2.3 %collective-permute-done.sent = bf16[208,768]{1,0:T(8,128)(2,1)S(1)} collective-permute-done((bf16[208,768]{1,0:T(8,128)(2,1)}, bf16[208,768]{1,0:T(8,128)(2,1)S(1)}, u32[]{:S(2)}, u32[]{:S(2)}) %collective-permute-start) | collective-permute-done | bytes 319520 | tf_op jit(solution)/shard_map/ppermute | solution.py:486
  22.0 1.8 %couple_far.1 = (bf16[16,576]{1,0:T(8,128)(2,1)S(1)}, bf16[16,576]{1,0:T(8,128)(2,1)S(1)}, bf16[16,576]{1,0:T(8,128)(2,1)S(1)}) custom-call(bf16[208,768]{1,0:T(8,128)(2,1)S(1)} %collective-permute-done.sent, bf16[768,768]{1,0:T(8,128)(2,1)S(1)} %get-tuple-element.18.refs_0_.masked, bf16[768,768]{1,0:T(8,128)(2,1)S(1)} %get-tuple-element.20.refs_1_.block_amps, ...), custom_call_target="tpu_custom_call" | custom-call | flops 1000000000 | bytes 3000000 | tf_op jit(solution)/shard_map/couple_far/pallas_call | solution.py:432
  23.8 0.0 collective-permute-start.3
  23.8 1.6 %collective-permute-start.4 = (bf16[16,576]{1,0:T(8,128)(2,1)S(1)}, bf16[16,576]{1,0:T(8,128)(2,1)S(1)}, u32[]{:S(2)}, u32[]{:S(2)}) collective-permute-start(bf16[16,576]{1,0:T(8,128)(2,1)S(1)} %get-tuple-element.28), channel_id=1, source_target_pairs={{0,2},{1,3},{2,0},{3,1},{4,6},{5,7},{6,4},{7,5},{8,10},{9,11},{10,... | collective-permute-start | bytes 55304 | tf_op jit(solution)/shard_map/ppermute | solution.py:537
  25.4 0.0 collective-permute-start.5
  25.4 0.0 collective-permute-done.2.refs_0_
  25.4 1.1 %couple_near.1 = (f32[16,576]{1,0:T(8,128)S(1)}, bf16[16,576]{1,0:T(8,128)(2,1)S(1)}) custom-call(bf16[208,768]{1,0:T(8,128)(2,1)S(1)} %collective-permute-done.sent, bf16[768,768]{1,0:T(8,128)(2,1)S(1)} %get-tuple-element.18.refs_0_.masked, f32[4,8,192]{2,1,0:T(8,128)S(1)} %get-tuple-element.33.weight_in, f32[4,48,192]{2,1,0:T(8,128)S(1)} %get-tuple-element.23.acc, ...), custom_call_target="tpu_custom_call" | custom-call | flops 1000000000 | bytes 3000000 | tf_op jit(solution)/shard_map/couple_near/pallas_call | solution.py:432
  26.5 0.7 %collective-permute-start.6 = (bf16[16,576]{1,0:T(8,128)(2,1)S(1)}, bf16[16,576]{1,0:T(8,128)(2,1)S(1)}, u32[]{:S(2)}, u32[]{:S(2)}) collective-permute-start(bf16[16,576]{1,0:T(8,128)(2,1)S(1)} %get-tuple-element.30), channel_id=1, source_target_pairs={{0,1},{1,0},{2,3},{3,2},{4,5},{5,4},{6,7},{7,6},{8,9},{9,8},{10,11... | collective-permute-start | bytes 55304 | tf_op jit(solution)/shard_map/ppermute | solution.py:537
  27.2 0.4 %collective-permute-done.3.refs_1_ = bf16[16,576]{1,0:T(8,128)(2,1)S(1)} collective-permute-done((bf16[16,576]{1,0:T(8,128)(2,1)S(1)}, bf16[16,576]{1,0:T(8,128)(2,1)S(1)}, u32[]{:S(2)}, u32[]{:S(2)}) %collective-permute-start.3) | collective-permute-done | bytes 18464 | tf_op jit(solution)/shard_map/ppermute | solution.py:526
  27.6 0.1 collective-permute-done.4.refs_2_
  27.7 0.9 %collective-permute-done.5.refs_3_ = bf16[16,576]{1,0:T(8,128)(2,1)S(1)} collective-permute-done((bf16[16,576]{1,0:T(8,128)(2,1)S(1)}, bf16[16,576]{1,0:T(8,128)(2,1)S(1)}, u32[]{:S(2)}, u32[]{:S(2)}) %collective-permute-start.5) | collective-permute-done | bytes 18464 | tf_op jit(solution)/shard_map/ppermute | solution.py:537
  28.6 0.0 collective-permute-done.6.refs_4_
  28.6 0.8 %finish.1 = f32[4,2304]{1,0:T(4,128)} custom-call(f32[16,576]{1,0:T(8,128)S(1)} %get-tuple-element.26.refs_0_, bf16[16,576]{1,0:T(8,128)(2,1)S(1)} %collective-permute-done.3.refs_1_, bf16[16,576]{1,0:T(8,128)(2,1)S(1)} %collective-permute-done.4.refs_2_, bf16[16,576]{1,0:T(8,128)(2,1)S(1)} %collective-permute-done.5.refs_3_, ...), custom_call_target="tpu_custom_call" | custom-call | flops 1000000 | bytes 3000000 | tf_op jit(solution)/shard_map/finish/pallas_call | solution.py:432
  (11 shorter events, 0.0 us)
Async XLA Ops:
  0.0 7.4 %copy-start.9 = (bf16[16,2304]{1,0:T(8,128)(2,1)S(1)}, bf16[16,2304]{1,0:T(8,128)(2,1)}, u32[]{:S(2)}) copy-start(bf16[16,2304]{1,0:T(8,128)(2,1)} %amps.1) | copy-start | bytes 221188
  0.0 7.7 %copy-start = (bf16[16,48,768]{2,1,0:T(8,128)(2,1)S(1)}, bf16[16,48,768]{2,1,0:T(8,128)(2,1)}, u32[]{:S(2)}) copy-start(bf16[16,48,768]{2,1,0:T(8,128)(2,1)} %panels.3) | copy-start | bytes 3538948
  0.0 7.7 %copy-start.2 = (s32[16]{0:T(128)S(1)}, s32[16]{0:T(128)}, u32[]{:S(2)}) copy-start(s32[16]{0:T(128)} %count.3) | copy-start | bytes 196
  0.0 7.7 %copy-start.4 = (s32[64,28,2]{0,2,1:T(2,128)S(1)}, s32[64,28,2]{0,2,1:T(2,128)}, u32[]{:S(2)}) copy-start(s32[64,28,2]{0,2,1:T(2,128)} %param.17) | copy-start | bytes 43012
  0.0 7.7 %copy-start.5 = (s32[64,28]{0,1:T(8,128)S(1)}, s32[64,28]{0,1:T(8,128)}, u32[]{:S(2)}) copy-start(s32[64,28]{0,1:T(8,128)} %param.18) | copy-start | bytes 21508
  0.0 7.7 %copy-start.7 = (s32[64,2]{0,1:T(2,128)S(1)}, s32[64,2]{0,1:T(2,128)}, u32[]{:S(2)}) copy-start(s32[64,2]{0,1:T(2,128)} %param.19) | copy-start | bytes 1540
  0.0 7.7 %copy-start.8 = (s32[64]{0:T(128)S(1)}, s32[64]{0:T(128)}, u32[]{:S(2)}) copy-start(s32[64]{0:T(128)} %param.16) | copy-start | bytes 772
  0.0 7.7 %copy-start.6 = (f32[16,48]{1,0:T(8,128)S(1)}, f32[16,48]{1,0:T(8,128)}, u32[]{:S(2)}) copy-start(f32[16,48]{1,0:T(8,128)} %energy.1) | copy-start | bytes 9220
  0.0 7.7 %copy-start.3 = (f32[64,64]{1,0:T(8,128)S(1)}, f32[64,64]{1,0:T(8,128)}, u32[]{:S(2)}) copy-start(f32[64,64]{1,0:T(8,128)} %fock.1) | copy-start | bytes 49156
  2.0 11.7 %collective-permute-start.1 = (bf16[208,768]{1,0:T(8,128)(2,1)}, bf16[208,768]{1,0:T(8,128)(2,1)S(1)}, u32[]{:S(2)}, u32[]{:S(2)}) collective-permute-start(bf16[208,768]{1,0:T(8,128)(2,1)} %pack.1.refs_6_), channel_id=1, source_target_pairs={{0,8},{12,4},{8,12},{4,0},{1,9},{13,5},{9,13},{5,1},{2,10},{14,6},... | collective-permute-start | bytes 958472 | tf_op jit(solution)/shard_map/ppermute | solution.py:486
  6.1 15.9 %collective-permute-start = (bf16[208,768]{1,0:T(8,128)(2,1)}, bf16[208,768]{1,0:T(8,128)(2,1)S(1)}, u32[]{:S(2)}, u32[]{:S(2)}) collective-permute-start(bf16[208,768]{1,0:T(8,128)(2,1)} %pack.1.refs_6_), channel_id=1, source_target_pairs={{4,8},{12,0},{5,9},{13,1},{6,10},{14,2},{7,11},{15,3},{20,24},{28,... | collective-permute-start | bytes 958472 | tf_op jit(solution)/shard_map/ppermute | solution.py:486
  7.7 6.0 %copy-start.1 = (bf16[208,768]{1,0:T(8,128)(2,1)S(1)}, bf16[208,768]{1,0:T(8,128)(2,1)}, u32[]{:S(2)}) copy-start(bf16[208,768]{1,0:T(8,128)(2,1)} %pack.1.refs_6_) | copy-start | bytes 958468
  16.8 8.7 %collective-permute-start.2 = (bf16[16,576]{1,0:T(8,128)(2,1)S(1)}, bf16[16,576]{1,0:T(8,128)(2,1)S(1)}, u32[]{:S(2)}, u32[]{:S(2)}) collective-permute-start(bf16[16,576]{1,0:T(8,128)(2,1)S(1)} %get-tuple-element.25), channel_id=1, source_target_pairs={{8,0},{4,12},{12,8},{0,4},{9,1},{5,13},{13,9},{1,5},{10,2},{6,14},... | collective-permute-start | bytes 55304 | tf_op jit(solution)/shard_map/ppermute | solution.py:518
  23.8 3.8 %collective-permute-start.3 = (bf16[16,576]{1,0:T(8,128)(2,1)S(1)}, bf16[16,576]{1,0:T(8,128)(2,1)S(1)}, u32[]{:S(2)}, u32[]{:S(2)}) collective-permute-start(bf16[16,576]{1,0:T(8,128)(2,1)S(1)} %get-tuple-element.27), channel_id=1, source_target_pairs={{8,4},{0,12},{4,0},{12,8},{9,5},{1,13},{5,1},{13,9},{10,6},{2,14},... | collective-permute-start | bytes 55304 | tf_op jit(solution)/shard_map/ppermute | solution.py:526
  23.8 3.8 %collective-permute-start.4 = (bf16[16,576]{1,0:T(8,128)(2,1)S(1)}, bf16[16,576]{1,0:T(8,128)(2,1)S(1)}, u32[]{:S(2)}, u32[]{:S(2)}) collective-permute-start(bf16[16,576]{1,0:T(8,128)(2,1)S(1)} %get-tuple-element.28), channel_id=1, source_target_pairs={{0,2},{1,3},{2,0},{3,1},{4,6},{5,7},{6,4},{7,5},{8,10},{9,11},{10,... | collective-permute-start | bytes 55304 | tf_op jit(solution)/shard_map/ppermute | solution.py:537
  25.4 3.2 %collective-permute-start.5 = (bf16[16,576]{1,0:T(8,128)(2,1)S(1)}, bf16[16,576]{1,0:T(8,128)(2,1)S(1)}, u32[]{:S(2)}, u32[]{:S(2)}) collective-permute-start(bf16[16,576]{1,0:T(8,128)(2,1)S(1)} %get-tuple-element.29), channel_id=1, source_target_pairs={{0,3},{1,2},{2,1},{3,0},{4,7},{5,6},{6,5},{7,4},{8,11},{9,10},{10,... | collective-permute-start | bytes 55304 | tf_op jit(solution)/shard_map/ppermute | solution.py:537
  26.5 2.1 %collective-permute-start.6 = (bf16[16,576]{1,0:T(8,128)(2,1)S(1)}, bf16[16,576]{1,0:T(8,128)(2,1)S(1)}, u32[]{:S(2)}, u32[]{:S(2)}) collective-permute-start(bf16[16,576]{1,0:T(8,128)(2,1)S(1)} %get-tuple-element.30), channel_id=1, source_target_pairs={{0,1},{1,0},{2,3},{3,2},{4,5},{5,4},{6,7},{7,6},{8,9},{9,8},{10,11... | collective-permute-start | bytes 55304 | tf_op jit(solution)/shard_map/ppermute | solution.py:537

commit v4 on v3

--- a/solution.py
+++ b/solution.py
@@ -182,82 +182,99 @@
     couplings = orbital.shape[0]
     per_dev = energy.shape[0]
     pair_devices = total // per_dev
+    wide = per_dev * width
+    thin = block * width
+    functions = held.shape[2]
+    pao = held.shape[3]
     pair = lax.axis_index("pair")
     first = lax.axis_index("aux") * block
-    here = pos[...] == iota((total, total), 0)
-    label_at = jnp.sum(jnp.where(here, iota((total, total), 1), 0), axis=1, keepdims=True)
     level = iota((occ, total), 0)
     hot_i = (lmo[0:1, :] == level).astype(F32)
     hot_j = (lmo[1:2, :] == level).astype(F32)
-    fock_of[0] = dot_nn(fock[...], hot_j, HIGHEST)
-    fock_of[1] = lax.dot_general(
-        fock[...], hot_i, (((0,), (0,)), ((), ())), precision=HIGHEST, preferred_element_type=F32
-    )
-    weight[...] = jnp.zeros_like(weight)
-
-    def add(c, carry):
-        hot_k = orbital[pl.ds(c, 1), :] == level
-        for h in range(2):
-            value = jnp.sum(jnp.where(hot_k, fock_of[h], 0.0), axis=0, keepdims=True)
-            named = coupling[pl.ds(2 * c + h, 1), :] == label_at
-            weight[...] += jnp.where(named, value, 0.0)
-        return carry
-
-    lax.fori_loop(0, couplings, add, 0, unroll=4)
-
-    def of_pairs(rows, start):
-        hot = (iota((rows, total), 1) == start + iota((rows, total), 0)).astype(F32)
-        return dot_nt(hot, weight[...], HIGHEST)
-
-    wide = per_dev * width
-    thin = block * width
-    wide_pair, wide_pno = lane_in(width, wide)
-    thin_pair, _ = lane_in(width, thin)
-    mine = of_pairs(per_dev, pair * per_dev)
-    local = (iota((total, wide), 0) == pair * per_dev + wide_pair).astype(F32)
-    for k in range(len(ways) + 1):
-        start = pair
-        if k > 0:
-            start = jnp.int32(-pair_devices)
-            for sender, receiver in ways[k - 1]:
-                start = jnp.where(pair == receiver, sender, start)
-        source = start * per_dev + first
-        spread = (iota((total, thin), 0) == source + thin_pair).astype(F32)
-        spread = dot_nn(mine, spread, HIGHEST)
-        for group in range(groups):
-            part = slice(group * block, (group + 1) * block)
-            weight_in[k, group, :block, :] = spread[part, :]
-        if k > 0:
-            weight_out[k - 1] = dot_nn(of_pairs(8, source), local, HIGHEST)
-
-    repeat = (iota((width, wide), 0) == wide_pno).astype(F32).astype(BF16)
-    tiled = dot_nn(amps[...], repeat)
-    row_pair, _ = row_in(width, wide)
-    block_amps[...] = jnp.where(row_pair == wide_pair, tiled, 0.0).astype(BF16)
-
-    for copy in copies:
-        copy.wait()
-    across = iota((occ, occ), 0) == iota((occ, occ), 1)
-    diagonal = jnp.sum(jnp.where(across, fock[...], 0.0), axis=1, keepdims=True)
-    gap_of = jnp.sum((hot_i + hot_j) * diagonal, axis=0, keepdims=True)
-    row = iota((width, width), 0)
-    column = iota((width, width), 1)
-    for j in range(block):
-        at = iota((1, total), 1) == pair * per_dev + first + j
-        gap = jnp.sum(jnp.where(at, gap_of, 0.0), axis=1, keepdims=True)
-        flat = energy[pl.ds(first + j, 1), :]
-        upright = jnp.sum(jnp.where(row == column, flat, 0.0), axis=1, keepdims=True)
-        live = count_held[first + j]
-        values = amps[pl.ds((first + j) * width, width), :].astype(F32)
-        term = (upright + flat - gap) * values
-        own[:, j * width : (j + 1) * width] = jnp.where((row < live) & (column < live), term, 0.0)
-
-    functions = held.shape[2]
-    pao = held.shape[3]
-    for p in range(per_dev):
-        masked[p * width : (p + 1) * width, :] = masked_rows(panels_held[p], count_held[p])
-    for group in range(groups):
-        fits[group].wait()
+
+    def weights_of_targets():
+        here = pos[...] == iota((total, total), 0)
+        label_at = jnp.sum(jnp.where(here, iota((total, total), 1), 0), axis=1, keepdims=True)
+        fock_of[0] = dot_nn(fock[...], hot_j, HIGHEST)
+        fock_of[1] = lax.dot_general(
+            fock[...], hot_i, (((0,), (0,)), ((), ())), precision=HIGHEST, preferred_element_type=F32
+        )
+
+        def add(c, value):
+            hot_k = orbital[pl.ds(c, 1), :] == level
+            for h in range(2):
+                fock_k = jnp.sum(jnp.where(hot_k, fock_of[h], 0.0), axis=0, keepdims=True)
+                named = coupling[pl.ds(2 * c + h, 1), :] == label_at
+                value = value + jnp.where(named, fock_k, 0.0)
+            return value
+
+        if total <= 128:
+            value = jnp.zeros((total, total), F32)
+            for c in range(couplings):
+                value = add(c, value)
+            weight[...] = value
+        else:
+            weight[...] = jnp.zeros_like(weight)
+
+            def step(c, carry):
+                weight[...] = add(c, weight[...])
+                return carry
+
+            lax.fori_loop(0, couplings, step, 0)
+
+    def spread_weights():
+        def of_pairs(rows, start):
+            hot = (iota((rows, total), 1) == start + iota((rows, total), 0)).astype(F32)
+            return dot_nt(hot, weight[...], HIGHEST)
+
+        wide_pair, _ = lane_in(width, wide)
+        thin_pair, _ = lane_in(width, thin)
+        mine = of_pairs(per_dev, pair * per_dev)
+        local = (iota((total, wide), 0) == pair * per_dev + wide_pair).astype(F32)
+        for k in range(len(ways) + 1):
+            start = pair
+            if k > 0:
+                start = jnp.int32(-pair_devices)
+                for sender, receiver in ways[k - 1]:
+                    start = jnp.where(pair == receiver, sender, start)
+            source = start * per_dev + first
+            spread = (iota((total, thin), 0) == source + thin_pair).astype(F32)
+            spread = dot_nn(mine, spread, HIGHEST)
+            for group in range(groups):
+                part = slice(group * block, (group + 1) * block)
+                weight_in[k, group, :block, :] = spread[part, :]
+            if k > 0:
+                weight_out[k - 1] = dot_nn(of_pairs(8, source), local, HIGHEST)
+
+    def amplitudes_and_energies():
+        wide_pair, wide_pno = lane_in(width, wide)
+        repeat = (iota((width, wide), 0) == wide_pno).astype(F32).astype(BF16)
+        tiled = dot_nn(amps[...], repeat)
+        row_pair, _ = row_in(width, wide)
+        block_amps[...] = jnp.where(row_pair == wide_pair, tiled, 0.0).astype(BF16)
+        across = iota((occ, occ), 0) == iota((occ, occ), 1)
+        diagonal = jnp.sum(jnp.where(across, fock[...], 0.0), axis=1, keepdims=True)
+        gap_of = jnp.sum((hot_i + hot_j) * diagonal, axis=0, keepdims=True)
+        row = iota((width, width), 0)
+        column = iota((width, width), 1)
+        for j in range(block):
+            at = iota((1, total), 1) == pair * per_dev + first + j
+            gap = jnp.sum(jnp.where(at, gap_of, 0.0), axis=1, keepdims=True)
+            flat = energy[pl.ds(first + j, 1), :]
+            upright = jnp.sum(jnp.where(row == column, flat, 0.0), axis=1, keepdims=True)
+            live = count_held[first + j]
+            values = amps[pl.ds((first + j) * width, width), :].astype(F32)
+            inside = (row < live) & (column < live)
+            lanes = slice(j * width, (j + 1) * width)
+            own[:, lanes] = jnp.where(inside, (upright + flat - gap) * values, 0.0)
+
+    def masked_panels():
+        for copy in copies:
+            copy.wait()
+        for p in range(per_dev):
+            masked[p * width : (p + 1) * width, :] = masked_rows(panels_held[p], count_held[p])
+
+    def exchange(group):
         for p in range(group * block, (group + 1) * block):
             rows = slice(p * width, (p + 1) * width)
             if functions % 128 == 0:
@@ -269,6 +286,18 @@
                     both[h, rows, :] = dot_nt(masked[rows, :], held[p, h]).astype(BF16)
         rows = slice(group * thin, (group + 1) * thin)
         out[group] = fold_diagonal(dot_nt(both[0, rows, :], both[1, rows, :]), width)
+
+    beside = [weights_of_targets, spread_weights, amplitudes_and_energies]
+    beside.pop(0)()
+    beside.pop(0)()
+    masked_panels()
+    for group in range(groups):
+        fits[group].wait()
+        exchange(group)
+        if beside:
+            beside.pop(0)()
+    for piece in beside:
+        piece()
 
 
 def local(coupling, orbital, lmo, pos, fock, amps, energy, count, fit, panels, block, ways):
@@ -535,7 +564,7 @@
     sums = {0: last_back}
     for k in range(1, aux_devices):
         sums[k] = lax.ppermute(parts[k], "aux", [(d, d ^ k) for d in range(aux_devices)])
-    order = [0, 2, 3]
+    order = [0, 3, 2]
     order += [k for k in range(1, aux_devices) if k not in order]
     sums = [parts[0]] + [sums[k] for k in order]
     return call(

time: 29.6 us -> 28.8 us (0.973)
  Pallas kernels: 14.7 us -> 14.1 us
  waiting for transfers between devices: 3.74 us -> 3.39 us
    ppermute x3, waiting for transfers between devices: 0.99 us -> 0.22 us  [on_device(): lax.ppermute(parts[k], 'aux', [(d, d ^ k) for d in range(aux_devices)])]
    pallas_call x1, Pallas kernels: 5.98 us -> 5.35 us  [local(): pl.pallas_call(functools.partial(local_kernel, block, width, ways), out_s...]
    ppermute x1, starting transfers between devices: 2.92 us -> 3.42 us  [on_device(): returned.append(lax.ppermute(back, 'pair', back_ways[k - 1]))]
    ppermute x3, starting transfers between devices: 2.23 us -> 1.93 us  [on_device(): lax.ppermute(parts[k], 'aux', [(d, d ^ k) for d in range(aux_devices)])]
  transfers between devices with their start and end apart: 7 -> 7, of which waited for: 4 -> 5; matrix products, arithmetic and copies ran while one was open for 1% -> 1% of each run, Pallas kernels for 40% -> 39%
where the time goes in v4:
time: 28.8 us; the launch traced here: 28.7 us
  Pallas kernels  14.1 us (49%)
  starting transfers between devices  10.7 us (37%)
  waiting for transfers between devices  3.39 us (12%)
    pallas_call x4, Pallas kernels, call(): pl.pallas_call(kernel, out_shape=out_shape, in_specs=[whole()] * len(args...  6.76 us
    ppermute x2, starting transfers between devices, on_device(): arrived = [lax.ppermute(sent, 'pair', way) for way in ways]  5.38 us
    pallas_call x1, Pallas kernels, local(): pl.pallas_call(functools.partial(local_kernel, block, width, ways), out_s...  5.35 us
    ppermute x1, starting transfers between devices, on_device(): returned.append(lax.ppermute(back, 'pair', back_ways[k - 1]))  3.42 us
    ppermute x2, waiting for transfers between devices, on_device(): arrived = [lax.ppermute(sent, 'pair', way) for way in ways]  2.48 us
    pallas_call x1, Pallas kernels, pack(): pl.pallas_call(functools.partial(pack_kernel, block, width, chunks), out_...  1.97 us
    ppermute x3, starting transfers between devices, on_device(): lax.ppermute(parts[k], 'aux', [(d, d ^ k) for d in range(aux_devices)])  1.93 us
    ppermute x1, waiting for transfers between devices, on_device(): last_back = lax.ppermute(back, 'pair', back_ways[-1])  0.68 us
  transfers between devices with their start and end apart: 7, of which 5 were waited for; matrix products, arithmetic and copies ran while one was open for 1% of the time, Pallas kernels for 39%

profile of v4, /device:TPU:0, one launch (start us, length us, event | category | flops | bytes accessed | tf_op | source)
XLA Modules:
  0.0 28.7 jit_solution(1717095206755059854)
XLA Ops:
  0.0 0.0 copy-start.7
  0.0 0.0 copy-start.8
  0.0 0.0 copy-start.6
  0.0 0.0 copy-start.3
  0.1 2.0 %pack.1.refs_6_ = bf16[208,768]{1,0:T(8,128)(2,1)} custom-call(bf16[16,48,768]{2,1,0:T(8,128)(2,1)} %panels.3, bf16[16,2304]{1,0:T(8,128)(2,1)} %amps.1, s32[16]{0:T(128)} %count.3), custom_call_target="tpu_custom_call" | custom-call | tf_op jit(solution)/shard_map/pack/pallas_call | solution.py:124
  2.0 4.1 %collective-permute-start.1 = (bf16[208,768]{1,0:T(8,128)(2,1)}, bf16[208,768]{1,0:T(8,128)(2,1)S(1)}, u32[]{:S(2)}, u32[]{:S(2)}) collective-permute-start(bf16[208,768]{1,0:T(8,128)(2,1)} %pack.1.refs_6_), channel_id=1, source_target_pairs={{0,8},{12,4},{8,12},{4,0},{1,9},{13,5},{9,13},{5,1},{2,10},{14,6},... | collective-permute-start | bytes 958472 | tf_op jit(solution)/shard_map/ppermute | solution.py:515
  6.1 1.3 %collective-permute-start = (bf16[208,768]{1,0:T(8,128)(2,1)}, bf16[208,768]{1,0:T(8,128)(2,1)S(1)}, u32[]{:S(2)}, u32[]{:S(2)}) collective-permute-start(bf16[208,768]{1,0:T(8,128)(2,1)} %pack.1.refs_6_), channel_id=1, source_target_pairs={{4,8},{12,0},{5,9},{13,1},{6,10},{14,2},{7,11},{15,3},{20,24},{28,... | collective-permute-start | bytes 958472 | tf_op jit(solution)/shard_map/ppermute | solution.py:515
  7.4 0.0 copy-done.9
  7.4 0.2 reshape.7.amps
  7.7 0.0 copy-done
  7.7 0.0 copy-done.2
  7.7 0.0 copy-done.4
  7.7 0.0 copy-done.5
  7.7 0.0 copy-done.7
  7.7 5.3 %local.1 = (f32[3,4,8,192]{3,2,1,0:T(8,128)S(1)}, f32[2,8,768]{2,1,0:T(8,128)S(1)}, bf16[768,768]{1,0:T(8,128)(2,1)S(1)}, f32[48,192]{1,0:T(8,128)S(1)}, bf16[76...) custom-call(s32[56,64]{1,0:T(8,128)S(1)} %bitcast.16, s32[28,64]{1,0:T(8,128)S(1)} %bitcast.17, s32[2,64]{1,0:T(2,128)S(1)} %bitcast.18, ...), custom_call_target="tpu_custom_call" | custom-call | flops 6000000000 | bytes 6291456 | tf_op jit(solution)/shard_map/local/pallas_call | solution.py:311
  13.1 0.1 collective-permute-done.1.refs_3_
  13.3 0.0 copy-done.1
  13.3 3.0 %couple.1 = (f32[4,48,192]{2,1,0:T(8,128)S(1)}, bf16[16,576]{1,0:T(8,128)(2,1)S(1)}) custom-call(bf16[768,768]{1,0:T(8,128)(2,1)S(1)} %get-tuple-element.18.refs_0_.masked, bf16[768,768]{1,0:T(8,128)(2,1)S(1)} %get-tuple-element.20.refs_1_.block_amps, f32[4,48,192]{2,1,0:T(8,128)S(1)} %get-tuple-element.21.refs_2_, ...), custom_call_target="tpu_custom_call" | custom-call | flops 2000000000 | bytes 3000000 | tf_op jit(solution)/shard_map/couple/pallas_call | solution.py:461
  16.2 3.4 %collective-permute-start.2 = (bf16[16,576]{1,0:T(8,128)(2,1)S(1)}, bf16[16,576]{1,0:T(8,128)(2,1)S(1)}, u32[]{:S(2)}, u32[]{:S(2)}) collective-permute-start(bf16[16,576]{1,0:T(8,128)(2,1)S(1)} %get-tuple-element.25), channel_id=1, source_target_pairs={{8,0},{4,12},{12,8},{0,4},{9,1},{5,13},{13,9},{1,5},{10,2},{6,14},... | collective-permute-start | bytes 55304 | tf_op jit(solution)/shard_map/ppermute | solution.py:547
  19.7 2.3 %collective-permute-done.sent = bf16[208,768]{1,0:T(8,128)(2,1)S(1)} collective-permute-done((bf16[208,768]{1,0:T(8,128)(2,1)}, bf16[208,768]{1,0:T(8,128)(2,1)S(1)}, u32[]{:S(2)}, u32[]{:S(2)}) %collective-permute-start) | collective-permute-done | bytes 319520 | tf_op jit(solution)/shard_map/ppermute | solution.py:515
  22.0 1.8 %couple_far.1 = (bf16[16,576]{1,0:T(8,128)(2,1)S(1)}, bf16[16,576]{1,0:T(8,128)(2,1)S(1)}, bf16[16,576]{1,0:T(8,128)(2,1)S(1)}) custom-call(bf16[208,768]{1,0:T(8,128)(2,1)S(1)} %collective-permute-done.sent, bf16[768,768]{1,0:T(8,128)(2,1)S(1)} %get-tuple-element.18.refs_0_.masked, bf16[768,768]{1,0:T(8,128)(2,1)S(1)} %get-tuple-element.20.refs_1_.block_amps, ...), custom_call_target="tpu_custom_call" | custom-call | flops 1000000000 | bytes 3000000 | tf_op jit(solution)/shard_map/couple_far/pallas_call | solution.py:461
  23.8 0.0 collective-permute-start.3
  23.8 0.1 collective-permute-start.4
  23.9 1.6 %collective-permute-start.5 = (bf16[16,576]{1,0:T(8,128)(2,1)S(1)}, bf16[16,576]{1,0:T(8,128)(2,1)S(1)}, u32[]{:S(2)}, u32[]{:S(2)}) collective-permute-start(bf16[16,576]{1,0:T(8,128)(2,1)S(1)} %get-tuple-element.29), channel_id=1, source_target_pairs={{0,2},{1,3},{2,0},{3,1},{4,6},{5,7},{6,4},{7,5},{8,10},{9,11},{10,... | collective-permute-start | bytes 55304 | tf_op jit(solution)/shard_map/ppermute | solution.py:566
  25.5 0.0 collective-permute-done.2.refs_0_
  25.5 1.2 %couple_near.1 = (f32[16,576]{1,0:T(8,128)S(1)}, bf16[16,576]{1,0:T(8,128)(2,1)S(1)}) custom-call(bf16[208,768]{1,0:T(8,128)(2,1)S(1)} %collective-permute-done.sent, bf16[768,768]{1,0:T(8,128)(2,1)S(1)} %get-tuple-element.18.refs_0_.masked, f32[4,8,192]{2,1,0:T(8,128)S(1)} %get-tuple-element.33.weight_in, f32[4,48,192]{2,1,0:T(8,128)S(1)} %get-tuple-element.23.acc, ...), custom_call_target="tpu_custom_call" | custom-call | flops 1000000000 | bytes 3000000 | tf_op jit(solution)/shard_map/couple_near/pallas_call | solution.py:461
  26.6 0.3 %collective-permute-start.6 = (bf16[16,576]{1,0:T(8,128)(2,1)S(1)}, bf16[16,576]{1,0:T(8,128)(2,1)S(1)}, u32[]{:S(2)}, u32[]{:S(2)}) collective-permute-start(bf16[16,576]{1,0:T(8,128)(2,1)S(1)} %get-tuple-element.30), channel_id=1, source_target_pairs={{0,1},{1,0},{2,3},{3,2},{4,5},{5,4},{6,7},{7,6},{8,9},{9,8},{10,11... | collective-permute-start | bytes 55304 | tf_op jit(solution)/shard_map/ppermute | solution.py:566
  26.9 0.7 %collective-permute-done.3.refs_1_ = bf16[16,576]{1,0:T(8,128)(2,1)S(1)} collective-permute-done((bf16[16,576]{1,0:T(8,128)(2,1)S(1)}, bf16[16,576]{1,0:T(8,128)(2,1)S(1)}, u32[]{:S(2)}, u32[]{:S(2)}) %collective-permute-start.3) | collective-permute-done | bytes 18464 | tf_op jit(solution)/shard_map/ppermute | solution.py:555
  27.6 0.0 collective-permute-done.4.refs_2_
  27.6 0.1 collective-permute-done.5.refs_3_
  27.8 0.1 collective-permute-done.6.refs_4_
  27.8 0.8 %finish.1 = f32[4,2304]{1,0:T(4,128)} custom-call(f32[16,576]{1,0:T(8,128)S(1)} %get-tuple-element.26.refs_0_, bf16[16,576]{1,0:T(8,128)(2,1)S(1)} %collective-permute-done.3.refs_1_, bf16[16,576]{1,0:T(8,128)(2,1)S(1)} %collective-permute-done.4.refs_2_, bf16[16,576]{1,0:T(8,128)(2,1)S(1)} %collective-permute-done.5.refs_3_, ...), custom_call_target="tpu_custom_call" | custom-call | flops 1000000 | bytes 3000000 | tf_op jit(solution)/shard_map/finish/pallas_call | solution.py:461
  (11 shorter events, 0.0 us)
Async XLA Ops:
  0.0 7.4 %copy-start.9 = (bf16[16,2304]{1,0:T(8,128)(2,1)S(1)}, bf16[16,2304]{1,0:T(8,128)(2,1)}, u32[]{:S(2)}) copy-start(bf16[16,2304]{1,0:T(8,128)(2,1)} %amps.1) | copy-start | bytes 221188
  0.0 7.7 %copy-start = (bf16[16,48,768]{2,1,0:T(8,128)(2,1)S(1)}, bf16[16,48,768]{2,1,0:T(8,128)(2,1)}, u32[]{:S(2)}) copy-start(bf16[16,48,768]{2,1,0:T(8,128)(2,1)} %panels.3) | copy-start | bytes 3538948
  0.0 7.7 %copy-start.2 = (s32[16]{0:T(128)S(1)}, s32[16]{0:T(128)}, u32[]{:S(2)}) copy-start(s32[16]{0:T(128)} %count.3) | copy-start | bytes 196
  0.0 7.7 %copy-start.4 = (s32[64,28,2]{0,2,1:T(2,128)S(1)}, s32[64,28,2]{0,2,1:T(2,128)}, u32[]{:S(2)}) copy-start(s32[64,28,2]{0,2,1:T(2,128)} %param.17) | copy-start | bytes 43012
  0.0 7.7 %copy-start.5 = (s32[64,28]{0,1:T(8,128)S(1)}, s32[64,28]{0,1:T(8,128)}, u32[]{:S(2)}) copy-start(s32[64,28]{0,1:T(8,128)} %param.18) | copy-start | bytes 21508
  0.0 7.7 %copy-start.7 = (s32[64,2]{0,1:T(2,128)S(1)}, s32[64,2]{0,1:T(2,128)}, u32[]{:S(2)}) copy-start(s32[64,2]{0,1:T(2,128)} %param.19) | copy-start | bytes 1540
  0.0 7.7 %copy-start.8 = (s32[64]{0:T(128)S(1)}, s32[64]{0:T(128)}, u32[]{:S(2)}) copy-start(s32[64]{0:T(128)} %param.16) | copy-start | bytes 772
  0.0 7.7 %copy-start.6 = (f32[16,48]{1,0:T(8,128)S(1)}, f32[16,48]{1,0:T(8,128)}, u32[]{:S(2)}) copy-start(f32[16,48]{1,0:T(8,128)} %energy.1) | copy-start | bytes 9220
  0.0 7.7 %copy-start.3 = (f32[64,64]{1,0:T(8,128)S(1)}, f32[64,64]{1,0:T(8,128)}, u32[]{:S(2)}) copy-start(f32[64,64]{1,0:T(8,128)} %fock.1) | copy-start | bytes 49156
  2.0 11.3 %collective-permute-start.1 = (bf16[208,768]{1,0:T(8,128)(2,1)}, bf16[208,768]{1,0:T(8,128)(2,1)S(1)}, u32[]{:S(2)}, u32[]{:S(2)}) collective-permute-start(bf16[208,768]{1,0:T(8,128)(2,1)} %pack.1.refs_6_), channel_id=1, source_target_pairs={{0,8},{12,4},{8,12},{4,0},{1,9},{13,5},{9,13},{5,1},{2,10},{14,6},... | collective-permute-start | bytes 958472 | tf_op jit(solution)/shard_map/ppermute | solution.py:515
  6.1 15.9 %collective-permute-start = (bf16[208,768]{1,0:T(8,128)(2,1)}, bf16[208,768]{1,0:T(8,128)(2,1)S(1)}, u32[]{:S(2)}, u32[]{:S(2)}) collective-permute-start(bf16[208,768]{1,0:T(8,128)(2,1)} %pack.1.refs_6_), channel_id=1, source_target_pairs={{4,8},{12,0},{5,9},{13,1},{6,10},{14,2},{7,11},{15,3},{20,24},{28,... | collective-permute-start | bytes 958472 | tf_op jit(solution)/shard_map/ppermute | solution.py:515
  7.7 5.5 %copy-start.1 = (bf16[208,768]{1,0:T(8,128)(2,1)S(1)}, bf16[208,768]{1,0:T(8,128)(2,1)}, u32[]{:S(2)}) copy-start(bf16[208,768]{1,0:T(8,128)(2,1)} %pack.1.refs_6_) | copy-start | bytes 958468
  16.2 9.2 %collective-permute-start.2 = (bf16[16,576]{1,0:T(8,128)(2,1)S(1)}, bf16[16,576]{1,0:T(8,128)(2,1)S(1)}, u32[]{:S(2)}, u32[]{:S(2)}) collective-permute-start(bf16[16,576]{1,0:T(8,128)(2,1)S(1)} %get-tuple-element.25), channel_id=1, source_target_pairs={{8,0},{4,12},{12,8},{0,4},{9,1},{5,13},{13,9},{1,5},{10,2},{6,14},... | collective-permute-start | bytes 55304 | tf_op jit(solution)/shard_map/ppermute | solution.py:547
  23.8 3.8 %collective-permute-start.3 = (bf16[16,576]{1,0:T(8,128)(2,1)S(1)}, bf16[16,576]{1,0:T(8,128)(2,1)S(1)}, u32[]{:S(2)}, u32[]{:S(2)}) collective-permute-start(bf16[16,576]{1,0:T(8,128)(2,1)S(1)} %get-tuple-element.27), channel_id=1, source_target_pairs={{8,4},{0,12},{4,0},{12,8},{9,5},{1,13},{5,1},{13,9},{10,6},{2,14},... | collective-permute-start | bytes 55304 | tf_op jit(solution)/shard_map/ppermute | solution.py:555
  23.8 3.8 %collective-permute-start.4 = (bf16[16,576]{1,0:T(8,128)(2,1)S(1)}, bf16[16,576]{1,0:T(8,128)(2,1)S(1)}, u32[]{:S(2)}, u32[]{:S(2)}) collective-permute-start(bf16[16,576]{1,0:T(8,128)(2,1)S(1)} %get-tuple-element.28), channel_id=1, source_target_pairs={{0,3},{1,2},{2,1},{3,0},{4,7},{5,6},{6,5},{7,4},{8,11},{9,10},{10,... | collective-permute-start | bytes 55304 | tf_op jit(solution)/shard_map/ppermute | solution.py:566
  23.9 3.8 %collective-permute-start.5 = (bf16[16,576]{1,0:T(8,128)(2,1)S(1)}, bf16[16,576]{1,0:T(8,128)(2,1)S(1)}, u32[]{:S(2)}, u32[]{:S(2)}) collective-permute-start(bf16[16,576]{1,0:T(8,128)(2,1)S(1)} %get-tuple-element.29), channel_id=1, source_target_pairs={{0,2},{1,3},{2,0},{3,1},{4,6},{5,7},{6,4},{7,5},{8,10},{9,11},{10,... | collective-permute-start | bytes 55304 | tf_op jit(solution)/shard_map/ppermute | solution.py:566
  26.6 1.2 %collective-permute-start.6 = (bf16[16,576]{1,0:T(8,128)(2,1)S(1)}, bf16[16,576]{1,0:T(8,128)(2,1)S(1)}, u32[]{:S(2)}, u32[]{:S(2)}) collective-permute-start(bf16[16,576]{1,0:T(8,128)(2,1)S(1)} %get-tuple-element.30), channel_id=1, source_target_pairs={{0,1},{1,0},{2,3},{3,2},{4,5},{5,4},{6,7},{7,6},{8,9},{9,8},{10,11... | collective-permute-start | bytes 55304 | tf_op jit(solution)/shard_map/ppermute | solution.py:566

commit v5 on v4

--- a/solution.py
+++ b/solution.py
@@ -379,13 +379,22 @@
         put(group, fold_diagonal(square, width))
 
 
-def add_in_group(block, width, masked, sent, amps, weight_in, group):
+def add_in_two(block, width, masked, sent, amps, weight_in, away):
     thin = block * width
-    rows = pl.ds(pl.multiple_of(group * thin, thin), thin)
+    aux = lax.axis_index("aux")
+    odd = lax.bitwise_and(aux, 1)
+    base = lax.bitwise_xor(aux, away) - odd
+    rows = pl.ds(pl.multiple_of(base * thin, thin), 2 * thin)
     inter = dot_nt(masked[rows, :], sent[:thin, :]).astype(BF16)
     half = dot_nn(inter, amps).astype(BF16).astype(F32)
-    high, low = split_high_low(scaled(half, weight_in[group], width))
-    return fold_diagonal(dot_nt(high, inter) + dot_nt(low, inter), width)
+    added = []
+    for n in range(2):
+        part = slice(n * thin, (n + 1) * thin)
+        high, low = split_high_low(scaled(half[part, :], weight_in[base + n], width))
+        square = dot_nt(high, inter[part, :])
+        added.append(fold_diagonal(square, width))
+    first, second = added
+    return jnp.where(odd == 0, first, second), jnp.where(odd == 0, second, first)
 
 
 def add_back(block, width, sent, masked, block_amps, weight_out):
@@ -393,7 +402,7 @@
     inter = dot_nt(sent[:thin, :], masked[...]).astype(BF16)
     half = dot_nn(inter, block_amps[...]).astype(BF16).astype(F32)
     high, low = split_high_low(scaled(half, weight_out, width))
-    return fold_diagonal(dot_nt(high, inter) + dot_nt(low, inter), width)
+    return fold_diagonal(dot_nt(high, inter), width)
 
 
 def both_kernel(block, width, *refs):
@@ -415,26 +424,23 @@
     amps = unpack_amps(sent, block, width)
     aux = lax.axis_index("aux")
     back[...] = as_sent(add_back(block, width, sent, masked, block_amps, weight_out)).astype(BF16)
-    for k, out in enumerate(outs, NEAR):
-        group = lax.bitwise_xor(aux, k)
-        added = add_in_group(block, width, masked, sent, amps, weight_in, group)
-        out[...] = as_sent(acc[group] - added).astype(BF16)
+    for k in range(0, len(outs), 2):
+        added = add_in_two(block, width, masked, sent, amps, weight_in, NEAR + k)
+        for n in range(2):
+            group = lax.bitwise_xor(aux, NEAR + k + n)
+            outs[k + n][...] = as_sent(acc[group] - added[n]).astype(BF16)
 
 
 def near_kernel(block, width, returned, sent, masked, weight_in, acc, own, *refs):
     backs, outs = refs[:returned], refs[returned:]
     amps = unpack_amps(sent, block, width)
     aux = lax.axis_index("aux")
-    for k, out in enumerate(outs):
-        group = lax.bitwise_xor(aux, k)
-        added = add_in_group(block, width, masked, sent, amps, weight_in, group)
-        if k > 0:
-            out[...] = as_sent(acc[group] - added).astype(BF16)
-        else:
-            mine = as_sent(acc[group] - added + own[...])
-            for back in backs:
-                mine -= back[...].astype(F32)
-            out[...] = mine
+    added = add_in_two(block, width, masked, sent, amps, weight_in, 0)
+    mine = as_sent(acc[aux] - added[0] + own[...])
+    for back in backs:
+        mine -= back[...].astype(F32)
+    outs[0][...] = mine
+    outs[1][...] = as_sent(acc[lax.bitwise_xor(aux, 1)] - added[1]).astype(BF16)
 
 
 def finish_kernel(block, width, count, *refs):

time: 28.8 us -> 28.6 us (level)
  Pallas kernels: 14.1 us -> 13.6 us
    pallas_call x4, Pallas kernels: 6.76 us -> 6.25 us  [call(): pl.pallas_call(kernel, out_shape=out_shape, in_specs=[whole()] * len(args...]
  transfers between devices with their start and end apart: 7 -> 7, of which waited for: 5 -> 4; matrix products, arithmetic and copies ran while one was open for 1% -> 1% of each run, Pallas kernels for 39% -> 38%
where the time goes in v5:
time: 28.6 us; the launch traced here: 28.4 us
  Pallas kernels  13.6 us (48%)
  starting transfers between devices  10.8 us (38%)
  waiting for transfers between devices  3.63 us (13%)
    pallas_call x4, Pallas kernels, call(): pl.pallas_call(kernel, out_shape=out_shape, in_specs=[whole()] * len(args...  6.25 us
    ppermute x2, starting transfers between devices, on_device(): arrived = [lax.ppermute(sent, 'pair', way) for way in ways]  5.38 us
    pallas_call x1, Pallas kernels, local(): pl.pallas_call(functools.partial(local_kernel, block, width, ways), out_s...  5.35 us
    ppermute x1, starting transfers between devices, on_device(): returned.append(lax.ppermute(back, 'pair', back_ways[k - 1]))  3.42 us
    ppermute x2, waiting for transfers between devices, on_device(): arrived = [lax.ppermute(sent, 'pair', way) for way in ways]  2.57 us
    pallas_call x1, Pallas kernels, pack(): pl.pallas_call(functools.partial(pack_kernel, block, width, chunks), out_...  1.97 us
    ppermute x3, starting transfers between devices, on_device(): lax.ppermute(parts[k], 'aux', [(d, d ^ k) for d in range(aux_devices)])  1.96 us
    ppermute x1, waiting for transfers between devices, on_device(): last_back = lax.ppermute(back, 'pair', back_ways[-1])  0.9 us
  transfers between devices with their start and end apart: 7, of which 4 were waited for; matrix products, arithmetic and copies ran while one was open for 1% of the time, Pallas kernels for 38%

profile of v5, /device:TPU:0, one launch (start us, length us, event | category | flops | bytes accessed | tf_op | source)
XLA Modules:
  0.0 28.4 jit_solution(15967401226883214827)
XLA Ops:
  0.0 0.0 copy-start.7
  0.0 0.0 copy-start.8
  0.0 0.0 copy-start.6
  0.0 0.0 copy-start.3
  0.1 2.0 %pack.1.refs_6_ = bf16[208,768]{1,0:T(8,128)(2,1)} custom-call(bf16[16,48,768]{2,1,0:T(8,128)(2,1)} %panels.3, bf16[16,2304]{1,0:T(8,128)(2,1)} %amps.1, s32[16]{0:T(128)} %count.3), custom_call_target="tpu_custom_call" | custom-call | tf_op jit(solution)/shard_map/pack/pallas_call | solution.py:124
  2.0 4.1 %collective-permute-start.1 = (bf16[208,768]{1,0:T(8,128)(2,1)}, bf16[208,768]{1,0:T(8,128)(2,1)S(1)}, u32[]{:S(2)}, u32[]{:S(2)}) collective-permute-start(bf16[208,768]{1,0:T(8,128)(2,1)} %pack.1.refs_6_), channel_id=1, source_target_pairs={{0,8},{12,4},{8,12},{4,0},{1,9},{13,5},{9,13},{5,1},{2,10},{14,6},... | collective-permute-start | bytes 958472 | tf_op jit(solution)/shard_map/ppermute | solution.py:521
  6.1 1.3 %collective-permute-start = (bf16[208,768]{1,0:T(8,128)(2,1)}, bf16[208,768]{1,0:T(8,128)(2,1)S(1)}, u32[]{:S(2)}, u32[]{:S(2)}) collective-permute-start(bf16[208,768]{1,0:T(8,128)(2,1)} %pack.1.refs_6_), channel_id=1, source_target_pairs={{4,8},{12,0},{5,9},{13,1},{6,10},{14,2},{7,11},{15,3},{20,24},{28,... | collective-permute-start | bytes 958472 | tf_op jit(solution)/shard_map/ppermute | solution.py:521
  7.4 0.0 copy-done.9
  7.4 0.2 reshape.7.amps
  7.7 0.0 copy-done
  7.7 0.0 copy-done.2
  7.7 0.0 copy-done.4
  7.7 0.0 copy-done.5
  7.7 0.0 copy-done.7
  7.7 5.3 %local.1 = (f32[3,4,8,192]{3,2,1,0:T(8,128)S(1)}, f32[2,8,768]{2,1,0:T(8,128)S(1)}, bf16[768,768]{1,0:T(8,128)(2,1)S(1)}, f32[48,192]{1,0:T(8,128)S(1)}, bf16[76...) custom-call(s32[56,64]{1,0:T(8,128)S(1)} %bitcast.16, s32[28,64]{1,0:T(8,128)S(1)} %bitcast.17, s32[2,64]{1,0:T(2,128)S(1)} %bitcast.18, ...), custom_call_target="tpu_custom_call" | custom-call | flops 6000000000 | bytes 6291456 | tf_op jit(solution)/shard_map/local/pallas_call | solution.py:311
  13.1 0.1 collective-permute-done.1.refs_3_
  13.3 0.0 copy-done.1
  13.3 2.9 %couple.1 = (f32[4,48,192]{2,1,0:T(8,128)S(1)}, bf16[16,576]{1,0:T(8,128)(2,1)S(1)}) custom-call(bf16[768,768]{1,0:T(8,128)(2,1)S(1)} %get-tuple-element.18.refs_0_.masked, bf16[768,768]{1,0:T(8,128)(2,1)S(1)} %get-tuple-element.20.refs_1_.block_amps, f32[4,48,192]{2,1,0:T(8,128)S(1)} %get-tuple-element.21.refs_2_, ...), custom_call_target="tpu_custom_call" | custom-call | flops 2000000000 | bytes 3000000 | tf_op jit(solution)/shard_map/couple/pallas_call | solution.py:467
  16.2 3.4 %collective-permute-start.2 = (bf16[16,576]{1,0:T(8,128)(2,1)S(1)}, bf16[16,576]{1,0:T(8,128)(2,1)S(1)}, u32[]{:S(2)}, u32[]{:S(2)}) collective-permute-start(bf16[16,576]{1,0:T(8,128)(2,1)S(1)} %get-tuple-element.25), channel_id=1, source_target_pairs={{8,0},{4,12},{12,8},{0,4},{9,1},{5,13},{13,9},{1,5},{10,2},{6,14},... | collective-permute-start | bytes 55304 | tf_op jit(solution)/shard_map/ppermute | solution.py:553
  19.6 2.4 %collective-permute-done.sent = bf16[208,768]{1,0:T(8,128)(2,1)S(1)} collective-permute-done((bf16[208,768]{1,0:T(8,128)(2,1)}, bf16[208,768]{1,0:T(8,128)(2,1)S(1)}, u32[]{:S(2)}, u32[]{:S(2)}) %collective-permute-start) | collective-permute-done | bytes 319520 | tf_op jit(solution)/shard_map/ppermute | solution.py:521
  22.0 1.6 %couple_far.1 = (bf16[16,576]{1,0:T(8,128)(2,1)S(1)}, bf16[16,576]{1,0:T(8,128)(2,1)S(1)}, bf16[16,576]{1,0:T(8,128)(2,1)S(1)}) custom-call(bf16[208,768]{1,0:T(8,128)(2,1)S(1)} %collective-permute-done.sent, bf16[768,768]{1,0:T(8,128)(2,1)S(1)} %get-tuple-element.18.refs_0_.masked, bf16[768,768]{1,0:T(8,128)(2,1)S(1)} %get-tuple-element.20.refs_1_.block_amps, ...), custom_call_target="tpu_custom_call" | custom-call | flops 1000000000 | bytes 3000000 | tf_op jit(solution)/shard_map/couple_far/pallas_call | solution.py:467
  23.7 0.0 collective-permute-start.3
  23.7 0.1 collective-permute-start.4
  23.8 1.6 %collective-permute-start.5 = (bf16[16,576]{1,0:T(8,128)(2,1)S(1)}, bf16[16,576]{1,0:T(8,128)(2,1)S(1)}, u32[]{:S(2)}, u32[]{:S(2)}) collective-permute-start(bf16[16,576]{1,0:T(8,128)(2,1)S(1)} %get-tuple-element.29), channel_id=1, source_target_pairs={{0,2},{1,3},{2,0},{3,1},{4,6},{5,7},{6,4},{7,5},{8,10},{9,11},{10,... | collective-permute-start | bytes 55304 | tf_op jit(solution)/shard_map/ppermute | solution.py:572
  25.3 0.0 collective-permute-done.2.refs_0_
  25.3 0.9 %couple_near.1 = (f32[16,576]{1,0:T(8,128)S(1)}, bf16[16,576]{1,0:T(8,128)(2,1)S(1)}) custom-call(bf16[208,768]{1,0:T(8,128)(2,1)S(1)} %collective-permute-done.sent, bf16[768,768]{1,0:T(8,128)(2,1)S(1)} %get-tuple-element.18.refs_0_.masked, f32[4,8,192]{2,1,0:T(8,128)S(1)} %get-tuple-element.33.weight_in, f32[4,48,192]{2,1,0:T(8,128)S(1)} %get-tuple-element.23.acc, ...), custom_call_target="tpu_custom_call" | custom-call | flops 1000000000 | bytes 3000000 | tf_op jit(solution)/shard_map/couple_near/pallas_call | solution.py:467
  26.2 0.3 %collective-permute-start.6 = (bf16[16,576]{1,0:T(8,128)(2,1)S(1)}, bf16[16,576]{1,0:T(8,128)(2,1)S(1)}, u32[]{:S(2)}, u32[]{:S(2)}) collective-permute-start(bf16[16,576]{1,0:T(8,128)(2,1)S(1)} %get-tuple-element.30), channel_id=1, source_target_pairs={{0,1},{1,0},{2,3},{3,2},{4,5},{5,4},{6,7},{7,6},{8,9},{9,8},{10,11... | collective-permute-start | bytes 55304 | tf_op jit(solution)/shard_map/ppermute | solution.py:572
  26.6 0.9 %collective-permute-done.3.refs_1_ = bf16[16,576]{1,0:T(8,128)(2,1)S(1)} collective-permute-done((bf16[16,576]{1,0:T(8,128)(2,1)S(1)}, bf16[16,576]{1,0:T(8,128)(2,1)S(1)}, u32[]{:S(2)}, u32[]{:S(2)}) %collective-permute-start.3) | collective-permute-done | bytes 18464 | tf_op jit(solution)/shard_map/ppermute | solution.py:561
  27.4 0.0 collective-permute-done.4.refs_2_
  27.5 0.2 collective-permute-done.5.refs_3_
  27.6 0.0 collective-permute-done.6.refs_4_
  27.6 0.8 %finish.1 = f32[4,2304]{1,0:T(4,128)} custom-call(f32[16,576]{1,0:T(8,128)S(1)} %get-tuple-element.26.refs_0_, bf16[16,576]{1,0:T(8,128)(2,1)S(1)} %collective-permute-done.3.refs_1_, bf16[16,576]{1,0:T(8,128)(2,1)S(1)} %collective-permute-done.4.refs_2_, bf16[16,576]{1,0:T(8,128)(2,1)S(1)} %collective-permute-done.5.refs_3_, ...), custom_call_target="tpu_custom_call" | custom-call | flops 1000000 | bytes 3000000 | tf_op jit(solution)/shard_map/finish/pallas_call | solution.py:467
  (11 shorter events, 0.0 us)
Async XLA Ops:
  0.0 7.4 %copy-start.9 = (bf16[16,2304]{1,0:T(8,128)(2,1)S(1)}, bf16[16,2304]{1,0:T(8,128)(2,1)}, u32[]{:S(2)}) copy-start(bf16[16,2304]{1,0:T(8,128)(2,1)} %amps.1) | copy-start | bytes 221188
  0.0 7.7 %copy-start = (bf16[16,48,768]{2,1,0:T(8,128)(2,1)S(1)}, bf16[16,48,768]{2,1,0:T(8,128)(2,1)}, u32[]{:S(2)}) copy-start(bf16[16,48,768]{2,1,0:T(8,128)(2,1)} %panels.3) | copy-start | bytes 3538948
  0.0 7.7 %copy-start.2 = (s32[16]{0:T(128)S(1)}, s32[16]{0:T(128)}, u32[]{:S(2)}) copy-start(s32[16]{0:T(128)} %count.3) | copy-start | bytes 196
  0.0 7.7 %copy-start.4 = (s32[64,28,2]{0,2,1:T(2,128)S(1)}, s32[64,28,2]{0,2,1:T(2,128)}, u32[]{:S(2)}) copy-start(s32[64,28,2]{0,2,1:T(2,128)} %param.17) | copy-start | bytes 43012
  0.0 7.7 %copy-start.5 = (s32[64,28]{0,1:T(8,128)S(1)}, s32[64,28]{0,1:T(8,128)}, u32[]{:S(2)}) copy-start(s32[64,28]{0,1:T(8,128)} %param.18) | copy-start | bytes 21508
  0.0 7.7 %copy-start.7 = (s32[64,2]{0,1:T(2,128)S(1)}, s32[64,2]{0,1:T(2,128)}, u32[]{:S(2)}) copy-start(s32[64,2]{0,1:T(2,128)} %param.19) | copy-start | bytes 1540
  0.0 7.7 %copy-start.8 = (s32[64]{0:T(128)S(1)}, s32[64]{0:T(128)}, u32[]{:S(2)}) copy-start(s32[64]{0:T(128)} %param.16) | copy-start | bytes 772
  0.0 7.7 %copy-start.6 = (f32[16,48]{1,0:T(8,128)S(1)}, f32[16,48]{1,0:T(8,128)}, u32[]{:S(2)}) copy-start(f32[16,48]{1,0:T(8,128)} %energy.1) | copy-start | bytes 9220
  0.0 7.7 %copy-start.3 = (f32[64,64]{1,0:T(8,128)S(1)}, f32[64,64]{1,0:T(8,128)}, u32[]{:S(2)}) copy-start(f32[64,64]{1,0:T(8,128)} %fock.1) | copy-start | bytes 49156
  2.0 11.3 %collective-permute-start.1 = (bf16[208,768]{1,0:T(8,128)(2,1)}, bf16[208,768]{1,0:T(8,128)(2,1)S(1)}, u32[]{:S(2)}, u32[]{:S(2)}) collective-permute-start(bf16[208,768]{1,0:T(8,128)(2,1)} %pack.1.refs_6_), channel_id=1, source_target_pairs={{0,8},{12,4},{8,12},{4,0},{1,9},{13,5},{9,13},{5,1},{2,10},{14,6},... | collective-permute-start | bytes 958472 | tf_op jit(solution)/shard_map/ppermute | solution.py:521
  6.1 15.9 %collective-permute-start = (bf16[208,768]{1,0:T(8,128)(2,1)}, bf16[208,768]{1,0:T(8,128)(2,1)S(1)}, u32[]{:S(2)}, u32[]{:S(2)}) collective-permute-start(bf16[208,768]{1,0:T(8,128)(2,1)} %pack.1.refs_6_), channel_id=1, source_target_pairs={{4,8},{12,0},{5,9},{13,1},{6,10},{14,2},{7,11},{15,3},{20,24},{28,... | collective-permute-start | bytes 958472 | tf_op jit(solution)/shard_map/ppermute | solution.py:521
  7.7 5.5 %copy-start.1 = (bf16[208,768]{1,0:T(8,128)(2,1)S(1)}, bf16[208,768]{1,0:T(8,128)(2,1)}, u32[]{:S(2)}) copy-start(bf16[208,768]{1,0:T(8,128)(2,1)} %pack.1.refs_6_) | copy-start | bytes 958468
  16.2 9.2 %collective-permute-start.2 = (bf16[16,576]{1,0:T(8,128)(2,1)S(1)}, bf16[16,576]{1,0:T(8,128)(2,1)S(1)}, u32[]{:S(2)}, u32[]{:S(2)}) collective-permute-start(bf16[16,576]{1,0:T(8,128)(2,1)S(1)} %get-tuple-element.25), channel_id=1, source_target_pairs={{8,0},{4,12},{12,8},{0,4},{9,1},{5,13},{13,9},{1,5},{10,2},{6,14},... | collective-permute-start | bytes 55304 | tf_op jit(solution)/shard_map/ppermute | solution.py:553
  23.7 3.8 %collective-permute-start.3 = (bf16[16,576]{1,0:T(8,128)(2,1)S(1)}, bf16[16,576]{1,0:T(8,128)(2,1)S(1)}, u32[]{:S(2)}, u32[]{:S(2)}) collective-permute-start(bf16[16,576]{1,0:T(8,128)(2,1)S(1)} %get-tuple-element.27), channel_id=1, source_target_pairs={{8,4},{0,12},{4,0},{12,8},{9,5},{1,13},{5,1},{13,9},{10,6},{2,14},... | collective-permute-start | bytes 55304 | tf_op jit(solution)/shard_map/ppermute | solution.py:561
  23.7 3.8 %collective-permute-start.4 = (bf16[16,576]{1,0:T(8,128)(2,1)S(1)}, bf16[16,576]{1,0:T(8,128)(2,1)S(1)}, u32[]{:S(2)}, u32[]{:S(2)}) collective-permute-start(bf16[16,576]{1,0:T(8,128)(2,1)S(1)} %get-tuple-element.28), channel_id=1, source_target_pairs={{0,3},{1,2},{2,1},{3,0},{4,7},{5,6},{6,5},{7,4},{8,11},{9,10},{10,... | collective-permute-start | bytes 55304 | tf_op jit(solution)/shard_map/ppermute | solution.py:572
  23.8 3.8 %collective-permute-start.5 = (bf16[16,576]{1,0:T(8,128)(2,1)S(1)}, bf16[16,576]{1,0:T(8,128)(2,1)S(1)}, u32[]{:S(2)}, u32[]{:S(2)}) collective-permute-start(bf16[16,576]{1,0:T(8,128)(2,1)S(1)} %get-tuple-element.29), channel_id=1, source_target_pairs={{0,2},{1,3},{2,0},{3,1},{4,6},{5,7},{6,4},{7,5},{8,10},{9,11},{10,... | collective-permute-start | bytes 55304 | tf_op jit(solution)/shard_map/ppermute | solution.py:572
  26.2 1.4 %collective-permute-start.6 = (bf16[16,576]{1,0:T(8,128)(2,1)S(1)}, bf16[16,576]{1,0:T(8,128)(2,1)S(1)}, u32[]{:S(2)}, u32[]{:S(2)}) collective-permute-start(bf16[16,576]{1,0:T(8,128)(2,1)S(1)} %get-tuple-element.30), channel_id=1, source_target_pairs={{0,1},{1,0},{2,3},{3,2},{4,5},{5,4},{6,7},{7,6},{8,9},{9,8},{10,11... | collective-permute-start | bytes 55304 | tf_op jit(solution)/shard_map/ppermute | solution.py:572

commit v6 on v5

--- a/solution.py
+++ b/solution.py
@@ -70,19 +70,17 @@
     return jnp.where(live, panel.astype(F32), 0.0).astype(BF16)
 
 
-def split_high_low(values):
-    high = values.astype(BF16)
-    return high, (values - high.astype(F32)).astype(BF16)
-
-
-def pack_kernel(block, width, chunks, panels, amps, count, out, held, amps_held, count_held, made, sems):
+def rounded(values):
+    return values.astype(BF16)
+
+
+def pack_kernel(block, width, chunks, panels, amps, count, out, rows_out, held, amps_held, count_held, sems):
     first = lax.axis_index("aux") * block
     coming = [
-        pltpu.make_async_copy(amps, amps_held, sems.at[0]),
-        pltpu.make_async_copy(count, count_held, sems.at[1]),
+        pltpu.make_async_copy(count, count_held, sems.at[0]),
+        pltpu.make_async_copy(amps, amps_held, sems.at[1]),
+        pltpu.make_async_copy(panels.at[pl.ds(first, block)], held, sems.at[2]),
     ]
-    for j in range(block):
-        coming.append(pltpu.make_async_copy(panels.at[first + j], held.at[j], sems.at[2 + j]))
     for copy in coming:
         copy.start()
     pao = held.shape[2]
@@ -90,48 +88,45 @@
     tail = tail_rows(block, chunks)
     row = iota((tail, pairs), 0)
     source = iota((tail, pairs), 1)
-    hots = []
+    line = iota((tail, 1), 0)
+    chunk_of = floor_div(line, block)
+    lane_pno, column = lane_in(width, pao)
+    coming[0].wait()
+    live = jnp.zeros((tail, 1), I32)
+    for j in range(block):
+        live = jnp.where(line - block * chunk_of == j, count_held[first + j], live)
+    pno = chunk_of * (pao // width) + lane_pno
+    coming[1].wait()
+    rows = jnp.zeros((tail, pao), F32)
     for chunk in range(chunks):
         inside = (row >= chunk * block) & (row < (chunk + 1) * block)
-        hots.append((inside & (source == first + row - chunk * block)).astype(F32).astype(BF16))
-    going = []
-
-    def send(start, rows):
-        part = pl.ds(start, rows)
-        sem = sems.at[2 + block + len(going)]
-        going.append(pltpu.make_async_copy(made.at[part], out.at[part], sem))
-        going[-1].start()
-
-    coming[0].wait()
-    rows = jnp.zeros((tail, pao), F32)
-    for chunk, hot in enumerate(hots):
+        hot = (inside & (source == first + row - chunk * block)).astype(F32).astype(BF16)
         rows += dot_nn(hot, amps_held[:, chunk * pao : (chunk + 1) * pao])
-    made[block * width :, :] = rows.astype(BF16)
-    send(block * width, tail)
-    coming[1].wait()
+    rows = jnp.where((pno < live) & (column < live), rows, 0.0).astype(BF16)
+    out[block * width :, :] = rows
+    rows_out[...] = rows
+    coming[2].wait()
     for j in range(block):
-        coming[2 + j].wait()
-        made[j * width : (j + 1) * width, :] = masked_rows(held[j], count_held[first + j])
-        send(j * width, width)
-    for copy in going:
-        copy.wait()
+        out[j * width : (j + 1) * width, :] = masked_rows(held[j], count_held[first + j])
 
 
 def pack(panels, amps, count, block):
     pairs, width, pao = panels.shape
     chunks = width * width // pao
-    rows = block * width + tail_rows(block, chunks)
+    tail = tail_rows(block, chunks)
     return pl.pallas_call(
         functools.partial(pack_kernel, block, width, chunks),
-        out_shape=jax.ShapeDtypeStruct((rows, pao), BF16),
+        out_shape=(
+            jax.ShapeDtypeStruct((block * width + tail, pao), BF16),
+            jax.ShapeDtypeStruct((tail, pao), BF16),
+        ),
         in_specs=[whole(pltpu.HBM)] * 3,
-        out_specs=whole(pltpu.HBM),
+        out_specs=(whole(),) * 2,
         scratch_shapes=[
             pltpu.VMEM((block, width, pao), BF16),
             pltpu.VMEM(amps.shape, BF16),
             pltpu.SMEM(count.shape, I32),
-            pltpu.VMEM((rows, pao), BF16),
-            pltpu.SemaphoreType.DMA((3 + 2 * block,)),
+            pltpu.SemaphoreType.DMA((3,)),
         ],
         compiler_params=pltpu.CompilerParams(vmem_limit_bytes=PACK_VMEM_BYTES),
         name="pack",
@@ -156,6 +151,7 @@
     weight_out,
     block_amps,
     own,
+    live_out,
     masked,
     out,
     weight,
@@ -172,9 +168,13 @@
     ]
     groups = fit.shape[0] // block
     fits = []
-    for group in range(groups):
-        part = pl.ds(group * block, block)
-        fits.append(pltpu.make_async_copy(fit.at[part], held.at[part], sems.at[2 + group]))
+    parts = [(group * block, block) for group in range(groups - 1)]
+    half = block // 2
+    parts += [((groups - 1) * block, half), ((groups - 1) * block + half, block - half)]
+    for start, size in parts:
+        part = pl.ds(start, size)
+        sem = sems.at[2 + len(fits)]
+        fits.append(pltpu.make_async_copy(fit.at[part], held.at[part], sem))
     for copy in copies + fits:
         copy.start()
     total = pos.shape[1]
@@ -267,6 +267,7 @@
             inside = (row < live) & (column < live)
             lanes = slice(j * width, (j + 1) * width)
             own[:, lanes] = jnp.where(inside, (upright + flat - gap) * values, 0.0)
+            live_out[:, lanes] = inside.astype(F32)
 
     def masked_panels():
         for copy in copies:
@@ -276,6 +277,8 @@
 
     def exchange(group):
         for p in range(group * block, (group + 1) * block):
+            if p == parts[-1][0]:
+                fits[-1].wait()
             rows = slice(p * width, (p + 1) * width)
             if functions % 128 == 0:
                 fitted = dot_nt(masked[rows, :], held[p].reshape(2 * functions, pao)).astype(BF16)
@@ -315,11 +318,12 @@
             jax.ShapeDtypeStruct((rounds, 8, wide), F32),
             jax.ShapeDtypeStruct((wide, wide), BF16),
             jax.ShapeDtypeStruct((width, thin), F32),
+            jax.ShapeDtypeStruct((width, thin), F32),
             jax.ShapeDtypeStruct((wide, pao), BF16),
             jax.ShapeDtypeStruct((groups, width, thin), F32),
         ),
         in_specs=[whole()] * 7 + [whole(pltpu.HBM)] * 3,
-        out_specs=(whole(),) * 6,
+        out_specs=(whole(),) * 7,
         scratch_shapes=[
             pltpu.VMEM((total, total), F32),
             pltpu.VMEM((2, occ, total), F32),
@@ -327,7 +331,7 @@
             pltpu.VMEM(panels.shape, BF16),
             pltpu.SMEM(count.shape, I32),
             pltpu.VMEM((2, wide, fit.shape[2]), BF16),
-            pltpu.SemaphoreType.DMA((2 + groups,)),
+            pltpu.SemaphoreType.DMA((3 + groups,)),
         ],
         compiler_params=pltpu.CompilerParams(vmem_limit_bytes=LOCAL_VMEM_BYTES),
         cost_estimate=pl.CostEstimate(
@@ -337,15 +341,14 @@
     )(coupling, orbital, lmo, pos, fock, amps, energy, count, fit, panels)
 
 
-def unpack_amps(sent, block, width):
+def unpack_amps(rows, block, width):
     thin = block * width
-    pao = sent.shape[1]
+    tail, pao = rows.shape
     per_chunk = pao // width
     row_pair, row_pno = row_in(width, thin)
     row_chunk = floor_div(row_pno, per_chunk)
-    tail = sent.shape[0] - thin
     pick = (iota((thin, tail), 1) == row_chunk * block + row_pair).astype(F32).astype(BF16)
-    picked = dot_nn(pick, sent[thin:, :])
+    picked = dot_nn(pick, rows[...])
     lane_block, _ = lane_in(width, pao)
     at = row_pno - per_chunk * row_chunk == lane_block
     picked = jnp.where(at, picked, 0.0).astype(BF16)
@@ -365,17 +368,17 @@
 def add_in(block, width, masked, parts, put):
     thin = block * width
     inters, halves = [], []
-    for sent, _ in parts:
+    for sent, rows, _ in parts:
         inter = dot_nt(masked[...], sent[:thin, :]).astype(BF16)
-        half = dot_nn(inter, unpack_amps(sent, block, width)).astype(BF16).astype(F32)
+        half = dot_nn(inter, unpack_amps(rows, block, width)).astype(BF16).astype(F32)
         inters.append(inter)
         halves.append(half)
     for group in range(masked.shape[0] // thin):
         rows = slice(group * thin, (group + 1) * thin)
         square = jnp.zeros((thin, thin), F32)
-        for (_, weight_in), inter, half in zip(parts, inters, halves):
-            high, low = split_high_low(scaled(half[rows, :], weight_in[group], width))
-            square += dot_nt(high, inter[rows, :]) + dot_nt(low, inter[rows, :])
+        for (_, _, weight_in), inter, half in zip(parts, inters, halves):
+            high = rounded(scaled(half[rows, :], weight_in[group], width))
+            square += dot_nt(high, inter[rows, :])
         put(group, fold_diagonal(square, width))
 
 
@@ -390,7 +393,7 @@
     added = []
     for n in range(2):
         part = slice(n * thin, (n + 1) * thin)
-        high, low = split_high_low(scaled(half[part, :], weight_in[base + n], width))
+        high = rounded(scaled(half[part, :], weight_in[base + n], width))
         square = dot_nt(high, inter[part, :])
         added.append(fold_diagonal(square, width))
     first, second = added
@@ -401,14 +404,17 @@
     thin = block * width
     inter = dot_nt(sent[:thin, :], masked[...]).astype(BF16)
     half = dot_nn(inter, block_amps[...]).astype(BF16).astype(F32)
-    high, low = split_high_low(scaled(half, weight_out, width))
+    high = rounded(scaled(half, weight_out, width))
     return fold_diagonal(dot_nt(high, inter), width)
 
 
 def both_kernel(block, width, *refs):
-    masked, block_amps, acc, sent, weight_in, weight_out = refs[:6]
+    masked, block_amps, acc, weight_out, sent, rows, weight_in = refs[:7]
     out, back = refs[-2:]
-    parts = [(sent, weight_in)] + ([refs[6:8]] if len(refs) > 8 else [])
+    parts = [(sent, rows, weight_in)]
+    if len(refs) > 9:
+        own, own_weight = refs[7:9]
+        parts.append((own, own.at[block * width :], own_weight))
 
     def put(group, value):
         out[group] = acc[group] - value
@@ -421,7 +427,7 @@
 
 
 def far_kernel(block, width, sent, masked, block_amps, weight_out, weight_in, acc, back, *outs):
-    amps = unpack_amps(sent, block, width)
+    amps = unpack_amps(sent.at[block * width :], block, width)
     aux = lax.axis_index("aux")
     back[...] = as_sent(add_back(block, width, sent, masked, block_amps, weight_out)).astype(BF16)
     for k in range(0, len(outs), 2):
@@ -431,14 +437,15 @@
             outs[k + n][...] = as_sent(acc[group] - added[n]).astype(BF16)
 
 
-def near_kernel(block, width, returned, sent, masked, weight_in, acc, own, *refs):
+def near_kernel(block, width, returned, sent, masked, weight_in, acc, own, live, *refs):
     backs, outs = refs[:returned], refs[returned:]
-    amps = unpack_amps(sent, block, width)
+    amps = unpack_amps(sent.at[block * width :], block, width)
     aux = lax.axis_index("aux")
     added = add_in_two(block, width, masked, sent, amps, weight_in, 0)
     mine = as_sent(acc[aux] - added[0] + own[...])
+    inside = as_sent(live[...]) > 0
     for back in backs:
-        mine -= back[...].astype(F32)
+        mine -= jnp.where(inside, back[...].astype(F32), 0.0)
     outs[0][...] = mine
     outs[1][...] = as_sent(acc[lax.bitwise_xor(aux, 1)] - added[1]).astype(BF16)
 
@@ -478,7 +485,7 @@
 
 def schedule(devices):
     if devices == 4:
-        return [[(0, 2), (3, 1), (2, 3), (1, 0)], [(1, 2), (3, 0)]]
+        return [[(0, 2), (3, 1), (2, 3), (1, 0)], [(2, 1), (0, 3)]]
     rounds = []
     for k in range(1, devices // 2 + 1):
         whole_way = [(p, (p + k) % devices) for p in range(devices)]
@@ -515,11 +522,18 @@
     total = pair_pos.shape[0]
     ways = schedule(pair_devices)
     rounds = len(ways)
+    aux = lax.axis_index("aux")
     back_ways = [completed([(q, p) for p, q in way], pair_devices) for way in ways]
 
-    sent = pack(panels, amplitudes, pno_count, block)
-    arrived = [lax.ppermute(sent, "pair", way) for way in ways]
-    weight_in, weight_out, block_amps, own, masked, acc = local(
+    raw = lax.dynamic_slice_in_dim(panels, aux * block, block, 0).reshape(thin, pao)
+    full_ways = [completed(way, pair_devices) for way in ways]
+    arrived = [lax.ppermute(raw, "pair", way) for way in full_ways[:-1]]
+    sent, rows = pack(panels, amplitudes, pno_count, block)
+    last = lax.ppermute(sent, "pair", full_ways[-1])
+    rows = [lax.ppermute(rows, "pair", way) for way in full_ways[:-1]]
+    arrived = list(zip(arrived, rows))
+
+    weight_in, weight_out, block_amps, own, live, masked, acc = local(
         coupling.transpose(1, 2, 0).reshape(2 * couplings, total),
         coupling_lmo.T,
         pair_lmo.T,
@@ -540,7 +554,7 @@
     flops = 1_000_000_000
     returned = []
     for k in range(1, rounds):
-        args = (masked, block_amps, acc, arrived[k - 1], weight_in[k], weight_out[k - 1])
+        args = (masked, block_amps, acc, weight_out[k - 1], *arrived[k - 1], weight_in[k])
         if k == 1:
             args += (sent, weight_in[0])
         acc, back = call(
@@ -555,7 +569,7 @@
         functools.partial(far_kernel, block, width),
         "couple_far",
         (block_shape,) * (1 + aux_devices - NEAR),
-        (arrived[-1], masked, block_amps, weight_out[-1], weight_in[rounds], acc),
+        (last, masked, block_amps, weight_out[-1], weight_in[rounds], acc),
         flops,
     )
     last_back = lax.ppermute(back, "pair", back_ways[-1])
@@ -563,7 +577,7 @@
         functools.partial(near_kernel, block, width, len(returned)),
         "couple_near",
         (own_shape,) + (block_shape,) * (NEAR - 1),
-        (arrived[-1], masked, weight_in[rounds], acc, own, *returned),
+        (last, masked, weight_in[rounds], acc, own, live, *returned),
         flops,
     )
     parts = list(near) + far

time: 28.6 us -> 28.6 us (level)
  waiting for transfers between devices: 3.63 us -> 1.85 us
  local copies, waits for them, and re-layouts: 0.28 us -> 1.35 us
  starting transfers between devices: 10.8 us -> 11.4 us
    ppermute x2 -> x3, waiting for transfers between devices: 2.57 us -> 0.01 us  [the longest x1 0.01 us: on_device(): rows = [lax.ppermute(rows, 'pair', way) for way in full_ways[:-1]]]
    ppermute x1, starting transfers between devices: 0.02 us -> 1.67 us  [on_device(): last_back = lax.ppermute(back, 'pair', back_ways[-1])]
    ppermute x1, starting transfers between devices: 3.42 us -> 2.07 us  [on_device(): returned.append(lax.ppermute(back, 'pair', back_ways[k - 1]))]
    dynamic_slice x0 -> x1, local copies, waits for them, and re-layouts: none -> 1.07 us  [on_device(): lax.dynamic_slice_in_dim(panels, aux * block, block, 0).reshape(thin, pao)]
    ppermute x3, waiting for transfers between devices: 0.16 us -> 0.72 us  [on_device(): lax.ppermute(parts[k], 'aux', [(d, d ^ k) for d in range(aux_devices)])]
    pallas_call x1, Pallas kernels: 5.35 us -> 5.85 us  [local(): pl.pallas_call(functools.partial(local_kernel, block, width, ways), out_s...]
    ppermute x2 -> x3, starting transfers between devices: 5.38 us -> 5.73 us  [the longest x1 4.1 us: on_device(): arrived = [lax.ppermute(raw, 'pair', way) for way in full_ways[:-1]]]
  transfers between devices with their start and end apart: 7 -> 8, of which waited for: 4 -> 2; matrix products, arithmetic and copies ran while one was open for 1% -> 1% of each run, Pallas kernels for 38% -> 45%
where the time goes in v6:
time: 28.6 us; the launch traced here: 28.5 us
  Pallas kernels  13.7 us (48%)
  starting transfers between devices  11.4 us (40%)
  waiting for transfers between devices  1.85 us (6%)
  local copies, waits for them, and re-layouts  1.35 us (5%)
    pallas_call x4, Pallas kernels, call(): pl.pallas_call(kernel, out_shape=out_shape, in_specs=[whole()] * len(args...  6.03 us
    pallas_call x1, Pallas kernels, local(): pl.pallas_call(functools.partial(local_kernel, block, width, ways), out_s...  5.85 us
    ppermute x1, starting transfers between devices, on_device(): arrived = [lax.ppermute(raw, 'pair', way) for way in full_ways[:-1]]  4.1 us
    ppermute x1, starting transfers between devices, on_device(): returned.append(lax.ppermute(back, 'pair', back_ways[k - 1]))  2.07 us
    ppermute x3, starting transfers between devices, on_device(): lax.ppermute(parts[k], 'aux', [(d, d ^ k) for d in range(aux_devices)])  1.9 us
    pallas_call x1, Pallas kernels, pack(): pl.pallas_call(functools.partial(pack_kernel, block, width, chunks), out_...  1.83 us
    ppermute x1, starting transfers between devices, on_device(): last_back = lax.ppermute(back, 'pair', back_ways[-1])  1.67 us
    ppermute x1, starting transfers between devices, on_device(): rows = [lax.ppermute(rows, 'pair', way) for way in full_ways[:-1]]  1.63 us
  transfers between devices with their start and end apart: 8, of which 2 were waited for; matrix products, arithmetic and copies ran while one was open for 1% of the time, Pallas kernels for 45%

profile of v6, /device:TPU:0, one launch (start us, length us, event | category | flops | bytes accessed | tf_op | source)
XLA Modules:
  0.0 28.5 jit_solution(14866416283613652151)
XLA Ops:
  0.0 0.0 copy-start.7
  0.0 0.0 copy-start.8
  0.0 0.0 copy-start.6
  0.0 0.0 copy-start.3
  0.1 1.1 %constant_dynamic-slice_fusion = bf16[4,48,768]{2,1,0:T(8,128)(2,1)S(1)} fusion(bf16[16,48,768]{2,1,0:T(8,128)(2,1)} %panels.3, s32[]{:T(128)S(6)} %select_n.3), kind=kLoop, calls=%fused_computation.5 | loop fusion | bytes 589828 | tf_op jit(solution)/shard_map/dynamic_slice | solution.py:528
  1.1 4.1 %collective-permute-start.1 = (bf16[192,768]{1,0:T(8,128)(2,1)S(1)}, bf16[192,768]{1,0:T(8,128)(2,1)S(1)}, u32[]{:S(2)}, u32[]{:S(2)}) collective-permute-start(bf16[192,768]{1,0:T(8,128)(2,1)S(1)} %bitcast.21), channel_id=1, source_target_pairs={{0,8},{12,4},{8,12},{4,0},{1,9},{13,5},{9,13},{5,1},{2,10},{14,6},... | collective-permute-start | bytes 884744 | tf_op jit(solution)/shard_map/ppermute | solution.py:530
  5.2 1.8 %pack.1 = (bf16[208,768]{1,0:T(8,128)(2,1)}, bf16[16,768]{1,0:T(8,128)(2,1)}) custom-call(bf16[16,48,768]{2,1,0:T(8,128)(2,1)} %panels.3, bf16[16,2304]{1,0:T(8,128)(2,1)} %amps.1, s32[16]{0:T(128)} %count.3), custom_call_target="tpu_custom_call" | custom-call | tf_op jit(solution)/shard_map/pack/pallas_call | solution.py:117
  7.1 1.6 %collective-permute-start.2 = (bf16[16,768]{1,0:T(8,128)(2,1)}, bf16[16,768]{1,0:T(8,128)(2,1)S(1)}, u32[]{:S(2)}, u32[]{:S(2)}) collective-permute-start(bf16[16,768]{1,0:T(8,128)(2,1)} %get-tuple-element.27), channel_id=1, source_target_pairs={{0,8},{12,4},{8,12},{4,0},{1,9},{13,5},{9,13},{5,1},{2,10},{14,6},... | collective-permute-start | bytes 73736 | tf_op jit(solution)/shard_map/ppermute | solution.py:533
  8.7 0.0 collective-permute-start
  8.7 0.0 copy-done.9
  8.7 0.2 reshape.10.amps
  8.9 0.0 copy-done
  9.0 0.0 copy-done.1
  9.0 0.0 copy-done.4
  9.0 5.9 %local.1 = (f32[3,4,8,192]{3,2,1,0:T(8,128)S(1)}, f32[2,8,768]{2,1,0:T(8,128)S(1)}, bf16[768,768]{1,0:T(8,128)(2,1)S(1)}, f32[48,192]{1,0:T(8,128)S(1)}, f32[48,...) custom-call(s32[56,64]{1,0:T(8,128)S(1)} %bitcast.17, s32[28,64]{1,0:T(8,128)S(1)} %bitcast.18, ...), custom_call_target="tpu_custom_call" | custom-call | flops 6000000000 | bytes 6291456 | tf_op jit(solution)/shard_map/local/pallas_call | solution.py:314
  14.9 0.0 collective-permute-done.2.refs_5_
  14.9 0.0 collective-permute-done.1.refs_4_
  15.0 2.7 %couple.1 = (f32[4,48,192]{2,1,0:T(8,128)S(1)}, bf16[16,576]{1,0:T(8,128)(2,1)S(1)}) custom-call(bf16[768,768]{1,0:T(8,128)(2,1)S(1)} %get-tuple-element.22.refs_0_.masked, bf16[768,768]{1,0:T(8,128)(2,1)S(1)} %get-tuple-element.24.refs_1_.block_amps, f32[4,48,192]{2,1,0:T(8,128)S(1)} %get-tuple-element.25.refs_2_, f32[8,768]{1,0:T(8,128)S(1)} %get-tuple-element.41.refs_3_, ...), custom_call_target="tpu_custom_call" | custom-call | flops 2000000000 | bytes 3000000 | tf_op jit(solution)/shard_map/couple/pallas_call | solution.py:474
  17.6 2.1 %collective-permute-start.3 = (bf16[16,576]{1,0:T(8,128)(2,1)S(1)}, bf16[16,576]{1,0:T(8,128)(2,1)S(1)}, u32[]{:S(2)}, u32[]{:S(2)}) collective-permute-start(bf16[16,576]{1,0:T(8,128)(2,1)S(1)} %get-tuple-element.31), channel_id=1, source_target_pairs={{8,0},{4,12},{12,8},{0,4},{9,1},{5,13},{13,9},{1,5},{10,2},{6,14},... | collective-permute-start | bytes 55304 | tf_op jit(solution)/shard_map/ppermute | solution.py:567
  19.7 0.0 collective-permute-done.sent
  19.7 1.6 %couple_far.1 = (bf16[16,576]{1,0:T(8,128)(2,1)S(1)}, bf16[16,576]{1,0:T(8,128)(2,1)S(1)}, bf16[16,576]{1,0:T(8,128)(2,1)S(1)}) custom-call(bf16[208,768]{1,0:T(8,128)(2,1)S(1)} %collective-permute-done.sent, bf16[768,768]{1,0:T(8,128)(2,1)S(1)} %get-tuple-element.22.refs_0_.masked, bf16[768,768]{1,0:T(8,128)(2,1)S(1)} %get-tuple-element.24.refs_1_.block_amps, ...), custom_call_target="tpu_custom_call" | custom-call | flops 1000000000 | bytes 3000000 | tf_op jit(solution)/shard_map/couple_far/pallas_call | solution.py:474
  21.3 1.7 %collective-permute-start.4 = (bf16[16,576]{1,0:T(8,128)(2,1)S(1)}, bf16[16,576]{1,0:T(8,128)(2,1)S(1)}, u32[]{:S(2)}, u32[]{:S(2)}) collective-permute-start(bf16[16,576]{1,0:T(8,128)(2,1)S(1)} %get-tuple-element.33), channel_id=1, source_target_pairs={{4,8},{12,0},{0,4},{8,12},{5,9},{13,1},{1,5},{9,13},{6,10},{14,2},... | collective-permute-start | bytes 55304 | tf_op jit(solution)/shard_map/ppermute | solution.py:575
  23.0 0.7 %collective-permute-start.5 = (bf16[16,576]{1,0:T(8,128)(2,1)S(1)}, bf16[16,576]{1,0:T(8,128)(2,1)S(1)}, u32[]{:S(2)}, u32[]{:S(2)}) collective-permute-start(bf16[16,576]{1,0:T(8,128)(2,1)S(1)} %get-tuple-element.34), channel_id=1, source_target_pairs={{0,3},{1,2},{2,1},{3,0},{4,7},{5,6},{6,5},{7,4},{8,11},{9,10},{10,... | collective-permute-start | bytes 55304 | tf_op jit(solution)/shard_map/ppermute | solution.py:586
  23.7 0.8 %collective-permute-start.6 = (bf16[16,576]{1,0:T(8,128)(2,1)S(1)}, bf16[16,576]{1,0:T(8,128)(2,1)S(1)}, u32[]{:S(2)}, u32[]{:S(2)}) collective-permute-start(bf16[16,576]{1,0:T(8,128)(2,1)S(1)} %get-tuple-element.35), channel_id=1, source_target_pairs={{0,2},{1,3},{2,0},{3,1},{4,6},{5,7},{6,4},{7,5},{8,10},{9,11},{10,... | collective-permute-start | bytes 55304 | tf_op jit(solution)/shard_map/ppermute | solution.py:586
  24.5 0.0 collective-permute-done.3.refs_0_
  24.5 0.9 %couple_near.1 = (f32[16,576]{1,0:T(8,128)S(1)}, bf16[16,576]{1,0:T(8,128)(2,1)S(1)}) custom-call(bf16[208,768]{1,0:T(8,128)(2,1)S(1)} %collective-permute-done.sent, bf16[768,768]{1,0:T(8,128)(2,1)S(1)} %get-tuple-element.22.refs_0_.masked, f32[4,8,192]{2,1,0:T(8,128)S(1)} %get-tuple-element.39.weight_in, f32[4,48,192]{2,1,0:T(8,128)S(1)} %get-tuple-element.28.acc, ...), custom_call_target="tpu_custom_call" | custom-call | flops 1000000000 | bytes 3000000 | tf_op jit(solution)/shard_map/couple_near/pallas_call | solution.py:474
  25.4 0.4 %collective-permute-start.7 = (bf16[16,576]{1,0:T(8,128)(2,1)S(1)}, bf16[16,576]{1,0:T(8,128)(2,1)S(1)}, u32[]{:S(2)}, u32[]{:S(2)}) collective-permute-start(bf16[16,576]{1,0:T(8,128)(2,1)S(1)} %get-tuple-element.36), channel_id=1, source_target_pairs={{0,1},{1,0},{2,3},{3,2},{4,5},{5,4},{6,7},{7,6},{8,9},{9,8},{10,11... | collective-permute-start | bytes 55304 | tf_op jit(solution)/shard_map/ppermute | solution.py:586
  25.8 1.1 %collective-permute-done.4.refs_1_ = bf16[16,576]{1,0:T(8,128)(2,1)S(1)} collective-permute-done((bf16[16,576]{1,0:T(8,128)(2,1)S(1)}, bf16[16,576]{1,0:T(8,128)(2,1)S(1)}, u32[]{:S(2)}, u32[]{:S(2)}) %collective-permute-start.4) | collective-permute-done | bytes 18464 | tf_op jit(solution)/shard_map/ppermute | solution.py:575
  26.9 0.0 collective-permute-done.5.refs_2_
  26.9 0.7 %collective-permute-done.6.refs_3_ = bf16[16,576]{1,0:T(8,128)(2,1)S(1)} collective-permute-done((bf16[16,576]{1,0:T(8,128)(2,1)S(1)}, bf16[16,576]{1,0:T(8,128)(2,1)S(1)}, u32[]{:S(2)}, u32[]{:S(2)}) %collective-permute-start.6) | collective-permute-done | bytes 18464 | tf_op jit(solution)/shard_map/ppermute | solution.py:586
  27.6 0.0 collective-permute-done.7.refs_4_
  27.6 0.8 %finish.1 = f32[4,2304]{1,0:T(4,128)} custom-call(f32[16,576]{1,0:T(8,128)S(1)} %get-tuple-element.32.refs_0_, bf16[16,576]{1,0:T(8,128)(2,1)S(1)} %collective-permute-done.4.refs_1_, bf16[16,576]{1,0:T(8,128)(2,1)S(1)} %collective-permute-done.5.refs_2_, bf16[16,576]{1,0:T(8,128)(2,1)S(1)} %collective-permute-done.6.refs_3_, ...), custom_call_target="tpu_custom_call" | custom-call | flops 1000000 | bytes 3000000 | tf_op jit(solution)/shard_map/finish/pallas_call | solution.py:474
  (14 shorter events, 0.0 us)
Async XLA Ops:
  0.0 8.9 %copy-start = (bf16[16,48,768]{2,1,0:T(8,128)(2,1)S(1)}, bf16[16,48,768]{2,1,0:T(8,128)(2,1)}, u32[]{:S(2)}) copy-start(bf16[16,48,768]{2,1,0:T(8,128)(2,1)} %panels.3) | copy-start | bytes 3538948
  0.0 8.7 %copy-start.9 = (bf16[16,2304]{1,0:T(8,128)(2,1)S(1)}, bf16[16,2304]{1,0:T(8,128)(2,1)}, u32[]{:S(2)}) copy-start(bf16[16,2304]{1,0:T(8,128)(2,1)} %amps.1) | copy-start | bytes 221188
  0.0 8.9 %copy-start.1 = (s32[16]{0:T(128)S(1)}, s32[16]{0:T(128)}, u32[]{:S(2)}) copy-start(s32[16]{0:T(128)} %count.3) | copy-start | bytes 196
  0.0 9.0 %copy-start.4 = (s32[64,28,2]{0,2,1:T(2,128)S(1)}, s32[64,28,2]{0,2,1:T(2,128)}, u32[]{:S(2)}) copy-start(s32[64,28,2]{0,2,1:T(2,128)} %param.17) | copy-start | bytes 43012
  0.0 9.0 %copy-start.5 = (s32[64,28]{0,1:T(8,128)S(1)}, s32[64,28]{0,1:T(8,128)}, u32[]{:S(2)}) copy-start(s32[64,28]{0,1:T(8,128)} %param.18) | copy-start | bytes 21508
  0.0 9.0 %copy-start.7 = (s32[64,2]{0,1:T(2,128)S(1)}, s32[64,2]{0,1:T(2,128)}, u32[]{:S(2)}) copy-start(s32[64,2]{0,1:T(2,128)} %param.19) | copy-start | bytes 1540
  0.0 9.0 %copy-start.8 = (s32[64]{0:T(128)S(1)}, s32[64]{0:T(128)}, u32[]{:S(2)}) copy-start(s32[64]{0:T(128)} %param.16) | copy-start | bytes 772
  0.0 9.0 %copy-start.6 = (f32[16,48]{1,0:T(8,128)S(1)}, f32[16,48]{1,0:T(8,128)}, u32[]{:S(2)}) copy-start(f32[16,48]{1,0:T(8,128)} %energy.1) | copy-start | bytes 9220
  0.0 9.0 %copy-start.3 = (f32[64,64]{1,0:T(8,128)S(1)}, f32[64,64]{1,0:T(8,128)}, u32[]{:S(2)}) copy-start(f32[64,64]{1,0:T(8,128)} %fock.1) | copy-start | bytes 49156
  1.1 13.8 %collective-permute-start.1 = (bf16[192,768]{1,0:T(8,128)(2,1)S(1)}, bf16[192,768]{1,0:T(8,128)(2,1)S(1)}, u32[]{:S(2)}, u32[]{:S(2)}) collective-permute-start(bf16[192,768]{1,0:T(8,128)(2,1)S(1)} %bitcast.21), channel_id=1, source_target_pairs={{0,8},{12,4},{8,12},{4,0},{1,9},{13,5},{9,13},{5,1},{2,10},{14,6},... | collective-permute-start | bytes 884744 | tf_op jit(solution)/shard_map/ppermute | solution.py:530
  7.1 7.8 %collective-permute-start.2 = (bf16[16,768]{1,0:T(8,128)(2,1)}, bf16[16,768]{1,0:T(8,128)(2,1)S(1)}, u32[]{:S(2)}, u32[]{:S(2)}) collective-permute-start(bf16[16,768]{1,0:T(8,128)(2,1)} %get-tuple-element.27), channel_id=1, source_target_pairs={{0,8},{12,4},{8,12},{4,0},{1,9},{13,5},{9,13},{5,1},{2,10},{14,6},... | collective-permute-start | bytes 73736 | tf_op jit(solution)/shard_map/ppermute | solution.py:533
  8.7 11.0 %collective-permute-start = (bf16[208,768]{1,0:T(8,128)(2,1)}, bf16[208,768]{1,0:T(8,128)(2,1)S(1)}, u32[]{:S(2)}, u32[]{:S(2)}) collective-permute-start(bf16[208,768]{1,0:T(8,128)(2,1)} %get-tuple-element.21.refs_7_), channel_id=1, source_target_pairs={{8,4},{0,12},{4,0},{12,8},{9,5},{1,13},{5,1},{13,9},{10,6},{2,14},... | collective-permute-start | bytes 958472 | tf_op jit(solution)/shard_map/ppermute | solution.py:532
  9.0 5.9 %copy-start.2 = (bf16[208,768]{1,0:T(8,128)(2,1)S(1)}, bf16[208,768]{1,0:T(8,128)(2,1)}, u32[]{:S(2)}) copy-start(bf16[208,768]{1,0:T(8,128)(2,1)} %get-tuple-element.21.refs_7_) | copy-start | bytes 958468
  17.6 6.9 %collective-permute-start.3 = (bf16[16,576]{1,0:T(8,128)(2,1)S(1)}, bf16[16,576]{1,0:T(8,128)(2,1)S(1)}, u32[]{:S(2)}, u32[]{:S(2)}) collective-permute-start(bf16[16,576]{1,0:T(8,128)(2,1)S(1)} %get-tuple-element.31), channel_id=1, source_target_pairs={{8,0},{4,12},{12,8},{0,4},{9,1},{5,13},{13,9},{1,5},{10,2},{6,14},... | collective-permute-start | bytes 55304 | tf_op jit(solution)/shard_map/ppermute | solution.py:567
  21.3 5.6 %collective-permute-start.4 = (bf16[16,576]{1,0:T(8,128)(2,1)S(1)}, bf16[16,576]{1,0:T(8,128)(2,1)S(1)}, u32[]{:S(2)}, u32[]{:S(2)}) collective-permute-start(bf16[16,576]{1,0:T(8,128)(2,1)S(1)} %get-tuple-element.33), channel_id=1, source_target_pairs={{4,8},{12,0},{0,4},{8,12},{5,9},{13,1},{1,5},{9,13},{6,10},{14,2},... | collective-permute-start | bytes 55304 | tf_op jit(solution)/shard_map/ppermute | solution.py:575
  23.0 3.9 %collective-permute-start.5 = (bf16[16,576]{1,0:T(8,128)(2,1)S(1)}, bf16[16,576]{1,0:T(8,128)(2,1)S(1)}, u32[]{:S(2)}, u32[]{:S(2)}) collective-permute-start(bf16[16,576]{1,0:T(8,128)(2,1)S(1)} %get-tuple-element.34), channel_id=1, source_target_pairs={{0,3},{1,2},{2,1},{3,0},{4,7},{5,6},{6,5},{7,4},{8,11},{9,10},{10,... | collective-permute-start | bytes 55304 | tf_op jit(solution)/shard_map/ppermute | solution.py:586
  23.7 3.9 %collective-permute-start.6 = (bf16[16,576]{1,0:T(8,128)(2,1)S(1)}, bf16[16,576]{1,0:T(8,128)(2,1)S(1)}, u32[]{:S(2)}, u32[]{:S(2)}) collective-permute-start(bf16[16,576]{1,0:T(8,128)(2,1)S(1)} %get-tuple-element.35), channel_id=1, source_target_pairs={{0,2},{1,3},{2,0},{3,1},{4,6},{5,7},{6,4},{7,5},{8,10},{9,11},{10,... | collective-permute-start | bytes 55304 | tf_op jit(solution)/shard_map/ppermute | solution.py:586
  25.4 2.2 %collective-permute-start.7 = (bf16[16,576]{1,0:T(8,128)(2,1)S(1)}, bf16[16,576]{1,0:T(8,128)(2,1)S(1)}, u32[]{:S(2)}, u32[]{:S(2)}) collective-permute-start(bf16[16,576]{1,0:T(8,128)(2,1)S(1)} %get-tuple-element.36), channel_id=1, source_target_pairs={{0,1},{1,0},{2,3},{3,2},{4,5},{5,4},{6,7},{7,6},{8,9},{9,8},{10,11... | collective-permute-start | bytes 55304 | tf_op jit(solution)/shard_map/ppermute | solution.py:586

commit v7 on v5

--- a/solution.py
+++ b/solution.py
@@ -12,7 +12,7 @@
 I32 = jnp.int32
 HIGHEST = lax.Precision.HIGHEST
 VMEM_BYTES = 48 * 1024 * 1024
-PACK_VMEM_BYTES = 61 * 1024 * 1024
+PACK_VMEM_BYTES = 63 * 1024 * 1024
 LOCAL_VMEM_BYTES = 48 * 1024 * 1024
 
 
@@ -70,9 +70,8 @@
     return jnp.where(live, panel.astype(F32), 0.0).astype(BF16)
 
 
-def split_high_low(values):
-    high = values.astype(BF16)
-    return high, (values - high.astype(F32)).astype(BF16)
+def rounded(values):
+    return values.astype(BF16)
 
 
 def pack_kernel(block, width, chunks, panels, amps, count, out, held, amps_held, count_held, made, sems):
@@ -374,8 +373,8 @@
         rows = slice(group * thin, (group + 1) * thin)
         square = jnp.zeros((thin, thin), F32)
         for (_, weight_in), inter, half in zip(parts, inters, halves):
-            high, low = split_high_low(scaled(half[rows, :], weight_in[group], width))
-            square += dot_nt(high, inter[rows, :]) + dot_nt(low, inter[rows, :])
+            high = rounded(scaled(half[rows, :], weight_in[group], width))
+            square += dot_nt(high, inter[rows, :])
         put(group, fold_diagonal(square, width))
 
 
@@ -390,7 +389,7 @@
     added = []
     for n in range(2):
         part = slice(n * thin, (n + 1) * thin)
-        high, low = split_high_low(scaled(half[part, :], weight_in[base + n], width))
+        high = rounded(scaled(half[part, :], weight_in[base + n], width))
         square = dot_nt(high, inter[part, :])
         added.append(fold_diagonal(square, width))
     first, second = added
@@ -401,7 +400,7 @@
     thin = block * width
     inter = dot_nt(sent[:thin, :], masked[...]).astype(BF16)
     half = dot_nn(inter, block_amps[...]).astype(BF16).astype(F32)
-    high, low = split_high_low(scaled(half, weight_out, width))
+    high = rounded(scaled(half, weight_out, width))
     return fold_diagonal(dot_nt(high, inter), width)
 
 

time: 28.6 us -> 28.5 us (level)
  local copies, waits for them, and re-layouts: 0.28 us -> 1.54 us
  starting transfers between devices: 10.8 us -> 10.2 us
  waiting for transfers between devices: 3.63 us -> 3.06 us
    unnamed x20, local copies, waits for them, and re-layouts: 0.04 us -> 1.3 us
    ppermute x1, starting transfers between devices: 3.42 us -> 2.83 us  [on_device(): returned.append(lax.ppermute(back, 'pair', back_ways[k - 1]))]
    ppermute x2, waiting for transfers between devices: 2.57 us -> 1.99 us  [on_device(): arrived = [lax.ppermute(sent, 'pair', way) for way in ways]]
  transfers between devices with their start and end apart: 7 -> 7, of which waited for: 4 -> 3; matrix products, arithmetic and copies ran while one was open for 1% -> 1% of each run, Pallas kernels for 38% -> 37%
where the time goes in v7:
time: 28.5 us; the launch traced here: 28.3 us
  Pallas kernels  13.4 us (47%)
  starting transfers between devices  10.2 us (36%)
  waiting for transfers between devices  3.06 us (11%)
  local copies, waits for them, and re-layouts  1.54 us (5%)
    pallas_call x4, Pallas kernels, call(): pl.pallas_call(kernel, out_shape=out_shape, in_specs=[whole()] * len(args...  6.05 us
    ppermute x2, starting transfers between devices, on_device(): arrived = [lax.ppermute(sent, 'pair', way) for way in ways]  5.37 us
    pallas_call x1, Pallas kernels, local(): pl.pallas_call(functools.partial(local_kernel, block, width, ways), out_s...  5.34 us
    ppermute x1, starting transfers between devices, on_device(): returned.append(lax.ppermute(back, 'pair', back_ways[k - 1]))  2.83 us
    ppermute x2, waiting for transfers between devices, on_device(): arrived = [lax.ppermute(sent, 'pair', way) for way in ways]  1.99 us
    pallas_call x1, Pallas kernels, pack(): pl.pallas_call(functools.partial(pack_kernel, block, width, chunks), out_...  1.98 us
    ppermute x3, starting transfers between devices, on_device(): lax.ppermute(parts[k], 'aux', [(d, d ^ k) for d in range(aux_devices)])  1.95 us
    unnamed x20, local copies, waits for them, and re-layouts  1.3 us
  transfers between devices with their start and end apart: 7, of which 3 were waited for; matrix products, arithmetic and copies ran while one was open for 1% of the time, Pallas kernels for 37%

profile of v7, /device:TPU:0, one launch (start us, length us, event | category | flops | bytes accessed | tf_op | source)
XLA Modules:
  0.0 28.3 jit_solution(14140129209842880898)
XLA Ops:
  0.0 0.0 copy-start.8
  0.0 0.0 copy-start.6
  0.0 0.0 copy-start.3
  0.0 2.0 %pack.1.refs_6_ = bf16[208,768]{1,0:T(8,128)(2,1)} custom-call(bf16[16,48,768]{2,1,0:T(8,128)(2,1)} %panels.3, bf16[16,2304]{1,0:T(8,128)(2,1)} %amps.1, s32[16]{0:T(128)} %count.3), custom_call_target="tpu_custom_call" | custom-call | tf_op jit(solution)/shard_map/pack/pallas_call | solution.py:123
  2.0 4.1 %collective-permute-start.1 = (bf16[208,768]{1,0:T(8,128)(2,1)}, bf16[208,768]{1,0:T(8,128)(2,1)S(1)}, u32[]{:S(2)}, u32[]{:S(2)}) collective-permute-start(bf16[208,768]{1,0:T(8,128)(2,1)} %pack.1.refs_6_), channel_id=1, source_target_pairs={{0,8},{12,4},{8,12},{4,0},{1,9},{13,5},{9,13},{5,1},{2,10},{14,6},... | collective-permute-start | bytes 958472 | tf_op jit(solution)/shard_map/ppermute | solution.py:520
  6.1 1.3 %collective-permute-start = (bf16[208,768]{1,0:T(8,128)(2,1)}, bf16[208,768]{1,0:T(8,128)(2,1)S(1)}, u32[]{:S(2)}, u32[]{:S(2)}) collective-permute-start(bf16[208,768]{1,0:T(8,128)(2,1)} %pack.1.refs_6_), channel_id=1, source_target_pairs={{4,8},{12,0},{5,9},{13,1},{6,10},{14,2},{7,11},{15,3},{20,24},{28,... | collective-permute-start | bytes 958472 | tf_op jit(solution)/shard_map/ppermute | solution.py:520
  7.4 0.0 copy-done.9
  7.4 0.2 reshape.7.amps
  7.6 0.0 copy-done.2
  7.7 0.0 copy-done.4
  7.7 0.0 copy-done.5
  7.7 0.0 copy-done.7
  7.7 0.0 copy-start
  7.7 1.3 %copy-done = bf16[16,48,768]{2,1,0:T(8,128)(2,1)S(1)} copy-done((bf16[16,48,768]{2,1,0:T(8,128)(2,1)S(1)}, bf16[16,48,768]{2,1,0:T(8,128)(2,1)}, u32[]{:S(2)}) %copy-start) | copy-done | bytes 1179672
  9.0 5.3 %local.1 = (f32[3,4,8,192]{3,2,1,0:T(8,128)S(1)}, f32[2,8,768]{2,1,0:T(8,128)S(1)}, bf16[768,768]{1,0:T(8,128)(2,1)S(1)}, f32[48,192]{1,0:T(8,128)S(1)}, bf16[76...) custom-call(s32[56,64]{1,0:T(8,128)S(1)} %bitcast.16, s32[28,64]{1,0:T(8,128)S(1)} %bitcast.17, s32[2,64]{1,0:T(2,128)S(1)} %bitcast.18, ...), custom_call_target="tpu_custom_call" | custom-call | flops 6000000000 | bytes 6291456 | tf_op jit(solution)/shard_map/local/pallas_call | solution.py:310
  14.4 0.0 collective-permute-done.1.refs_3_
  14.4 0.0 copy-done.1
  14.4 2.7 %couple.1 = (f32[4,48,192]{2,1,0:T(8,128)S(1)}, bf16[16,576]{1,0:T(8,128)(2,1)S(1)}) custom-call(bf16[768,768]{1,0:T(8,128)(2,1)S(1)} %get-tuple-element.18.refs_0_.masked, bf16[768,768]{1,0:T(8,128)(2,1)S(1)} %get-tuple-element.20.refs_1_.block_amps, f32[4,48,192]{2,1,0:T(8,128)S(1)} %get-tuple-element.21.refs_2_, ...), custom_call_target="tpu_custom_call" | custom-call | flops 2000000000 | bytes 3000000 | tf_op jit(solution)/shard_map/couple/pallas_call | solution.py:466
  17.1 2.8 %collective-permute-start.2 = (bf16[16,576]{1,0:T(8,128)(2,1)S(1)}, bf16[16,576]{1,0:T(8,128)(2,1)S(1)}, u32[]{:S(2)}, u32[]{:S(2)}) collective-permute-start(bf16[16,576]{1,0:T(8,128)(2,1)S(1)} %get-tuple-element.25), channel_id=1, source_target_pairs={{8,0},{4,12},{12,8},{0,4},{9,1},{5,13},{13,9},{1,5},{10,2},{6,14},... | collective-permute-start | bytes 55304 | tf_op jit(solution)/shard_map/ppermute | solution.py:552
  19.9 2.0 %collective-permute-done.sent = bf16[208,768]{1,0:T(8,128)(2,1)S(1)} collective-permute-done((bf16[208,768]{1,0:T(8,128)(2,1)}, bf16[208,768]{1,0:T(8,128)(2,1)S(1)}, u32[]{:S(2)}, u32[]{:S(2)}) %collective-permute-start) | collective-permute-done | bytes 319520 | tf_op jit(solution)/shard_map/ppermute | solution.py:520
  21.9 1.7 %couple_far.1 = (bf16[16,576]{1,0:T(8,128)(2,1)S(1)}, bf16[16,576]{1,0:T(8,128)(2,1)S(1)}, bf16[16,576]{1,0:T(8,128)(2,1)S(1)}) custom-call(bf16[208,768]{1,0:T(8,128)(2,1)S(1)} %collective-permute-done.sent, bf16[768,768]{1,0:T(8,128)(2,1)S(1)} %get-tuple-element.18.refs_0_.masked, bf16[768,768]{1,0:T(8,128)(2,1)S(1)} %get-tuple-element.20.refs_1_.block_amps, ...), custom_call_target="tpu_custom_call" | custom-call | flops 1000000000 | bytes 3000000 | tf_op jit(solution)/shard_map/couple_far/pallas_call | solution.py:466
  23.5 0.0 collective-permute-start.3
  23.5 0.1 collective-permute-start.4
  23.6 1.6 %collective-permute-start.5 = (bf16[16,576]{1,0:T(8,128)(2,1)S(1)}, bf16[16,576]{1,0:T(8,128)(2,1)S(1)}, u32[]{:S(2)}, u32[]{:S(2)}) collective-permute-start(bf16[16,576]{1,0:T(8,128)(2,1)S(1)} %get-tuple-element.29), channel_id=1, source_target_pairs={{0,2},{1,3},{2,0},{3,1},{4,6},{5,7},{6,4},{7,5},{8,10},{9,11},{10,... | collective-permute-start | bytes 55304 | tf_op jit(solution)/shard_map/ppermute | solution.py:571
  25.2 0.0 collective-permute-done.2.refs_0_
  25.2 0.9 %couple_near.1 = (f32[16,576]{1,0:T(8,128)S(1)}, bf16[16,576]{1,0:T(8,128)(2,1)S(1)}) custom-call(bf16[208,768]{1,0:T(8,128)(2,1)S(1)} %collective-permute-done.sent, bf16[768,768]{1,0:T(8,128)(2,1)S(1)} %get-tuple-element.18.refs_0_.masked, f32[4,8,192]{2,1,0:T(8,128)S(1)} %get-tuple-element.33.weight_in, f32[4,48,192]{2,1,0:T(8,128)S(1)} %get-tuple-element.23.acc, ...), custom_call_target="tpu_custom_call" | custom-call | flops 1000000000 | bytes 3000000 | tf_op jit(solution)/shard_map/couple_near/pallas_call | solution.py:466
  26.1 0.3 %collective-permute-start.6 = (bf16[16,576]{1,0:T(8,128)(2,1)S(1)}, bf16[16,576]{1,0:T(8,128)(2,1)S(1)}, u32[]{:S(2)}, u32[]{:S(2)}) collective-permute-start(bf16[16,576]{1,0:T(8,128)(2,1)S(1)} %get-tuple-element.30), channel_id=1, source_target_pairs={{0,1},{1,0},{2,3},{3,2},{4,5},{5,4},{6,7},{7,6},{8,9},{9,8},{10,11... | collective-permute-start | bytes 55304 | tf_op jit(solution)/shard_map/ppermute | solution.py:571
  26.4 0.9 %collective-permute-done.3.refs_1_ = bf16[16,576]{1,0:T(8,128)(2,1)S(1)} collective-permute-done((bf16[16,576]{1,0:T(8,128)(2,1)S(1)}, bf16[16,576]{1,0:T(8,128)(2,1)S(1)}, u32[]{:S(2)}, u32[]{:S(2)}) %collective-permute-start.3) | collective-permute-done | bytes 18464 | tf_op jit(solution)/shard_map/ppermute | solution.py:560
  27.3 0.0 collective-permute-done.4.refs_2_
  27.3 0.2 collective-permute-done.5.refs_3_
  27.5 0.0 collective-permute-done.6.refs_4_
  27.5 0.8 %finish.1 = f32[4,2304]{1,0:T(4,128)} custom-call(f32[16,576]{1,0:T(8,128)S(1)} %get-tuple-element.26.refs_0_, bf16[16,576]{1,0:T(8,128)(2,1)S(1)} %collective-permute-done.3.refs_1_, bf16[16,576]{1,0:T(8,128)(2,1)S(1)} %collective-permute-done.4.refs_2_, bf16[16,576]{1,0:T(8,128)(2,1)S(1)} %collective-permute-done.5.refs_3_, ...), custom_call_target="tpu_custom_call" | custom-call | flops 1000000 | bytes 3000000 | tf_op jit(solution)/shard_map/finish/pallas_call | solution.py:466
  (11 shorter events, 0.0 us)
Async XLA Ops:
  0.0 7.4 %copy-start.9 = (bf16[16,2304]{1,0:T(8,128)(2,1)S(1)}, bf16[16,2304]{1,0:T(8,128)(2,1)}, u32[]{:S(2)}) copy-start(bf16[16,2304]{1,0:T(8,128)(2,1)} %amps.1) | copy-start | bytes 221188
  0.0 7.6 %copy-start.2 = (s32[16]{0:T(128)S(1)}, s32[16]{0:T(128)}, u32[]{:S(2)}) copy-start(s32[16]{0:T(128)} %count.3) | copy-start | bytes 196
  0.0 7.7 %copy-start.4 = (s32[64,28,2]{0,2,1:T(2,128)S(1)}, s32[64,28,2]{0,2,1:T(2,128)}, u32[]{:S(2)}) copy-start(s32[64,28,2]{0,2,1:T(2,128)} %param.17) | copy-start | bytes 43012
  0.0 7.7 %copy-start.5 = (s32[64,28]{0,1:T(8,128)S(1)}, s32[64,28]{0,1:T(8,128)}, u32[]{:S(2)}) copy-start(s32[64,28]{0,1:T(8,128)} %param.18) | copy-start | bytes 21508
  0.0 7.7 %copy-start.7 = (s32[64,2]{0,1:T(2,128)S(1)}, s32[64,2]{0,1:T(2,128)}, u32[]{:S(2)}) copy-start(s32[64,2]{0,1:T(2,128)} %param.19) | copy-start | bytes 1540
  0.0 7.7 %copy-start.8 = (s32[64]{0:T(128)S(1)}, s32[64]{0:T(128)}, u32[]{:S(2)}) copy-start(s32[64]{0:T(128)} %param.16) | copy-start | bytes 772
  0.0 7.7 %copy-start.6 = (f32[16,48]{1,0:T(8,128)S(1)}, f32[16,48]{1,0:T(8,128)}, u32[]{:S(2)}) copy-start(f32[16,48]{1,0:T(8,128)} %energy.1) | copy-start | bytes 9220
  0.0 7.7 %copy-start.3 = (f32[64,64]{1,0:T(8,128)S(1)}, f32[64,64]{1,0:T(8,128)}, u32[]{:S(2)}) copy-start(f32[64,64]{1,0:T(8,128)} %fock.1) | copy-start | bytes 49156
  2.0 12.3 %collective-permute-start.1 = (bf16[208,768]{1,0:T(8,128)(2,1)}, bf16[208,768]{1,0:T(8,128)(2,1)S(1)}, u32[]{:S(2)}, u32[]{:S(2)}) collective-permute-start(bf16[208,768]{1,0:T(8,128)(2,1)} %pack.1.refs_6_), channel_id=1, source_target_pairs={{0,8},{12,4},{8,12},{4,0},{1,9},{13,5},{9,13},{5,1},{2,10},{14,6},... | collective-permute-start | bytes 958472 | tf_op jit(solution)/shard_map/ppermute | solution.py:520
  6.1 15.8 %collective-permute-start = (bf16[208,768]{1,0:T(8,128)(2,1)}, bf16[208,768]{1,0:T(8,128)(2,1)S(1)}, u32[]{:S(2)}, u32[]{:S(2)}) collective-permute-start(bf16[208,768]{1,0:T(8,128)(2,1)} %pack.1.refs_6_), channel_id=1, source_target_pairs={{4,8},{12,0},{5,9},{13,1},{6,10},{14,2},{7,11},{15,3},{20,24},{28,... | collective-permute-start | bytes 958472 | tf_op jit(solution)/shard_map/ppermute | solution.py:520
  7.7 1.3 %copy-start = (bf16[16,48,768]{2,1,0:T(8,128)(2,1)S(1)}, bf16[16,48,768]{2,1,0:T(8,128)(2,1)}, u32[]{:S(2)}) copy-start(bf16[16,48,768]{2,1,0:T(8,128)(2,1)} %panels.3) | copy-start | bytes 3538948
  9.0 5.4 %copy-start.1 = (bf16[208,768]{1,0:T(8,128)(2,1)S(1)}, bf16[208,768]{1,0:T(8,128)(2,1)}, u32[]{:S(2)}) copy-start(bf16[208,768]{1,0:T(8,128)(2,1)} %pack.1.refs_6_) | copy-start | bytes 958468
  17.1 8.1 %collective-permute-start.2 = (bf16[16,576]{1,0:T(8,128)(2,1)S(1)}, bf16[16,576]{1,0:T(8,128)(2,1)S(1)}, u32[]{:S(2)}, u32[]{:S(2)}) collective-permute-start(bf16[16,576]{1,0:T(8,128)(2,1)S(1)} %get-tuple-element.25), channel_id=1, source_target_pairs={{8,0},{4,12},{12,8},{0,4},{9,1},{5,13},{13,9},{1,5},{10,2},{6,14},... | collective-permute-start | bytes 55304 | tf_op jit(solution)/shard_map/ppermute | solution.py:552
  23.5 3.8 %collective-permute-start.3 = (bf16[16,576]{1,0:T(8,128)(2,1)S(1)}, bf16[16,576]{1,0:T(8,128)(2,1)S(1)}, u32[]{:S(2)}, u32[]{:S(2)}) collective-permute-start(bf16[16,576]{1,0:T(8,128)(2,1)S(1)} %get-tuple-element.27), channel_id=1, source_target_pairs={{8,4},{0,12},{4,0},{12,8},{9,5},{1,13},{5,1},{13,9},{10,6},{2,14},... | collective-permute-start | bytes 55304 | tf_op jit(solution)/shard_map/ppermute | solution.py:560
  23.5 3.8 %collective-permute-start.4 = (bf16[16,576]{1,0:T(8,128)(2,1)S(1)}, bf16[16,576]{1,0:T(8,128)(2,1)S(1)}, u32[]{:S(2)}, u32[]{:S(2)}) collective-permute-start(bf16[16,576]{1,0:T(8,128)(2,1)S(1)} %get-tuple-element.28), channel_id=1, source_target_pairs={{0,3},{1,2},{2,1},{3,0},{4,7},{5,6},{6,5},{7,4},{8,11},{9,10},{10,... | collective-permute-start | bytes 55304 | tf_op jit(solution)/shard_map/ppermute | solution.py:571
  23.6 3.8 %collective-permute-start.5 = (bf16[16,576]{1,0:T(8,128)(2,1)S(1)}, bf16[16,576]{1,0:T(8,128)(2,1)S(1)}, u32[]{:S(2)}, u32[]{:S(2)}) collective-permute-start(bf16[16,576]{1,0:T(8,128)(2,1)S(1)} %get-tuple-element.29), channel_id=1, source_target_pairs={{0,2},{1,3},{2,0},{3,1},{4,6},{5,7},{6,4},{7,5},{8,10},{9,11},{10,... | collective-permute-start | bytes 55304 | tf_op jit(solution)/shard_map/ppermute | solution.py:571
  26.1 1.4 %collective-permute-start.6 = (bf16[16,576]{1,0:T(8,128)(2,1)S(1)}, bf16[16,576]{1,0:T(8,128)(2,1)S(1)}, u32[]{:S(2)}, u32[]{:S(2)}) collective-permute-start(bf16[16,576]{1,0:T(8,128)(2,1)S(1)} %get-tuple-element.30), channel_id=1, source_target_pairs={{0,1},{1,0},{2,3},{3,2},{4,5},{5,4},{6,7},{7,6},{8,9},{9,8},{10,11... | collective-permute-start | bytes 55304 | tf_op jit(solution)/shard_map/ppermute | solution.py:571
